TPU v7x, 32 devices: a whole 2x2x4 slice. The times are simulated.
32 devices in a mesh: seq: 16 (over z, y, core), dp: 2 (over x).
Axes of the slice: x: 2, y: 2, z: 4, core: 2. Of those that a mesh axis runs over, the one named last changes fastest.
Arguments:
- tokens: bfloat16 [2, 4096, 1024], P('dp', 'seq'), may hold values from -6 to 6
- cotangent: bfloat16 [2, 4096, 1024], P('dp', 'seq'), may hold values from -6 to 6
- pre_gain: bfloat16 [1024], P('seq'), may hold values from 0.5 to 1.5
- pre_offset: bfloat16 [1024], P('seq'), may hold values from -1.25 to 1.25
- input_weight: bfloat16 [1024, 3072], P('seq'), may hold values from -0.1875 to 0.1875
- input_bias: bfloat16 [3072], P('seq'), may hold values from -1.25 to 1.25
- short_weight: bfloat16 [3, 3072], P(None, 'seq'), may hold values from -3.5 to 3.5
- short_bias: bfloat16 [3072], P('seq'), may hold values from -1.25 to 1.25
- skip_weight: bfloat16 [1024], P('seq'), may hold values from -6 to 6
- embed_weight: float32 [33, 64], replicated, may hold values from -1 to 1
- embed_bias: float32 [64], replicated, may hold values from -3 to 3
- hidden_weight: float32 [64, 64], replicated, may hold values from -0.75 to 0.75
- hidden_bias: float32 [64], replicated, may hold values from -3 to 3
- last_weight: float32 [64, 64], replicated, may hold values from -0.75 to 0.75
- last_bias: float32 [64], replicated, may hold values from -3 to 3
- frequency: float32 [64], replicated, may hold values from 0.5 to 1.5
- filter_weight: bfloat16 [64, 1024], P(None, 'seq'), may hold values from -0.02734375 to 0.02734375
- output_weight: bfloat16 [1024, 1024], P('seq'), may hold values from -0.1875 to 0.1875
- output_bias: bfloat16 [1024], P('seq'), may hold values from -1.25 to 1.25
- post_gain: bfloat16 [1024], P('seq'), may hold values from 0.5 to 1.5
- post_offset: bfloat16 [1024], P('seq'), may hold values from -1.25 to 1.25
- up_weight: bfloat16 [1024, 4096], P('seq'), may hold values from -0.1875 to 0.1875
- up_bias: bfloat16 [4096], P('seq'), may hold values from -1.25 to 1.25
- down_weight: bfloat16 [4096, 1024], P('seq'), may hold values from -0.09375 to 0.09375
- down_bias: bfloat16 [1024], P('seq'), may hold values from -1.25 to 1.25
Outputs:
- result: bfloat16 [2, 4096, 1024], P('dp', 'seq')
- tokens_grad: bfloat16 [2, 4096, 1024], P('dp', 'seq')
- pre_gain_grad: float32 [1024], P(('seq', 'dp'))
- pre_offset_grad: float32 [1024], P(('seq', 'dp'))
- input_weight_grad: float32 [1024, 3072], P(('seq', 'dp'))
- input_bias_grad: float32 [3072], P(('seq', 'dp'))
- short_weight_grad: float32 [3, 3072], P(None, ('seq', 'dp'))
- short_bias_grad: float32 [3072], P(('seq', 'dp'))
- skip_weight_grad: float32 [1024], P(('seq', 'dp'))
- embed_weight_grad: float32 [33, 64], replicated
- embed_bias_grad: float32 [64], replicated
- hidden_weight_grad: float32 [64, 64], replicated
- hidden_bias_grad: float32 [64], replicated
- last_weight_grad: float32 [64, 64], replicated
- last_bias_grad: float32 [64], replicated
- frequency_grad: float32 [64], replicated
- filter_weight_grad: float32 [64, 1024], P(None, ('seq', 'dp'))
- output_weight_grad: float32 [1024, 1024], P(('seq', 'dp'))
- output_bias_grad: float32 [1024], P(('seq', 'dp'))
- post_gain_grad: float32 [1024], P(('seq', 'dp'))
- post_offset_grad: float32 [1024], P(('seq', 'dp'))
- up_weight_grad: float32 [1024, 4096], P(('seq', 'dp'))
- up_bias_grad: float32 [4096], P(('seq', 'dp'))
- down_weight_grad: float32 [4096, 1024], P(('seq', 'dp'))
- down_bias_grad: float32 [1024], P(('seq', 'dp'))
All inputs are finite; a program needn't handle non-finite values.
Results may differ from a plain program's by a relative error of at most 0.015.
Values may be sent and summed in bfloat16 or wider, within the bound.
No kernel may reach another device: no remote copies, remote signals or barrier semaphores. Data moves between devices by JAX's collectives and lax.ppermute only.
A program may use at most 256 MiB of HBM per device.

v0:
```python
from functools import partial
import math

import jax
import jax.numpy as jnp
from jax import lax
from jax.sharding import PartitionSpec as P

FEATURES = 33


highest = lax.Precision.HIGHEST


def shifted(value, axis, steps):
    count = lax.axis_size(axis)
    initial, last = (max(0, -steps), min(count, count - steps))
    return lax.ppermute(value, axis, [(source, source + steps) for source in range(initial, last)])


def norm_forward(values, norm_gain, norm_offset):
    center = values - jnp.mean(values, axis=-1, keepdims=True)
    inverse = lax.rsqrt(jnp.mean(center * center, axis=-1, keepdims=True) + 1e-05)
    normed = center * inverse
    return (normed * norm_gain + norm_offset, normed, inverse)


def norm_backward(upstream, normed, inverse, norm_gain):
    scaled = upstream * norm_gain
    centered = (
        scaled
        - jnp.mean(scaled, axis=-1, keepdims=True)
        - normed * jnp.mean(scaled * normed, axis=-1, keepdims=True)
    )
    return (centered * inverse, jnp.sum(upstream * normed, axis=0), jnp.sum(upstream, axis=0))


def contract(left_side, right_side, left_dim, right_dim):
    return lax.dot_general(
        left_side,
        right_side,
        (((left_dim,), (right_dim,)), ((), ())),
        preferred_element_type=jnp.float32,
    )


def spectral_tables(rows_total, col_count):
    total_size = rows_total * col_count
    row_index = jnp.arange(rows_total, dtype=jnp.int32)
    col_index = jnp.arange(col_count, dtype=jnp.int32)
    row_angle = (row_index[:, None] * row_index[None, :] % rows_total).astype(jnp.float32) * (
        2.0 * math.pi / rows_total
    )
    col_angle = (col_index[:, None] * col_index[None, :] % col_count).astype(jnp.float32) * (
        2.0 * math.pi / col_count
    )
    twist_angle = (row_index[:, None] * col_index[None, :]).astype(jnp.float32) * (
        2.0 * math.pi / total_size
    )
    return (
        jnp.cos(row_angle),
        -jnp.sin(row_angle),
        jnp.cos(twist_angle),
        -jnp.sin(twist_angle),
        jnp.cos(col_angle),
        -jnp.sin(col_angle),
        total_size,
    )


def forward_transform(signal, tables):
    row_cos, row_sin, twist_cos, twist_sin, col_cos, col_sin, total_size = tables
    half_rows = signal.shape[1]
    first_re = jnp.einsum("ka,cab->ckb", row_cos[:, :half_rows], signal, precision=highest)
    first_im = jnp.einsum("ka,cab->ckb", row_sin[:, :half_rows], signal, precision=highest)
    turned_re = first_re * twist_cos - first_im * twist_sin
    turned_im = first_re * twist_sin + first_im * twist_cos
    out_re = jnp.einsum("ckb,bm->ckm", turned_re, col_cos, precision=highest) - jnp.einsum(
        "ckb,bm->ckm", turned_im, col_sin, precision=highest
    )
    out_im = jnp.einsum("ckb,bm->ckm", turned_re, col_sin, precision=highest) + jnp.einsum(
        "ckb,bm->ckm", turned_im, col_cos, precision=highest
    )
    return (out_re, out_im)


def inverse_transform(spec_re, spec_im, tables, half_rows):
    row_cos, row_sin, twist_cos, twist_sin, col_cos, col_sin, total_size = tables
    back_re = jnp.einsum("ckm,mb->ckb", spec_re, col_cos, precision=highest) + jnp.einsum(
        "ckm,mb->ckb", spec_im, col_sin, precision=highest
    )
    back_im = jnp.einsum("ckm,mb->ckb", spec_im, col_cos, precision=highest) - jnp.einsum(
        "ckm,mb->ckb", spec_re, col_sin, precision=highest
    )
    untwist_re = back_re * twist_cos + back_im * twist_sin
    untwist_im = back_im * twist_cos - back_re * twist_sin
    real_part = jnp.einsum(
        "ak,ckb->cab", row_cos[:half_rows], untwist_re, precision=highest
    ) + jnp.einsum("ak,ckb->cab", row_sin[:half_rows], untwist_im, precision=highest)
    return real_part / total_size


def filter_local(trunk, filter_full, features, window):
    embed_weight, embed_bias, hidden_weight, hidden_bias, last_weight, last_bias, frequency = trunk
    layer_out = jnp.sin(
        frequency * (jnp.dot(features, embed_weight, precision=highest) + embed_bias)
    )
    layer_out = jnp.sin(
        frequency * (jnp.dot(layer_out, hidden_weight, precision=highest) + hidden_bias)
    )
    layer_out = jnp.sin(
        frequency * (jnp.dot(layer_out, last_weight, precision=highest) + last_bias)
    )
    return (
        lax.dot_general(
            filter_full,
            layer_out,
            (((0,), (1,)), ((), ())),
            precision=highest,
            preferred_element_type=jnp.float32,
        )
        * window
    )


def per_device(
    tokens,
    cotangent,
    pre_gain,
    pre_offset,
    input_weight,
    input_bias,
    short_weight,
    short_bias,
    skip_weight,
    embed_weight,
    embed_bias,
    hidden_weight,
    hidden_bias,
    last_weight,
    last_bias,
    frequency,
    filter_weight,
    output_weight,
    output_bias,
    post_gain,
    post_offset,
    up_weight,
    up_bias,
    down_weight,
    down_bias,
):
    seq_count = lax.axis_size("seq")
    seq_index = lax.axis_index("seq")
    tok_count = tokens.shape[1]
    model_width = tokens.shape[2]
    length = tok_count * seq_count
    channels = model_width // seq_count
    half_rows = length // 128
    tables = spectral_tables(2 * half_rows, 128)
    mixer_full = (
        lax.all_gather(pre_gain, "seq", axis=0, tiled=True),
        lax.all_gather(pre_offset, "seq", axis=0, tiled=True),
        lax.all_gather(input_weight, "seq", axis=0, tiled=True),
        lax.all_gather(input_bias, "seq", axis=0, tiled=True),
        lax.all_gather(short_weight, "seq", axis=1, tiled=True),
        lax.all_gather(short_bias, "seq", axis=0, tiled=True),
        lax.all_gather(skip_weight, "seq", axis=0, tiled=True),
        lax.all_gather(filter_weight, "seq", axis=1, tiled=True),
        lax.all_gather(output_weight, "seq", axis=0, tiled=True),
        lax.all_gather(output_bias, "seq", axis=0, tiled=True),
    )
    mlp_full = (
        lax.all_gather(post_gain, "seq", axis=0, tiled=True),
        lax.all_gather(post_offset, "seq", axis=0, tiled=True),
        lax.all_gather(up_weight, "seq", axis=0, tiled=True),
        lax.all_gather(up_bias, "seq", axis=0, tiled=True),
        lax.all_gather(down_weight, "seq", axis=0, tiled=True),
        lax.all_gather(down_bias, "seq", axis=0, tiled=True),
    )
    (
        pre_gain_full,
        pre_offset_full,
        input_full,
        input_bias_full,
        short_full,
        short_bias_full,
        skip_full,
        filter_full,
        output_full,
        output_bias_full,
    ) = mixer_full
    post_gain_full, post_offset_full, up_full, up_bias_full, down_full, down_bias_full = mlp_full
    inputs = tokens[0].astype(jnp.float32)
    normed_one, unit_one, inverse_one = norm_forward(
        inputs, pre_gain_full.astype(jnp.float32), pre_offset_full.astype(jnp.float32)
    )
    normed_low = normed_one.astype(jnp.bfloat16)
    projected = (
        contract(input_full, normed_low, 0, 1) + input_bias_full.astype(jnp.float32)[:, None]
    )
    projected_low = projected.astype(jnp.bfloat16)
    earlier = shifted(projected_low[:, tok_count - 2 :], "seq", 1)
    extended = jnp.concatenate([earlier, projected_low], axis=1).astype(jnp.float32)
    short_taps = short_full.astype(jnp.float32)
    convolved = (
        short_taps[0][:, None] * extended[:, :tok_count]
        + short_taps[1][:, None] * extended[:, 1 : tok_count + 1]
        + short_taps[2][:, None] * extended[:, 2:]
        + short_bias_full.astype(jnp.float32)[:, None]
    )
    first_part = convolved[:model_width]
    second_part = convolved[model_width : 2 * model_width]
    values_part = convolved[2 * model_width :]
    gated_low = (values_part * second_part).astype(jnp.bfloat16)
    positions = (seq_index * tok_count + jnp.arange(tok_count, dtype=jnp.int32)).astype(jnp.float32)
    relative = positions / (length - 1)
    phases = positions * (2.0 * math.pi / length)
    band_count = (FEATURES - 1) // 2
    band_freq = jnp.linspace(0.0001, band_count - 1, band_count).astype(jnp.float32)
    angles = phases[:, None] * band_freq[None, :]
    features = jnp.concatenate([relative[:, None], jnp.cos(angles), -jnp.sin(angles)], axis=1)
    deltas = jnp.linspace(math.log(0.01) / 1.5, math.log(0.01) / 0.3, model_width).astype(
        jnp.float32
    )
    window = jnp.exp(-relative[None, :] * jnp.abs(deltas)[:, None]) + 0.05
    trunk = (
        embed_weight,
        embed_bias,
        hidden_weight,
        hidden_bias,
        last_weight,
        last_bias,
        frequency,
    )
    kernel_rows, filter_pull = jax.vjp(
        partial(filter_local, features=features, window=window),
        trunk,
        filter_full.astype(jnp.float32),
    )
    kernel_low = kernel_rows.astype(jnp.bfloat16)
    gated_ch, kernel_ch = (
        lax.all_to_all(
            gated_low.reshape(channels, seq_count, tok_count),
            "seq",
            split_axis=1,
            concat_axis=1,
            tiled=True,
        ),
        lax.all_to_all(
            kernel_low.reshape(channels, seq_count, tok_count),
            "seq",
            split_axis=1,
            concat_axis=1,
            tiled=True,
        ),
    )
    gated_f = gated_ch.astype(jnp.float32).reshape(channels, half_rows, 128)
    kernel_f = kernel_ch.astype(jnp.float32).reshape(channels, half_rows, 128)
    gated_re, gated_im = forward_transform(gated_f, tables)
    kernel_re, kernel_im = forward_transform(kernel_f, tables)
    skip_own = lax.dynamic_slice_in_dim(
        skip_full.astype(jnp.float32).reshape(channels, seq_count), seq_index, 1, 1
    )[:, :, None]
    conv_out = inverse_transform(
        gated_re * kernel_re - gated_im * kernel_im,
        gated_re * kernel_im + gated_im * kernel_re,
        tables,
        half_rows,
    )
    mixed_low = (
        (conv_out + gated_f * skip_own).astype(jnp.bfloat16).reshape(channels, seq_count, tok_count)
    )
    mixed_back = lax.all_to_all(mixed_low, "seq", split_axis=1, concat_axis=1, tiled=True)
    mixed_tok = mixed_back.reshape(model_width, tok_count).astype(jnp.float32)
    mix_low = (mixed_tok * first_part).astype(jnp.bfloat16)
    branch = contract(mix_low, output_full, 0, 0) + output_bias_full.astype(jnp.float32)
    hidden = inputs + branch
    normed_two, unit_two, inverse_two = norm_forward(
        hidden, post_gain_full.astype(jnp.float32), post_offset_full.astype(jnp.float32)
    )
    normed_two_low = normed_two.astype(jnp.bfloat16)
    before = jnp.dot(
        normed_two_low, up_full, preferred_element_type=jnp.float32
    ) + up_bias_full.astype(jnp.float32)
    activated, gelu_pull = jax.vjp(partial(jax.nn.gelu, approximate=False), before)
    activ_low = activated.astype(jnp.bfloat16)
    result = hidden + (
        jnp.dot(activ_low, down_full, preferred_element_type=jnp.float32)
        + down_bias_full.astype(jnp.float32)
    )
    again = (
        lax.all_gather(pre_gain, "seq", axis=0, tiled=True),
        lax.all_gather(input_weight, "seq", axis=0, tiled=True),
        lax.all_gather(short_weight, "seq", axis=1, tiled=True),
        lax.all_gather(output_weight, "seq", axis=0, tiled=True),
        lax.all_gather(post_gain, "seq", axis=0, tiled=True),
        lax.all_gather(up_weight, "seq", axis=0, tiled=True),
        lax.all_gather(down_weight, "seq", axis=0, tiled=True),
    )
    pre_gain_back, input_back, short_back, output_back, post_gain_back, up_back, down_back = again
    upstream = cotangent[0]
    upstream_f = upstream.astype(jnp.float32)
    down_bias_grad = jnp.sum(upstream_f, axis=0)
    down_weight_grad = contract(activ_low, upstream, 0, 0)
    act_grad = contract(upstream, down_back, 1, 1)
    before_low = gelu_pull(act_grad)[0].astype(jnp.bfloat16)
    up_bias_grad = jnp.sum(before_low.astype(jnp.float32), axis=0)
    up_weight_grad = contract(normed_two_low, before_low, 0, 0)
    normed_two_grad = contract(before_low, up_back, 1, 1)
    hidden_norm_grad, post_gain_grad, post_offset_grad = norm_backward(
        normed_two_grad, unit_two, inverse_two, post_gain_back.astype(jnp.float32)
    )
    hidden_grad = upstream_f + hidden_norm_grad
    branch_low = hidden_grad.astype(jnp.bfloat16)
    output_bias_grad = jnp.sum(branch_low.astype(jnp.float32), axis=0)
    output_weight_grad = contract(mix_low, branch_low, 1, 0)
    mix_grad = contract(output_back, branch_low, 1, 1)
    mixed_grad_low = (mix_grad * first_part).astype(jnp.bfloat16)
    first_grad = mix_grad * mixed_tok
    mixed_grad_ch = lax.all_to_all(
        mixed_grad_low.reshape(channels, seq_count, tok_count),
        "seq",
        split_axis=1,
        concat_axis=1,
        tiled=True,
    )
    grad_f = mixed_grad_ch.astype(jnp.float32).reshape(channels, half_rows, 128)
    grad_re, grad_im = forward_transform(grad_f, tables)
    gated_back = (
        inverse_transform(
            grad_re * kernel_re + grad_im * kernel_im,
            grad_im * kernel_re - grad_re * kernel_im,
            tables,
            half_rows,
        )
        + grad_f * skip_own
    )
    kernel_back = inverse_transform(
        grad_re * gated_re + grad_im * gated_im,
        grad_im * gated_re - grad_re * gated_im,
        tables,
        half_rows,
    )
    skip_own_grad = jnp.sum(grad_f * gated_f, axis=(1, 2))
    skip_grid = lax.dynamic_update_slice_in_dim(
        jnp.zeros((channels, seq_count), jnp.float32), skip_own_grad[:, None], seq_index, 1
    )
    skip_grad = skip_grid.reshape(model_width)
    gated_tok, kernel_tok = (
        lax.all_to_all(
            gated_back.astype(jnp.bfloat16).reshape(channels, seq_count, tok_count),
            "seq",
            split_axis=1,
            concat_axis=1,
            tiled=True,
        ),
        lax.all_to_all(
            kernel_back.astype(jnp.bfloat16).reshape(channels, seq_count, tok_count),
            "seq",
            split_axis=1,
            concat_axis=1,
            tiled=True,
        ),
    )
    gated_grad = gated_tok.reshape(model_width, tok_count).astype(jnp.float32)
    kernel_grad = kernel_tok.reshape(model_width, tok_count).astype(jnp.float32)
    trunk_grad, filter_weight_grad = filter_pull(kernel_grad)
    (
        embed_grad,
        embed_bias_grad,
        hidden_weight_grad,
        hidden_bias_grad,
        last_weight_grad,
        last_bias_grad,
        frequency_grad,
    ) = trunk_grad
    trunk_sums = lax.psum(
        (
            embed_grad,
            embed_bias_grad,
            hidden_weight_grad,
            hidden_bias_grad,
            last_weight_grad,
            last_bias_grad,
            frequency_grad,
        ),
        ("seq", "dp"),
    )
    values_grad = gated_grad * second_part
    second_grad = gated_grad * values_part
    conv_grad_low = jnp.concatenate([first_grad, second_grad, values_grad], axis=0).astype(
        jnp.bfloat16
    )
    following = shifted(conv_grad_low[:, :2], "seq", -1)
    grad_ext = jnp.concatenate([conv_grad_low, following], axis=1).astype(jnp.float32)
    back_taps = short_back.astype(jnp.float32)
    projected_grad = (
        back_taps[0][:, None] * grad_ext[:, 2:]
        + back_taps[1][:, None] * grad_ext[:, 1 : tok_count + 1]
        + back_taps[2][:, None] * grad_ext[:, :tok_count]
    )
    conv_grad = conv_grad_low.astype(jnp.float32)
    short_weight_grad = jnp.stack(
        [
            jnp.sum(conv_grad * extended[:, :tok_count], axis=1),
            jnp.sum(conv_grad * extended[:, 1 : tok_count + 1], axis=1),
            jnp.sum(conv_grad * extended[:, 2:], axis=1),
        ],
        axis=0,
    )
    short_bias_grad = jnp.sum(conv_grad, axis=1)
    projected_low_grad = projected_grad.astype(jnp.bfloat16)
    input_bias_grad = jnp.sum(projected_low_grad.astype(jnp.float32), axis=1)
    input_weight_grad = contract(normed_low, projected_low_grad, 0, 1)
    normed_one_grad = contract(projected_low_grad, input_back, 0, 1)
    input_norm_grad, pre_gain_grad, pre_offset_grad = norm_backward(
        normed_one_grad, unit_one, inverse_one, pre_gain_back.astype(jnp.float32)
    )
    tokens_grad = (hidden_grad + input_norm_grad).astype(jnp.bfloat16)
    all_sums = (
        lax.psum_scatter(pre_gain_grad, ("seq", "dp"), scatter_dimension=0, tiled=True),
        lax.psum_scatter(pre_offset_grad, ("seq", "dp"), scatter_dimension=0, tiled=True),
        lax.psum_scatter(input_weight_grad, ("seq", "dp"), scatter_dimension=0, tiled=True),
        lax.psum_scatter(input_bias_grad, ("seq", "dp"), scatter_dimension=0, tiled=True),
        lax.psum_scatter(short_weight_grad, ("seq", "dp"), scatter_dimension=1, tiled=True),
        lax.psum_scatter(short_bias_grad, ("seq", "dp"), scatter_dimension=0, tiled=True),
        lax.psum_scatter(skip_grad, ("seq", "dp"), scatter_dimension=0, tiled=True),
        lax.psum_scatter(filter_weight_grad, ("seq", "dp"), scatter_dimension=1, tiled=True),
        lax.psum_scatter(output_weight_grad, ("seq", "dp"), scatter_dimension=0, tiled=True),
        lax.psum_scatter(output_bias_grad, ("seq", "dp"), scatter_dimension=0, tiled=True),
        lax.psum_scatter(post_gain_grad, ("seq", "dp"), scatter_dimension=0, tiled=True),
        lax.psum_scatter(post_offset_grad, ("seq", "dp"), scatter_dimension=0, tiled=True),
        lax.psum_scatter(up_weight_grad, ("seq", "dp"), scatter_dimension=0, tiled=True),
        lax.psum_scatter(up_bias_grad, ("seq", "dp"), scatter_dimension=0, tiled=True),
        lax.psum_scatter(down_weight_grad, ("seq", "dp"), scatter_dimension=0, tiled=True),
        lax.psum_scatter(down_bias_grad, ("seq", "dp"), scatter_dimension=0, tiled=True),
    )
    mixer_sums = all_sums[:10]
    mlp_sums = all_sums[10:]
    return (
        result.astype(jnp.bfloat16)[None],
        tokens_grad[None],
        mixer_sums[0],
        mixer_sums[1],
        mixer_sums[2],
        mixer_sums[3],
        mixer_sums[4],
        mixer_sums[5],
        mixer_sums[6],
        trunk_sums[0],
        trunk_sums[1],
        trunk_sums[2],
        trunk_sums[3],
        trunk_sums[4],
        trunk_sums[5],
        trunk_sums[6],
        mixer_sums[7],
        mixer_sums[8],
        mixer_sums[9],
        mlp_sums[0],
        mlp_sums[1],
        mlp_sums[2],
        mlp_sums[3],
        mlp_sums[4],
        mlp_sums[5],
    )


def solution(mesh):
    placed = (
        P("dp", "seq", None),
        P("dp", "seq", None),
        P("seq"),
        P("seq"),
        P("seq", None),
        P("seq"),
        P(None, "seq"),
        P("seq"),
        P("seq"),
        P(),
        P(),
        P(),
        P(),
        P(),
        P(),
        P(),
        P(None, "seq"),
        P("seq", None),
        P("seq"),
        P("seq"),
        P("seq"),
        P("seq", None),
        P("seq"),
        P("seq", None),
        P("seq"),
    )
    return jax.shard_map(
        per_device,
        mesh=mesh,
        in_specs=placed,
        out_specs=(
            P("dp", "seq", None),
            P("dp", "seq", None),
            P(("seq", "dp")),
            P(("seq", "dp")),
            P(("seq", "dp"), None),
            P(("seq", "dp")),
            P(None, ("seq", "dp")),
            P(("seq", "dp")),
            P(("seq", "dp")),
            P(),
            P(),
            P(),
            P(),
            P(),
            P(),
            P(),
            P(None, ("seq", "dp")),
            P(("seq", "dp"), None),
            P(("seq", "dp")),
            P(("seq", "dp")),
            P(("seq", "dp")),
            P(("seq", "dp"), None),
            P(("seq", "dp")),
            P(("seq", "dp"), None),
            P(("seq", "dp")),
        ),
        check_vma=False,
    )
```

profile of v0, /device:TPU:9, one launch (start us, length us, event | category | flops | bytes accessed | tf_op | source)
XLA Modules:
  0.0 1932.6 jit_solution(7845957091760246120)
XLA Ops:
  10.2 20.5 %all_gather.61 = bf16[64,1024]{0,1:T(8,128)(2,1)S(1)} all-gather(bf16[64,64]{0,1:T(8,128)(2,1)S(1)} %copy.131), channel_id=1, replica_groups=mesh['seq'=16,'dp'=2] {'seq'}, dimensions={1}, use_global_device_ids=true | all-gather | bytes 139264 | tf_op jit(solution)/shard_map/all_gather | solution.py:169
  39.5 6.6 all-to-all-start.1
  47.1 37.5 %all-gather = bf16[16,192,3]{1,2,0:T(4,128)(2,1)S(1)} all-gather(bf16[1,192,3]{1,2,0:T(4,128)(2,1)S(1)} %bitcast.320), channel_id=1, replica_groups=mesh['seq'=16,'dp'=2] {'seq'}, dimensions={0}, use_global_device_ids=true | all-gather | bytes 19584 | tf_op jit(solution)/shard_map/all_gather | solution.py:166
  88.8 47.9 %all-reduce.20 = (bf16[3072]{0:T(1024)(128)(2,1)S(1)}, bf16[1024]{0:T(1024)(128)(2,1)S(1)}, bf16[1024]{0:T(1024)(128)(2,1)S(1)}, bf16[3072]{0:T(1024)(128)(2,1)S...) all-reduce(bf16[3072]{0:T(1024)(128)(2,1)S(1)} %dynamic-update-slic, ...), channel_id=1, replica_groups=mesh['seq'=16,'dp'=2] {'seq'}, use_global_device_ids=true, to_apply=%add.2 | all-reduce | flops 13312 | bytes 53248
  139.1 2.4 fusion.231
  141.4 4.9 fusion.7
  146.3 16.1 collective-permute-start
  162.4 3.4 fusion.132
  174.1 15.2 all-to-all-start
  189.3 4.7 fusion.134
  194.1 3.6 convolution_add_fusion.6
  197.6 3.6 convolution_subtract_fusion.4
  201.2 8.7 all-to-all-done
  214.1 2.3 copy.137
  216.4 2.3 reshape.256
  218.7 2.2 fusion.235
  221.9 2.2 fusion.126
  224.1 2.2 fusion.128
  226.3 2.6 convolution_subtract_fusion.5
  229.0 4.0 multiply_add_fusion.2
  239.3 2.3 convolution_add_fusion.5
  243.2 2.5 fusion.83
  245.7 2.2 reshape.259
  249.9 5.7 all-to-all-start.2
  255.7 37.3 %all-gather.1 = bf16[16,1,256]{2,1,0:T(2,128)(2,1)S(1)} all-gather(bf16[1,1,256]{2,1,0:T(2,128)(2,1)S(1)} %reshape.300), channel_id=1, replica_groups=mesh['seq'=16,'dp'=2] {'seq'}, dimensions={0}, use_global_device_ids=true | all-gather | bytes 8704 | tf_op jit(solution)/shard_map/all_gather | solution.py:177
  295.4 2.5 copy.140
  298.0 2.5 multiply_convert_fusion.5
  300.4 2.6 fusion.351
  304.4 16.4 multiply_convert_fusion
  320.9 10.4 convert_reduce_fusion.1
  332.6 7.0 multiply_reduce_fusion
  341.5 3.0 multiply_convert_fusion.4
  347.8 19.6 %all_to_all.30 = bf16[64,16,256]{2,0,1:T(8,128)(2,1)S(1)} all-to-all(bf16[64,16,256]{2,0,1:T(8,128)(2,1)S(1)} %copy.143), channel_id=1, replica_groups=mesh['seq'=16,'dp'=2] {'seq'}, dimensions={1} | all-to-all | bytes 1048576 | tf_op jit(solution)/shard_map/all_to_all | solution.py:321
  371.3 2.1 fusion.233
  374.5 3.5 fusion.138
  378.0 3.4 fusion.140
  383.7 2.3 copy.147
  386.0 2.3 reshape.262
  388.3 5.2 convolution_add_fusion.4
  393.6 7.3 multiply_subtract_fusion
  411.0 2.4 fusion.95
  417.4 4.4 all-to-all-start.5
  421.8 3.8 fusion.176
  425.7 2.1 fusion.174
  433.7 2.5 fusion.86
  440.2 6.4 all-to-all-start.4
  449.2 2.5 copy.157
  451.7 2.3 convolution_multiply_fusion.2
  463.3 2.6 copy.150
  465.8 2.3 multiply_convert_fusion.2
  477.6 7.2 fusion.106
  484.9 2.9 fusion.121
  488.1 2.7 fusion.267
  490.9 7.9 fusion.344
  500.1 9.9 fusion.347
  511.0 9.8 fusion.143
  521.4 7.5 fusion.98
  530.1 39.7 %reduce-scatter.19.cloned.1.call-done = f32[96,3]{1,0:T(8,128)} async-done(((f32[3072,3]{1,0:T(8,128)}), f32[96,3]{1,0:T(8,128)}) %reduce-scatter.19.cloned.1.call-update) | async-done | bytes 1168
  571.2 181.8 %all-reduce.23.cloned.1.call-done = (f32[1024]{0:T(1024)}, f32[1024]{0:T(1024)}, f32[3072]{0:T(1024)}, f32[3072]{0:T(1024)}, f32[1024]{0:T(1024)}, /*index=5*/f3...) async-done(((f32[1024]{0:T(1024)}, f32[1024]{0:T(1024)}, ...) | async-done | bytes 111888
  765.7 113.1 %reduce-scatter.11.cloned.1.call-done = f32[64,32]{0,1:T(8,128)} async-done(((f32[64,1024]{0,1:T(8,128)}), f32[64,32]{0,1:T(8,128)}) %reduce-scatter.11.cloned.1.call-update) | async-done | bytes 8208 | tf_op jit(solution)/shard_map/reduce_scatter | solution.py:429
  878.8 142.5 %reduce-scatter.13.cloned.1.call-done = f32[32,1024]{1,0:T(8,128)} async-done(((f32[1024,1024]{1,0:T(8,128)}), f32[32,1024]{1,0:T(8,128)}) %reduce-scatter.13.cloned.1.call-update) | async-done | bytes 131088 | tf_op jit(solution)/shard_map/reduce_scatter | solution.py:430
  1021.3 173.2 %reduce-scatter.9.cloned.1.call-done = f32[32,3072]{1,0:T(8,128)} async-done(((f32[1024,3072]{1,0:T(8,128)}), f32[32,3072]{1,0:T(8,128)}) %reduce-scatter.9.cloned.1.call-update) | async-done | bytes 393232 | tf_op jit(solution)/shard_map/reduce_scatter | solution.py:424
  1194.5 361.2 %reduce-scatter.15.cloned.1.call-done = f32[32,4096]{1,0:T(8,128)} async-done(((f32[1024,4096]{1,0:T(8,128)}), f32[32,4096]{1,0:T(8,128)}) %reduce-scatter.15.cloned.1.call-update) | async-done | bytes 524304 | tf_op jit(solution)/shard_map/reduce_scatter | solution.py:434
  1555.7 361.5 %reduce-scatter.17.cloned.1.call-done = f32[128,1024]{1,0:T(8,128)} async-done(((f32[4096,1024]{1,0:T(8,128)}), f32[128,1024]{1,0:T(8,128)}) %reduce-scatter.17.cloned.1.call-update) | async-done | bytes 524304 | tf_op jit(solution)/shard_map/reduce_scatter | solution.py:436
  (359 shorter events, 130.4 us)
Async XLA Ops:
  7.2 25.5 %copy-start = (f32[64,64]{1,0:T(8,128)S(1)}, f32[64,64]{1,0:T(8,128)}, u32[]{:S(2)}) copy-start(f32[64,64]{1,0:T(8,128)} %param.36) | copy-start | bytes 49156
  7.2 134.2 %all-gather.7.cloned.1.call-start = ((), (), s32[]{:S(2)}) async-start(), calls=%async_computation.12 | async-start | bytes 6684672 | tf_op jit(solution)/shard_map/all_gather | solution.py:164
  8.0 292.5 %all-gather.9.cloned.1.call-start = ((), (), s32[]{:S(2)}) async-start(), calls=%async_computation.13 | async-start | bytes 2228224 | tf_op jit(solution)/shard_map/all_gather | solution.py:170
  8.7 295.7 %all-gather.11.cloned.1.call-start = ((), (), s32[]{:S(2)}) async-start(), calls=%async_computation.14 | async-start | bytes 8912896 | tf_op jit(solution)/shard_map/all_gather | solution.py:176
  30.7 5.1 copy-start.46
  38.1 8.5 copy-start.25
  38.4 8.7 copy-start.78
  38.4 46.4 %copy-start.92 = (u32[32]{0:T(128)S(1)}, u32[32]{0:T(128)}, u32[]{:S(2)}) copy-start(u32[32]{0:T(128)} %constant.165) | copy-start | bytes 388
  38.4 48.3 %copy-start.82 = (bf16[64]{0:T(256)(128)(2,1)S(1)}, bf16[64]{0:T(256)(128)(2,1)}, u32[]{:S(2)}) copy-start(bf16[64]{0:T(256)(128)(2,1)} %param.44) | copy-start | bytes 388
  38.4 48.5 %copy-start.83 = (bf16[64]{0:T(256)(128)(2,1)S(1)}, bf16[64]{0:T(256)(128)(2,1)}, u32[]{:S(2)}) copy-start(bf16[64]{0:T(256)(128)(2,1)} %param.45) | copy-start | bytes 388
  38.4 48.7 %copy-start.84 = (bf16[64]{0:T(256)(128)(2,1)S(1)}, bf16[64]{0:T(256)(128)(2,1)}, u32[]{:S(2)}) copy-start(bf16[64]{0:T(256)(128)(2,1)} %param.43) | copy-start | bytes 388
  38.4 49.0 %copy-start.85 = (bf16[64]{0:T(256)(128)(2,1)S(1)}, bf16[64]{0:T(256)(128)(2,1)}, u32[]{:S(2)}) copy-start(bf16[64]{0:T(256)(128)(2,1)} %param.33) | copy-start | bytes 388
  38.4 49.2 %copy-start.86 = (bf16[64]{0:T(256)(128)(2,1)S(1)}, bf16[64]{0:T(256)(128)(2,1)}, u32[]{:S(2)}) copy-start(bf16[64]{0:T(256)(128)(2,1)} %param.27) | copy-start | bytes 388
  38.4 49.4 %copy-start.87 = (bf16[64]{0:T(256)(128)(2,1)S(1)}, bf16[64]{0:T(256)(128)(2,1)}, u32[]{:S(2)}) copy-start(bf16[64]{0:T(256)(128)(2,1)} %param.28) | copy-start | bytes 388
  38.5 49.6 %copy-start.88 = (bf16[64]{0:T(256)(128)(2,1)S(1)}, bf16[64]{0:T(256)(128)(2,1)}, u32[]{:S(2)}) copy-start(bf16[64]{0:T(256)(128)(2,1)} %param.49) | copy-start | bytes 388
  38.5 49.9 %copy-start.89 = (bf16[192]{0:T(256)(128)(2,1)S(1)}, bf16[192]{0:T(256)(128)(2,1)}, u32[]{:S(2)}) copy-start(bf16[192]{0:T(256)(128)(2,1)} %param.30) | copy-start | bytes 1156
  38.5 50.1 %copy-start.90 = (bf16[192]{0:T(256)(128)(2,1)S(1)}, bf16[192]{0:T(256)(128)(2,1)}, u32[]{:S(2)}) copy-start(bf16[192]{0:T(256)(128)(2,1)} %param.32) | copy-start | bytes 1156
  39.5 98.1 %all-to-all-start.1 = ((bf16[64,16,256]{2,0,1:T(8,128)(2,1)}), bf16[64,16,256]{2,0,1:T(8,128)(2,1)S(1)}, u32[]{:S(2)}, u32[]{:S(2)}) async-start(bf16[64,16,256]{2,0,1:T(8,128)(2,1)} %copy.133), calls=%async_computation.1 | async-start | bytes 1048576 | tf_op jit(solution)/shard_map/all_to_all | solution.py:250
  46.1 274.8 %all-gather.13.cloned.1.call-start = ((), (), s32[]{:S(2)}) async-start(), calls=%async_computation.15 | async-start | bytes 8912896 | tf_op jit(solution)/shard_map/all_gather | solution.py:178
  46.8 94.6 %copy-start.70 = (f32[256]{0:T(256)}, f32[256]{0:T(256)S(1)}, u32[]{:S(2)}) copy-start(f32[256]{0:T(256)S(1)} %broadcast_multiply_fusion.5) | copy-start | bytes 3076
  137.5 28.9 %copy-start.54 = (f32[1,3072]{1,0:T(1,128)}, f32[1,3072]{1,0:T(1,128)S(1)}, u32[]{:S(2)}) copy-start(f32[1,3072]{1,0:T(1,128)S(1)} %get-tuple-element.89) | copy-start | bytes 36868
  137.5 28.9 %copy-start.56 = (f32[1,3072]{1,0:T(1,128)}, f32[1,3072]{1,0:T(1,128)S(1)}, u32[]{:S(2)}) copy-start(f32[1,3072]{1,0:T(1,128)S(1)} %get-tuple-element.90) | copy-start | bytes 36868
  137.5 28.9 %copy-start.58 = (f32[1,3072]{1,0:T(1,128)}, f32[1,3072]{1,0:T(1,128)S(1)}, u32[]{:S(2)}) copy-start(f32[1,3072]{1,0:T(1,128)S(1)} %get-tuple-element.91) | copy-start | bytes 36868
  139.0 23.4 %copy-start.5 = (f32[64,128,64]{1,2,0:T(8,128)}, f32[64,128,64]{1,2,0:T(8,128)S(1)}, u32[]{:S(2)}) copy-start(f32[64,128,64]{1,2,0:T(8,128)S(1)} %fusion.234) | copy-start | bytes 6291460
  141.4 21.0 %copy-start.7 = (f32[64,128,64]{1,2,0:T(8,128)S(1)}, f32[64,128,64]{1,2,0:T(8,128)}, u32[]{:S(2)}) copy-start(f32[64,128,64]{1,2,0:T(8,128)} %fusion.231) | copy-start | bytes 6291460
  146.3 19.6 %collective-permute-start = (bf16[3072,2]{0,1:T(2,128)(2,1)S(1)}, bf16[3072,2]{0,1:T(2,128)(2,1)S(1)}, u32[]{:S(2)}, u32[]{:S(2)}) collective-permute-start(bf16[3072,2]{0,1:T(2,128)(2,1)S(1)} %slice.103), channel_id=1, source_target_pairs={{0,2},{2,4},{4,6},{6,8},{8,10},{10,12},{12,14},{14,16},{16,18},{18... | collective-permute-start | bytes 36872 | tf_op jit(solution)/shard_map/ppermute | solution.py:18
  174.1 35.9 %all-to-all-start = ((bf16[64,16,256]{2,0,1:T(8,128)(2,1)}), bf16[64,16,256]{2,0,1:T(8,128)(2,1)}, u32[]{:S(2)}, u32[]{:S(2)}) async-start(bf16[64,16,256]{2,0,1:T(8,128)(2,1)} %copy.129), calls=%async_computation | async-start | bytes 1048576 | tf_op jit(solution)/shard_map/all_to_all | solution.py:243
  245.7 9.9 copy-start.91
  249.9 43.1 %all-to-all-start.2 = ((bf16[64,16,256]{2,0,1:T(8,128)(2,1)}), bf16[64,16,256]{2,0,1:T(8,128)(2,1)}, u32[]{:S(2)}, u32[]{:S(2)}) async-start(bf16[64,16,256]{2,0,1:T(8,128)(2,1)} %copy.138), calls=%async_computation.2 | async-start | bytes 1048576 | tf_op jit(solution)/shard_map/all_to_all | solution.py:274
  303.1 36.5 %copy-start.68 = (f32[256]{0:T(256)}, f32[256]{0:T(256)S(1)}, u32[]{:S(2)}) copy-start(f32[256]{0:T(256)S(1)} %broadcast_multiply_fusion.4) | copy-start | bytes 3076
  304.4 35.3 %copy-start.72 = (f32[256]{0:T(256)}, f32[256]{0:T(256)S(1)}, u32[]{:S(2)}) copy-start(f32[256]{0:T(256)S(1)} %add_rsqrt_fusion) | copy-start | bytes 3076
  320.9 11.7 copy-start.20
  332.6 7.0 copy-start.41
  388.3 5.2 copy-start.2
  388.3 5.2 copy-start.4
  388.3 5.2 copy-start.13
  388.3 5.3 copy-start.15
  417.4 22.8 %all-to-all-start.5 = ((bf16[64,16,256]{2,0,1:T(8,128)(2,1)}), bf16[64,16,256]{2,0,1:T(8,128)(2,1)}, u32[]{:S(2)}, u32[]{:S(2)}) async-start(bf16[64,16,256]{2,0,1:T(8,128)(2,1)} %copy.155), calls=%async_computation.6 | async-start | bytes 1048576 | tf_op jit(solution)/shard_map/all_to_all | solution.py:358
  440.2 20.7 %all-to-all-start.4 = ((bf16[64,16,256]{2,0,1:T(8,128)(2,1)}), bf16[64,16,256]{2,0,1:T(8,128)(2,1)}, u32[]{:S(2)}, u32[]{:S(2)}) async-start(bf16[64,16,256]{2,0,1:T(8,128)(2,1)} %copy.148), calls=%async_computation.4 | async-start | bytes 1048576 | tf_op jit(solution)/shard_map/all_to_all | solution.py:351
  446.6 5.1 copy-start.47
  446.6 123.2 %reduce-scatter.19.cloned.1.call-start = ((), (), s32[]{:S(2)}) async-start(), calls=%async_computation.21 | async-start | bytes 1622016
  451.7 5.6 copy-start.61
  451.7 5.6 copy-start.63
  451.7 5.6 copy-start.64
  451.7 5.6 copy-start.81
  451.7 6.5 copy-start.49
  451.7 7.6 copy-start.53
  470.2 5.2 copy-start.33
  470.2 5.2 copy-start.35
  470.2 5.2 copy-start.37
  470.2 5.1 collective-permute-start.1
  474.0 279.0 %all-reduce.23.cloned.1.call-start = ((), (), s32[]{:S(2)}) async-start(), calls=%async_computation.22 | async-start | bytes 315392
  477.5 7.3 copy-start.29
  477.5 7.3 copy-start.22
  477.6 7.3 copy-start.51
  477.6 7.3 copy-start.65
  477.6 7.3 copy-start.67
  477.6 7.3 copy-start.77
  484.8 394.0 %reduce-scatter.11.cloned.1.call-start = ((), (), s32[]{:S(2)}) async-start(), calls=%async_computation.17 | async-start | bytes 540672 | tf_op jit(solution)/shard_map/reduce_scatter | solution.py:429
  487.9 533.4 %reduce-scatter.13.cloned.1.call-start = ((), (), s32[]{:S(2)}) async-start(), calls=%async_computation.18 | async-start | bytes 4325376 | tf_op jit(solution)/shard_map/reduce_scatter | solution.py:430
  490.9 703.6 %reduce-scatter.9.cloned.1.call-start = ((), (), s32[]{:S(2)}) async-start(), calls=%async_computation.16 | async-start | bytes 12976128 | tf_op jit(solution)/shard_map/reduce_scatter | solution.py:424
  498.9 1056.8 %reduce-scatter.15.cloned.1.call-start = ((), (), s32[]{:S(2)}) async-start(), calls=%async_computation.19 | async-start | bytes 17301504 | tf_op jit(solution)/shard_map/reduce_scatter | solution.py:434
  510.0 1407.2 %reduce-scatter.17.cloned.1.call-start = ((), (), s32[]{:S(2)}) async-start(), calls=%async_computation.20 | async-start | bytes 17301504 | tf_op jit(solution)/shard_map/reduce_scatter | solution.py:436
  521.4 7.5 copy-start.45
  (47 other events, 105.4 us)
Sparse Core Ops, SparseCore 0:
  10.3 70.0 all-gather.6
  82.6 42.8 all-gather.8
  127.6 81.0 all-gather.10
  210.7 81.3 all-gather.12
  474.2 95.5 reduce-scatter.18
  577.8 175.2 all-reduce.22
  757.2 121.5 reduce-scatter.10
  881.7 139.5 reduce-scatter.12
  1028.9 165.4 reduce-scatter.8
  1197.2 358.4 reduce-scatter.14
  1558.5 358.6 reduce-scatter.16
where the time goes:
time: 1940 us; the launch traced here: 1930 us
  waiting for transfers between devices  1390 us (72%)
  matrix products  201 us (10%)
  blocking collectives  163 us (8%)
  local copies, waits for them, and re-layouts  89.3 us (5%)
  starting transfers between devices  57.2 us (3%)
  other arithmetic  20.2 us (1%)
    reduce_scatter x1, waiting for transfers between devices, per_device(): lax.psum_scatter(down_weight_grad, ('seq', 'dp'), scatter_dimension=0, ti...  362 us
    reduce_scatter x1, waiting for transfers between devices, per_device(): lax.psum_scatter(up_weight_grad, ('seq', 'dp'), scatter_dimension=0, tile...  361 us
    unnamed x13, waiting for transfers between devices  224 us
    reduce_scatter x1, waiting for transfers between devices, per_device(): lax.psum_scatter(input_weight_grad, ('seq', 'dp'), scatter_dimension=0, t...  173 us
    reduce_scatter x1, waiting for transfers between devices, per_device(): lax.psum_scatter(output_weight_grad, ('seq', 'dp'), scatter_dimension=0,...  143 us
    reduce_scatter x1, waiting for transfers between devices, per_device(): lax.psum_scatter(filter_weight_grad, ('seq', 'dp'), scatter_dimension=1,...  113 us
    dot_general x10, matrix products, contract(): lax.dot_general(left_side, right_side, (((left_dim,), (right_dim,)), ((),...  65.4 us
    unnamed x1, blocking collectives  47.9 us
  transfers between devices with their start and end apart: 18, of which 10 were waited for; matrix products, arithmetic and copies ran while one was open for 11% of the time, Pallas kernels for 0%

commit v1 on v0

v1 whole, which is shorter than its diff:
```python
from functools import partial
import math

import jax
import jax.numpy as jnp
import numpy as np
from jax import lax
from jax.experimental import pallas as pl
from jax.experimental.pallas import tpu as pltpu
from jax.sharding import PartitionSpec as P

FEATURES = 33
LANES = 128
f32 = jnp.float32
bf16 = jnp.bfloat16
highest = lax.Precision.HIGHEST


def swap_seq(value, mask):
    count = lax.axis_size("seq")
    return lax.ppermute(value, "seq", [(i, i ^ mask) for i in range(count)])


def swap_core(value):
    return swap_seq(value, 1)


def swap_y(value):
    return swap_seq(value, 2)


def swap_z(value, mask):
    return swap_seq(value, 4 * mask)


def swap_x(value):
    count = lax.axis_size("dp")
    return lax.ppermute(value, "dp", [(i, i ^ 1) for i in range(count)])


def z_masks(count):
    if count == 4:
        return [3, 1]
    masks, step = [], count // 2
    while step:
        masks.append(step)
        step //= 2
    return masks


def z_order(count):
    order = [0]
    for mask in z_masks(count):
        order = order + [entry ^ mask for entry in order]
    return order


def chip_groups():
    count = lax.axis_size("seq")
    return [list(range(core, count, 2)) for core in range(2)]


def chip_exchange(value):
    return lax.all_to_all(
        value, "seq", split_axis=0, concat_axis=0, tiled=True, axis_index_groups=chip_groups()
    )


def pick(value, index, axis):
    return lax.dynamic_index_in_dim(value, index, axis, keepdims=False)


def both(mine, other, second):
    return jnp.where(second == 0, jnp.stack([mine, other]), jnp.stack([other, mine]))


def place():
    seq = lax.axis_index("seq")
    return seq // 4, (seq // 2) % 2, seq % 2, lax.axis_index("dp")


def by_index(have, order, own):
    bit = 1
    value = jnp.stack([have[order.index(entry)] for entry in range(len(order))])
    while bit < len(order):
        grid = value.reshape(-1, 2, bit, *value.shape[1:])
        turned = jnp.stack([grid[:, 1], grid[:, 0]], axis=1)
        value = jnp.where((own & bit) == 0, grid, turned).reshape(value.shape)
        bit *= 2
    return value


def gather_pieces(piece):
    z, y, _, x = place()
    z_count = lax.axis_size("seq") // 4
    have = piece[None]
    for mask in z_masks(z_count):
        have = jnp.concatenate([have, swap_z(have, mask)], axis=0)
    half = piece.shape[0] // 2
    first, second = have[:, :half], have[:, half:]
    first_y, second_x = swap_y(first), swap_x(second)
    first = jnp.stack([first, first_y])
    second = jnp.stack([second, second_x])
    first_x, second_y = swap_x(first), swap_y(second)
    first = jnp.stack([first, first_x], axis=1)
    second = jnp.stack([second, second_y])
    rel = jnp.concatenate([first, second], axis=3)
    order = z_order(z_count)
    rows = []
    for za in range(z_count):
        rel_z = z ^ za
        slot = sum(jnp.where(rel_z == entry, at, 0) for at, entry in enumerate(order))
        slab = pick(rel, slot, 2)
        slab = jnp.where(y == 0, slab, jnp.stack([slab[1], slab[0]]))
        slab = jnp.where(x == 0, slab, jnp.stack([slab[:, 1], slab[:, 0]], axis=1))
        rows.append(slab)
    return jnp.stack(rows)


def reduce_z(parts):
    z = place()[0]
    z_count = parts.shape[0]
    have = jnp.stack([pick(parts, z ^ rel, 0) for rel in z_order(z_count)])
    for mask in reversed(z_masks(z_count)):
        half = have.shape[0] // 2
        got = swap_z(have[half:].astype(bf16), mask)
        have = have[:half] + got.astype(f32)
    return have[0]


def reduce_pair(first, second):
    _, y, _, x = place()
    first_got = swap_x(pick(first, 1 - x, 2))
    second_got = swap_y(pick(second, 1 - y, 1))
    first = pick(first, x, 2).astype(f32) + first_got.astype(f32)
    second = pick(second, y, 1).astype(f32) + second_got.astype(f32)
    first_got = swap_y(pick(first, 1 - y, 1).astype(bf16))
    second_got = swap_x(pick(second, 1 - x, 1).astype(bf16))
    first = pick(first, y, 1) + first_got.astype(f32)
    second = pick(second, x, 1) + second_got.astype(f32)
    return reduce_z(first), reduce_z(second)


def sum_chips(value):
    for mask in z_masks(lax.axis_size("seq") // 4):
        value = value + swap_z(value, mask)
    value = value + swap_y(value)
    return value + swap_x(value)


def gather_small(value):
    seq = lax.axis_index("seq")
    count = lax.axis_size("seq")
    have = value[None]
    for mask in [1] + [4 * m for m in z_masks(count // 4)] + [2]:
        have = jnp.concatenate([have, swap_seq(have, mask)], axis=0)
    order = [0]
    for mask in [1] + [4 * m for m in z_masks(count // 4)] + [2]:
        order = order + [entry ^ mask for entry in order]
    return by_index(have, order, seq)


def twiddle(k, n):
    angle = -2.0 * math.pi * (k % n) / n
    return math.cos(angle), math.sin(angle)


def c_add(p, q):
    return (p[0] + q[0], q[1] if p[1] is None else (p[1] if q[1] is None else p[1] + q[1]))


def c_sub(p, q):
    if q[1] is None:
        return (p[0] - q[0], p[1])
    return (p[0] - q[0], -q[1] if p[1] is None else p[1] - q[1])


def c_conj(p):
    return (p[0], None if p[1] is None else -p[1])


def c_turn(p, k, n):
    k = k % n
    if k == 0:
        return p
    re, im = p
    if 4 * k == n:
        return (im if im is not None else jnp.zeros_like(re), -re)
    if 2 * k == n:
        return (-re, None if im is None else -im)
    if 4 * k == 3 * n:
        return (-im if im is not None else jnp.zeros_like(re), re)
    c, s = twiddle(k, n)
    if im is None:
        return (re * c, re * s)
    return (re * c - im * s, re * s + im * c)


def real_dft(xs):
    n = len(xs)
    if n == 1:
        return [(xs[0], None)]
    if n == 2:
        if xs[1] is None:
            return [(xs[0], None), (xs[0], None)]
        return [(xs[0] + xs[1], None), (xs[0] - xs[1], None)]
    even, odd = real_dft(xs[0::2]), real_dft(xs[1::2])
    out = [None] * (n // 2 + 1)
    for k in range(n // 4 + 1):
        turned = c_turn(odd[k], k, n)
        out[k] = c_add(even[k], turned)
        if n // 2 - k != k:
            out[n // 2 - k] = c_conj(c_sub(even[k], turned))
    return out


def real_inverse(spec):
    def whole(v):
        n = 2 * (len(v) - 1)
        if n == 2:
            return [v[0][0] + v[1][0], None]
        even, odd = [], []
        for k in range(n // 4 + 1):
            mirror = c_conj(v[n // 2 - k])
            e, o = c_add(v[k], mirror), c_turn(c_sub(v[k], mirror), -k, n)
            if k == 0 or 4 * k == n:
                e, o = (e[0], None), (o[0], None)
            even.append(e)
            odd.append(o)
        even, odd = whole(even), whole(odd)
        return [entry for pair in zip(even, odd) for entry in pair]

    values = whole(spec)
    return values[: len(values) // 2]


def split_terms(value):
    high = value.astype(bf16)
    return high, (value - high.astype(f32)).astype(bf16)


def conv_tables(pairs):
    rows = 4 * pairs
    total = rows * LANES
    slots = np.arange(pairs + 1)
    lanes = np.arange(LANES)
    upper = lanes >= LANES // 2
    angle = -2.0 * np.pi * slots[:, None] / rows * upper[None, :]
    lane_turn = np.stack([np.cos(angle), np.sin(angle)], axis=1).astype(np.float32)
    freq = slots[:, None] + np.where(upper, rows // 2, 0)[None, :]
    angle = -2.0 * np.pi * ((freq[:, None, :] * lanes[None, :, None]) % total) / total
    turn = np.stack([np.cos(angle), np.sin(angle)], axis=1).astype(np.float32)
    angle = 2.0 * np.pi * ((lanes[:, None] * lanes[None, :]) % LANES) / LANES
    c, s = np.cos(angle), np.sin(angle)

    def terms(table):
        table = table.astype(np.float32)
        high = table.astype(bf16)
        low = (table - high.astype(np.float32)).astype(bf16)
        return np.concatenate([high, low], axis=1)

    ahead = terms(np.block([[c, s], [-s, c]]))
    back = terms(np.block([[c, -s], [s, c]]) / total)
    return lane_turn, turn, ahead, back


CHUNK = 16


def put(terms_ref, start, slot, re, im):
    cols = pl.ds(slot * LANES, LANES)
    terms_ref[pl.ds(start, CHUNK), cols] = re
    terms_ref[pl.ds(LANES + start, CHUNK), cols] = im


COLUMNS = 4 * LANES


def table_product(table_ref, terms_ref, out_ref):
    width = terms_ref.shape[1]
    high_table, low_table = table_ref[:, :256], table_ref[:, 256:]
    for at in range(0, width, COLUMNS):
        cols = pl.ds(at, min(COLUMNS, width - at))
        high, low = split_terms(terms_ref[:, cols])
        out_ref[:, cols] = (
            jnp.dot(high_table, low, preferred_element_type=f32)
            + jnp.dot(low_table, high, preferred_element_type=f32)
            + jnp.dot(high_table, high, preferred_element_type=f32)
        )


def lane_sign(shape):
    return jnp.where(lax.broadcasted_iota(jnp.int32, shape, 1) < LANES // 2, 1.0, -1.0).astype(f32)


def transform(x_ref, pairs, lane_ref, turn_ref, ahead_ref, terms_ref, spec_ref):
    sign = lane_sign((CHUNK, LANES))

    def chunk(step, carry):
        start = pl.multiple_of(step * CHUNK, CHUNK)
        xs = [x_ref[j, pl.ds(start, CHUNK), :].astype(f32) for j in range(pairs)]
        spec = real_dft(xs + [None] * pairs)
        for k in range(pairs + 1):
            re, im = spec[k]
            c, s = lane_ref[k, 0:1, :], lane_ref[k, 1:2, :]
            if im is None:
                re, im = re * c, re * s
            else:
                re, im = re * c - im * s, re * s + im * c
            re = pltpu.roll(re, LANES // 2, 1) + sign * re
            im = pltpu.roll(im, LANES // 2, 1) + sign * im
            c, s = turn_ref[k, 0, pl.ds(start, CHUNK), :], turn_ref[k, 1, pl.ds(start, CHUNK), :]
            put(terms_ref, start, k, re * c - im * s, re * s + im * c)
        return carry

    lax.fori_loop(0, LANES // CHUNK, chunk, 0)
    table_product(ahead_ref, terms_ref, spec_ref)


def put_product(terms_ref, pairs, one_ref, other_ref, conjugate):
    def chunk(step, carry):
        start = pl.multiple_of(step * CHUNK, CHUNK)
        for k in range(pairs + 1):
            cols = pl.ds(k * LANES, LANES)
            a, b = one_ref[pl.ds(start, CHUNK), cols], one_ref[pl.ds(LANES + start, CHUNK), cols]
            c, d = other_ref[pl.ds(start, CHUNK), cols], other_ref[pl.ds(LANES + start, CHUNK), cols]
            if conjugate:
                put(terms_ref, start, k, a * c + b * d, b * c - a * d)
            else:
                put(terms_ref, start, k, a * c - b * d, a * d + b * c)
        return carry

    lax.fori_loop(0, LANES // CHUNK, chunk, 0)


def inverse(pairs, lane_ref, turn_ref, back_ref, terms_ref, spec_ref, finish):
    table_product(back_ref, terms_ref, spec_ref)
    sign = lane_sign((CHUNK, LANES))

    def chunk(step, carry):
        start = pl.multiple_of(step * CHUNK, CHUNK)
        spec = []
        for k in range(pairs + 1):
            cols = pl.ds(k * LANES, LANES)
            re, im = spec_ref[pl.ds(start, CHUNK), cols], spec_ref[pl.ds(LANES + start, CHUNK), cols]
            c, s = turn_ref[k, 0, pl.ds(start, CHUNK), :], turn_ref[k, 1, pl.ds(start, CHUNK), :]
            re, im = re * c + im * s, im * c - re * s
            re = pltpu.roll(re, LANES // 2, 1) + sign * re
            im = pltpu.roll(im, LANES // 2, 1) + sign * im
            c, s = lane_ref[k, 0:1, :], lane_ref[k, 1:2, :]
            re, im = re * c + im * s, im * c - re * s
            spec.append((re, None if k in (0, pairs) else im))
        for j, values in enumerate(real_inverse(spec)):
            finish(j, start, values)
        return carry

    lax.fori_loop(0, LANES // CHUNK, chunk, 0)


def window_of(j, start, delta, length):
    lane = lax.broadcasted_iota(jnp.int32, (CHUNK, LANES), 1)
    row = lax.broadcasted_iota(jnp.int32, (CHUNK, LANES), 0)
    position = (2 * j + lane // (LANES // 2)) * LANES + start + row
    return jnp.exp(-(position.astype(f32) / (length - 1)) * delta) + 0.05


def filter_body(pairs, h_ref, w_ref, delta_ref, lane_ref, turn_ref, ahead_ref, spec_ref, low_ref, terms_ref):
    delta = delta_ref[...]
    for j in range(pairs):
        rows = jnp.dot(h_ref[j], w_ref[...], precision=highest, preferred_element_type=f32)
        window = jnp.concatenate(
            [window_of(j, start, delta, 2 * pairs * LANES) for start in range(0, LANES, CHUNK)], axis=0
        )
        low_ref[j] = (rows * window).astype(bf16).astype(f32)
    transform(low_ref, pairs, lane_ref, turn_ref, ahead_ref, terms_ref, spec_ref)


def forward_body(
    pairs, x_ref, kernel_ref, skip_ref, lane_ref, turn_ref, ahead_ref, back_ref, out_ref, spec_ref, terms_ref, work_ref
):
    transform(x_ref, pairs, lane_ref, turn_ref, ahead_ref, terms_ref, spec_ref)
    put_product(terms_ref, pairs, spec_ref, kernel_ref, False)
    skip = skip_ref[...]

    def finish(j, start, values):
        rows = pl.ds(start, CHUNK)
        out_ref[j, rows, :] = (values + x_ref[j, rows, :].astype(f32) * skip).astype(bf16)

    inverse(pairs, lane_ref, turn_ref, back_ref, terms_ref, work_ref, finish)


def backward_body(
    pairs,
    g_ref,
    x_ref,
    x_spec_ref,
    kernel_ref,
    skip_ref,
    h_ref,
    w_ref,
    delta_ref,
    lane_ref,
    turn_ref,
    ahead_ref,
    back_ref,
    gx_ref,
    gh_ref,
    gw_ref,
    gskip_ref,
    terms_ref,
    spec_ref,
    work_ref,
    pre_ref,
):
    transform(g_ref, pairs, lane_ref, turn_ref, ahead_ref, terms_ref, spec_ref)
    put_product(terms_ref, pairs, spec_ref, kernel_ref, True)
    skip = skip_ref[...]

    def finish_x(j, start, values):
        rows = pl.ds(start, CHUNK)
        gx_ref[j, rows, :] = (values + g_ref[j, rows, :].astype(f32) * skip).astype(bf16)

    inverse(pairs, lane_ref, turn_ref, back_ref, terms_ref, work_ref, finish_x)
    put_product(terms_ref, pairs, spec_ref, x_spec_ref, True)
    delta = delta_ref[...]

    def finish_kernel(j, start, values):
        window = window_of(j, start, delta, 2 * pairs * LANES)
        pre_ref[j, pl.ds(start, CHUNK), :] = values.astype(bf16).astype(f32) * window

    inverse(pairs, lane_ref, turn_ref, back_ref, terms_ref, work_ref, finish_kernel)
    gw_ref[...] = jnp.zeros_like(gw_ref)
    gskip_ref[...] = jnp.zeros_like(gskip_ref)
    for j in range(pairs):
        pre = pre_ref[j]
        gh = lax.dot_general(
            pre, w_ref[...], (((1,), (1,)), ((), ())), precision=highest, preferred_element_type=f32
        )
        gh_ref[j] = gh.astype(bf16)
        gw_ref[...] += lax.dot_general(
            h_ref[j], pre, (((0,), (0,)), ((), ())), precision=highest, preferred_element_type=f32
        )
        gskip_ref[...] += jnp.sum(g_ref[j].astype(f32) * x_ref[j].astype(f32), axis=0, keepdims=True)


VMEM_BYTES = 50 * 1024 * 1024


def whole_call(body, outs, scratch, flops, moved, *operands):
    return pl.pallas_call(
        body,
        out_shape=outs,
        scratch_shapes=scratch,
        compiler_params=pltpu.CompilerParams(vmem_limit_bytes=VMEM_BYTES),
        cost_estimate=pl.CostEstimate(flops=flops, bytes_accessed=moved, transcendentals=0),
    )(*operands)


def spec_shape(pairs):
    return (256, (pairs + 1) * LANES)


def conv_filter(hidden, weight, delta, tables):
    pairs = hidden.shape[0]
    lane_turn, turn, ahead, _ = tables
    return whole_call(
        partial(filter_body, pairs),
        jax.ShapeDtypeStruct(spec_shape(pairs), f32),
        [pltpu.VMEM((pairs, LANES, LANES), f32), pltpu.VMEM(spec_shape(pairs), f32)],
        10**9,
        8 * 10**6,
        hidden,
        weight,
        delta,
        lane_turn,
        turn,
        ahead,
    )


def conv_forward(x, kernel_spec, skip, tables):
    pairs = x.shape[0]
    return whole_call(
        partial(forward_body, pairs),
        (jax.ShapeDtypeStruct(x.shape, bf16), jax.ShapeDtypeStruct(spec_shape(pairs), f32)),
        [pltpu.VMEM(spec_shape(pairs), f32), pltpu.VMEM(spec_shape(pairs), f32)],
        2 * 10**9,
        10 * 10**6,
        x,
        kernel_spec,
        skip,
        *tables,
    )


def conv_backward(g, x, x_spec, kernel_spec, skip, hidden, weight, delta, tables):
    pairs = x.shape[0]
    return whole_call(
        partial(backward_body, pairs),
        (
            jax.ShapeDtypeStruct(x.shape, bf16),
            jax.ShapeDtypeStruct(x.shape, bf16),
            jax.ShapeDtypeStruct((LANES, LANES), f32),
            jax.ShapeDtypeStruct((1, LANES), f32),
        ),
        [
            pltpu.VMEM(spec_shape(pairs), f32),
            pltpu.VMEM(spec_shape(pairs), f32),
            pltpu.VMEM(spec_shape(pairs), f32),
            pltpu.VMEM(x.shape, f32),
        ],
        4 * 10**9,
        16 * 10**6,
        g,
        x,
        x_spec,
        kernel_spec,
        skip,
        hidden,
        weight,
        delta,
        *tables,
    )


def plain_spectrum(x, length):
    pairs, _, lanes = x.shape
    flat = x.astype(f32).reshape(pairs, LANES, 2, lanes // 2).transpose(3, 0, 2, 1)
    tables = spectral_tables(length // 64, LANES)
    return forward_transform(flat.reshape(lanes // 2, length // LANES, LANES), tables)


def plain_inverse(re, im, length):
    tables = spectral_tables(length // 64, LANES)
    back = inverse_transform(re, im, tables, length // LANES)
    channels = back.shape[0]
    back = back.reshape(channels, length // 256, 2, LANES).transpose(1, 3, 2, 0)
    return back.reshape(length // 256, LANES, 2 * channels)


def spectral_tables(rows_total, col_count):
    total_size = rows_total * col_count
    row_index = jnp.arange(rows_total, dtype=jnp.int32)
    col_index = jnp.arange(col_count, dtype=jnp.int32)
    row_angle = (row_index[:, None] * row_index[None, :] % rows_total).astype(f32) * (
        2.0 * math.pi / rows_total
    )
    col_angle = (col_index[:, None] * col_index[None, :] % col_count).astype(f32) * (
        2.0 * math.pi / col_count
    )
    twist_angle = (row_index[:, None] * col_index[None, :]).astype(f32) * (2.0 * math.pi / total_size)
    return (
        jnp.cos(row_angle),
        -jnp.sin(row_angle),
        jnp.cos(twist_angle),
        -jnp.sin(twist_angle),
        jnp.cos(col_angle),
        -jnp.sin(col_angle),
        total_size,
    )


def forward_transform(signal, tables):
    row_cos, row_sin, twist_cos, twist_sin, col_cos, col_sin, _ = tables
    half_rows = signal.shape[1]
    product = partial(jnp.einsum, precision=highest)
    first_re = product("ka,cab->ckb", row_cos[:, :half_rows], signal)
    first_im = product("ka,cab->ckb", row_sin[:, :half_rows], signal)
    turned_re = first_re * twist_cos - first_im * twist_sin
    turned_im = first_re * twist_sin + first_im * twist_cos
    out_re = product("ckb,bm->ckm", turned_re, col_cos) - product("ckb,bm->ckm", turned_im, col_sin)
    out_im = product("ckb,bm->ckm", turned_re, col_sin) + product("ckb,bm->ckm", turned_im, col_cos)
    return (out_re, out_im)


def inverse_transform(spec_re, spec_im, tables, half_rows):
    row_cos, row_sin, twist_cos, twist_sin, col_cos, col_sin, total_size = tables
    product = partial(jnp.einsum, precision=highest)
    back_re = product("ckm,mb->ckb", spec_re, col_cos) + product("ckm,mb->ckb", spec_im, col_sin)
    back_im = product("ckm,mb->ckb", spec_im, col_cos) - product("ckm,mb->ckb", spec_re, col_sin)
    untwist_re = back_re * twist_cos + back_im * twist_sin
    untwist_im = back_im * twist_cos - back_re * twist_sin
    real_part = product("ak,ckb->cab", row_cos[:half_rows], untwist_re) + product(
        "ak,ckb->cab", row_sin[:half_rows], untwist_im
    )
    return real_part / total_size


def plain_window(shape, delta, length):
    pairs, _, lanes = shape
    position = jnp.arange(length, dtype=jnp.int32).reshape(pairs, 2, LANES, 1).astype(f32)
    window = jnp.exp(-(position / (length - 1)) * delta[0, : lanes // 2]) + 0.05
    return window.transpose(0, 2, 1, 3).reshape(shape)


def plain_filter(hidden, weight, delta):
    pairs = hidden.shape[0]
    length = 256 * pairs
    rows = jnp.einsum("jbh,hc->jbc", hidden, weight, precision=highest)
    rows = (rows * plain_window(rows.shape, delta, length)).astype(bf16)
    return plain_spectrum(rows, length)


def plain_forward(x, kernel_spec, skip):
    length = 256 * x.shape[0]
    re, im = plain_spectrum(x, length)
    kre, kim = kernel_spec
    out = plain_inverse(re * kre - im * kim, re * kim + im * kre, length)
    return (out + x.astype(f32) * skip).astype(bf16), (re, im)


def plain_backward(g, x, x_spec, kernel_spec, skip, hidden, weight, delta):
    length = 256 * x.shape[0]
    re, im = plain_spectrum(g, length)
    kre, kim = kernel_spec
    xre, xim = x_spec
    gx = plain_inverse(re * kre + im * kim, im * kre - re * kim, length) + g.astype(f32) * skip
    pre = plain_inverse(re * xre + im * xim, im * xre - re * xim, length).astype(bf16).astype(f32)
    pre = pre * plain_window(pre.shape, delta, length)
    gh = jnp.einsum("jbc,hc->jbh", pre, weight, precision=highest)
    gw = jnp.einsum("jbh,jbc->hc", hidden, pre, precision=highest)
    gskip = jnp.sum(g.astype(f32) * x.astype(f32), axis=(0, 1))[None]
    return gx.astype(bf16), gh.astype(bf16), gw, gskip


def feed_body(nt_ref, ct_ref, up_ref, bias_ref, down_ref, y_ref, gx_ref, gdown_ref, gup_ref, gbias_ref):
    @pl.when(pl.program_id(0) == 0)
    def _():
        y_ref[...] = jnp.zeros_like(y_ref)
        gx_ref[...] = jnp.zeros_like(gx_ref)

    nt, ct, up, down = nt_ref[...], ct_ref[...], up_ref[...], down_ref[...]
    before = jnp.dot(nt, up, preferred_element_type=f32) + bias_ref[...]
    cdf = 0.5 * (1.0 + lax.erf(before * math.sqrt(0.5)))
    active = (before * cdf).astype(bf16)
    slope = cdf + before * (jnp.exp(-0.5 * before * before) * (1.0 / math.sqrt(2.0 * math.pi)))
    g_act = lax.dot_general(ct, down, (((1,), (1,)), ((), ())), preferred_element_type=f32)
    g_before = (g_act * slope).astype(bf16)
    y_ref[...] += jnp.dot(active, down, preferred_element_type=f32)
    gx_ref[...] += lax.dot_general(g_before, up, (((1,), (1,)), ((), ())), preferred_element_type=f32)
    gdown_ref[...] = lax.dot_general(
        active, ct, (((0,), (0,)), ((), ())), preferred_element_type=f32
    ).astype(bf16)
    gup_ref[...] = lax.dot_general(
        nt, g_before, (((0,), (0,)), ((), ())), preferred_element_type=f32
    ).astype(bf16)
    gbias_ref[...] = jnp.sum(g_before.astype(f32), axis=0, keepdims=True)


def feed_forward(nt, ct, up, bias, down):
    rows, width = nt.shape
    hidden = up.shape[1]
    block = min(256, hidden)
    return pl.pallas_call(
        feed_body,
        grid=(hidden // block,),
        in_specs=[
            pl.BlockSpec((rows, width), lambda i: (0, 0)),
            pl.BlockSpec((rows, width), lambda i: (0, 0)),
            pl.BlockSpec((width, block), lambda i: (0, i)),
            pl.BlockSpec((1, block), lambda i: (0, i)),
            pl.BlockSpec((block, width), lambda i: (i, 0)),
        ],
        out_specs=[
            pl.BlockSpec((rows, width), lambda i: (0, 0)),
            pl.BlockSpec((rows, width), lambda i: (0, 0)),
            pl.BlockSpec((block, width), lambda i: (i, 0)),
            pl.BlockSpec((width, block), lambda i: (0, i)),
            pl.BlockSpec((1, block), lambda i: (0, i)),
        ],
        out_shape=[
            jax.ShapeDtypeStruct((rows, width), f32),
            jax.ShapeDtypeStruct((rows, width), f32),
            jax.ShapeDtypeStruct((hidden, width), bf16),
            jax.ShapeDtypeStruct((width, hidden), bf16),
            jax.ShapeDtypeStruct((1, hidden), f32),
        ],
        compiler_params=pltpu.CompilerParams(vmem_limit_bytes=VMEM_BYTES),
        cost_estimate=pl.CostEstimate(
            flops=12 * rows * width * hidden,
            bytes_accessed=8 * width * hidden + 12 * rows * width,
            transcendentals=2 * rows * hidden,
        ),
    )(nt, ct, up, bias, down)


def norm_forward(values, norm_gain, norm_offset):
    center = values - jnp.mean(values, axis=-1, keepdims=True)
    inverse_root = lax.rsqrt(jnp.mean(center * center, axis=-1, keepdims=True) + 1e-05)
    normed = center * inverse_root
    return (normed * norm_gain + norm_offset, normed, inverse_root)


def norm_backward(upstream, normed, inverse_root, norm_gain):
    scaled = upstream * norm_gain
    centered = (
        scaled
        - jnp.mean(scaled, axis=-1, keepdims=True)
        - normed * jnp.mean(scaled * normed, axis=-1, keepdims=True)
    )
    return centered * inverse_root


def contract(left_side, right_side, left_dim, right_dim):
    return lax.dot_general(
        left_side, right_side, (((left_dim,), (right_dim,)), ((), ())), preferred_element_type=f32
    )


def trunk_hidden(trunk, features):
    embed_weight, embed_bias, hidden_weight, hidden_bias, last_weight, last_bias, frequency = trunk
    layer_out = jnp.sin(frequency * (jnp.dot(features, embed_weight, precision=highest) + embed_bias))
    layer_out = jnp.sin(frequency * (jnp.dot(layer_out, hidden_weight, precision=highest) + hidden_bias))
    return jnp.sin(frequency * (jnp.dot(layer_out, last_weight, precision=highest) + last_bias))


def to_owners(value, chips):
    tokens, width = value.shape
    channels = width // chips
    grid = value.reshape(tokens // 256, 2, LANES, chips, channels)
    return grid.transpose(3, 0, 2, 1, 4).reshape(chips, tokens // 256, LANES, 2 * channels)


def from_owners(value):
    chips, pairs, _, lanes = value.shape
    grid = value.reshape(chips, pairs, LANES, 2, lanes // 2)
    return grid.transpose(1, 3, 2, 0, 4).reshape(pairs * 256, chips * (lanes // 2))


def exchange(value):
    return chip_exchange(value)


def flatten(*values):
    return jnp.concatenate([value.reshape(-1) for value in values])


def unflatten(flat, shapes):
    out, at = [], 0
    for shape in shapes:
        size = int(np.prod(shape))
        out.append(flat[at : at + size].reshape(shape))
        at += size
    return out


def to_rows(flat):
    rows = -(-flat.shape[0] // 1024) * 8
    return jnp.pad(flat, (0, rows * LANES - flat.shape[0])).reshape(rows, LANES)


def plain_device(
    tokens,
    cotangent,
    pre_gain,
    pre_offset,
    input_weight,
    input_bias,
    short_weight,
    short_bias,
    skip_weight,
    embed_weight,
    embed_bias,
    hidden_weight,
    hidden_bias,
    last_weight,
    last_bias,
    frequency,
    filter_weight,
    output_weight,
    output_bias,
    post_gain,
    post_offset,
    up_weight,
    up_bias,
    down_weight,
    down_bias,
):
    seq_count = lax.axis_size("seq")
    seq_index = lax.axis_index("seq")
    z, y, core, x = place()
    chips = seq_count // 2
    z_count = seq_count // 4
    chip = seq_index // 2
    tok_count = tokens.shape[1]
    width = tokens.shape[2]
    length = tok_count * seq_count
    channels = width // seq_count
    ff = up_weight.shape[1]
    hidden_own = ff // seq_count
    half = width // 2
    pairs = length // 256
    kernels = 2 * channels == LANES

    mine = jnp.stack([tokens[0], cotangent[0]])
    other = swap_core(mine)
    pair = both(mine, other, core)
    tok = pair[:, 0].reshape(2 * tok_count, width)
    cot = pair[:, 1].reshape(2 * tok_count, width)

    def half_columns(value, groups, run):
        rows = value.shape[0]
        grid = value.reshape(rows, groups, chips, 2, run)
        return [grid[:, :, :, side].reshape(rows, groups * chips * run) for side in range(2)]

    def own_rows(value, groups, run):
        sides = half_columns(value, groups, run)
        keep = jnp.where(core == 0, sides[0], sides[1])
        got = swap_core(jnp.where(core == 0, sides[1], sides[0]))
        return jnp.where(core == x, keep, got)

    in_piece = own_rows(input_weight, 3, channels)
    in_half = gather_pieces(in_piece).reshape(width, 3 * half)
    small_shapes = [(width // seq_count,)] * 2 + [(3, channels), (3, 3, channels), (3, channels)]
    small_shapes += [(width // seq_count,)] * 3 + [(hidden_own,), (width // seq_count,)]
    smalls = flatten(
        pre_gain, pre_offset, input_bias, short_weight, short_bias, output_bias, post_gain, post_offset, up_bias, down_bias
    )
    shapes = [v.shape for v in (pre_gain, pre_offset, input_bias, short_weight, short_bias)]
    shapes += [v.shape for v in (output_bias, post_gain, post_offset, up_bias, down_bias)]
    small_rows = to_rows(smalls)
    small_all = gather_small(small_rows.reshape(-1)).astype(f32)
    columns, at = [], 0
    for shape in shapes:
        size = int(np.prod(shape))
        columns.append(small_all[:, at : at + size])
        at += size

    def halved(value, run):
        lead = value.shape[:-1]
        return pick(value.reshape(*lead, -1, 2, run), core, len(lead) + 1).reshape(*lead, -1)

    pre_gain_full, pre_offset_full = columns[0].reshape(-1), columns[1].reshape(-1)
    input_bias_own = halved(columns[2].reshape(3, width), channels).reshape(-1)
    short_full = columns[3].reshape(seq_count, 3, -1).transpose(1, 0, 2).reshape(3, 3, width)
    short_taps = halved(short_full, channels).reshape(3, -1)
    short_bias_own = halved(columns[4].reshape(3, width), channels).reshape(-1)
    output_bias_full = columns[5].reshape(-1)
    post_gain_full, post_offset_full = columns[6].reshape(-1), columns[7].reshape(-1)
    up_bias_own = halved(columns[8].reshape(-1), hidden_own)
    down_bias_full = columns[9].reshape(-1)

    out_rows = output_weight.shape[0] // 2
    up_piece = own_rows(up_weight, 1, hidden_own)
    out_piece = pick(output_weight.reshape(2, out_rows, width), x, 0)
    down_piece = pick(down_weight.reshape(2, hidden_own // 2, width), x, 0)
    up_half = gather_pieces(up_piece).reshape(width, ff // 2)
    n_out, n_down = out_rows // 2, hidden_own // 4
    mixed_piece = jnp.concatenate(
        [out_piece[:n_out], down_piece[:n_down], out_piece[n_out:], down_piece[n_down:]], axis=0
    )
    later = gather_pieces(mixed_piece)
    later = later.reshape(chips, 2, 2, n_out + n_down, width)
    out_half = later[:, :, :, :n_out].reshape(half, width)
    down_half = later[:, :, :, n_out:].reshape(ff // 2, width)

    positions = (seq_index * tok_count + jnp.arange(tok_count, dtype=jnp.int32)).astype(f32)
    relative = positions / (length - 1)
    phases = positions * (2.0 * math.pi / length)
    band_count = (FEATURES - 1) // 2
    band_freq = jnp.linspace(0.0001, band_count - 1, band_count).astype(f32)
    angles = phases[:, None] * band_freq[None, :]
    features = jnp.concatenate([relative[:, None], jnp.cos(angles), -jnp.sin(angles)], axis=1)
    trunk = (embed_weight, embed_bias, hidden_weight, hidden_bias, last_weight, last_bias, frequency)
    hidden_rows, trunk_pull = jax.vjp(partial(trunk_hidden, features=features), trunk)
    units = hidden_rows.shape[1]
    own_pairs = tok_count // 256
    packed = hidden_rows.reshape(own_pairs, 2, LANES, units).transpose(0, 2, 1, 3)
    packed = packed.reshape(own_pairs, LANES, 2 * units)
    filter_hidden = lax.all_gather(packed, "seq", axis=0, tiled=True)
    filter_own = filter_weight.astype(f32)
    zero = jnp.zeros_like(filter_own)
    filter_pair = jnp.concatenate(
        [jnp.concatenate([filter_own, zero], axis=1), jnp.concatenate([zero, filter_own], axis=1)], axis=0
    )
    deltas = jnp.linspace(math.log(0.01) / 1.5, math.log(0.01) / 0.3, width).astype(f32)
    delta_own = jnp.abs(lax.dynamic_slice_in_dim(deltas, seq_index * channels, channels))
    delta_pair = jnp.concatenate([delta_own, delta_own])[None]
    skip_own = skip_weight.astype(f32)
    skip_pair = jnp.concatenate([skip_own, skip_own])[None]
    if kernels:
        tables = tuple(jnp.asarray(t) for t in conv_tables(pairs))
        kernel_spec = conv_filter(filter_hidden, filter_pair, delta_pair, tables)
    else:
        kernel_spec = plain_filter(filter_hidden, filter_pair, delta_pair)

    rows = 2 * tok_count
    inputs = tok.astype(f32)
    normed_one, unit_one, inverse_one = norm_forward(inputs, pre_gain_full, pre_offset_full)
    normed_low = normed_one.astype(bf16)
    projected_low = (contract(normed_low, in_half, 1, 0) + input_bias_own).astype(bf16)
    shift = [(i, i + 2) for i in range(seq_count - 2)]
    earlier = lax.ppermute(projected_low[rows - 2 :], "seq", shift)
    extended = jnp.concatenate([earlier, projected_low], axis=0).astype(f32)
    convolved = (
        short_taps[0] * extended[:rows]
        + short_taps[1] * extended[1 : rows + 1]
        + short_taps[2] * extended[2:]
        + short_bias_own
    )
    first_part, second_part, values_part = (convolved[:, i * half : (i + 1) * half] for i in range(3))
    gated_low = (values_part * second_part).astype(bf16)
    gated_ch = exchange(to_owners(gated_low, chips)).reshape(pairs, LANES, 2 * channels)
    if kernels:
        mixed_ch, gated_spec = conv_forward(gated_ch, kernel_spec, skip_pair, tables)
    else:
        mixed_ch, gated_spec = plain_forward(gated_ch, kernel_spec, skip_pair)
    chip_shape = (chips, rows // 256, LANES, 2 * channels)
    mixed_tok = from_owners(exchange(mixed_ch.reshape(chip_shape))).astype(f32)
    mix_low = (mixed_tok * first_part).astype(bf16)
    branch_part = contract(mix_low, out_half, 1, 0)
    branch = branch_part + swap_core(branch_part) + output_bias_full
    hidden = inputs + branch

    normed_two, unit_two, inverse_two = norm_forward(hidden, post_gain_full, post_offset_full)
    normed_two_low = normed_two.astype(bf16)
    down_part, back_part, down_grad, up_grad, up_bias_grad = feed_forward(
        normed_two_low, cot, up_half, up_bias_own[None], down_half
    )

    def own_tokens(value):
        return lax.dynamic_slice_in_dim(value, core * tok_count, tok_count, 0)

    def other_tokens(value):
        return lax.dynamic_slice_in_dim(value, (1 - core) * tok_count, tok_count, 0)

    result = own_tokens(hidden) + (
        own_tokens(down_part) + swap_core(other_tokens(down_part)) + down_bias_full
    )
    up_grad = up_grad.reshape(z_count, 2, 2, 2, -1, ff // 2).transpose(0, 1, 3, 2, 4, 5)
    down_sum, up_sum = reduce_pair(down_grad.reshape(z_count, 2, 2, hidden_own // 2, width), up_grad)

    cot_f = cot.astype(f32)
    down_bias_grad = jnp.sum(cot_f, axis=0)
    normed_two_grad = back_part + swap_core(back_part)
    post_gain_grad = jnp.sum(normed_two_grad * unit_two, axis=0)
    post_offset_grad = jnp.sum(normed_two_grad, axis=0)
    hidden_grad = cot_f + norm_backward(normed_two_grad, unit_two, inverse_two, post_gain_full)
    branch_low = hidden_grad.astype(bf16)
    output_bias_grad = jnp.sum(branch_low.astype(f32), axis=0)
    gate_grad = contract(branch_low, out_half, 1, 1)
    mixed_grad_low = (gate_grad * first_part).astype(bf16)
    first_grad = gate_grad * mixed_tok
    mixed_grad_ch = exchange(to_owners(mixed_grad_low, chips)).reshape(pairs, LANES, 2 * channels)
    back_args = (mixed_grad_ch, gated_ch, gated_spec, kernel_spec, skip_pair, filter_hidden, filter_pair, delta_pair)
    if kernels:
        gated_back, hidden_back, filter_square, skip_line = conv_backward(*back_args, tables)
    else:
        gated_back, hidden_back, filter_square, skip_line = plain_backward(*back_args)
    gated_grad = from_owners(exchange(gated_back.reshape(chip_shape))).astype(f32)
    output_grad = contract(mix_low, branch_low, 0, 0)

    hidden_got = lax.all_to_all(
        hidden_back.reshape(seq_count, own_pairs * LANES, 2 * units), "seq", split_axis=0, concat_axis=0, tiled=True
    )
    hidden_sum = jnp.sum(hidden_got.astype(f32), axis=0)
    hidden_sum = hidden_sum.reshape(own_pairs, LANES, 2, units).transpose(0, 2, 1, 3).reshape(tok_count, units)
    (trunk_grad,) = trunk_pull(hidden_sum)
    filter_grad = filter_square[:units, :channels] + filter_square[units:, channels:]
    skip_grad = skip_line[:, :channels] + skip_line[:, channels:]
    own_grad = jnp.concatenate([filter_grad, skip_grad], axis=0)
    own_grad = own_grad + swap_x(own_grad)
    own_grad = pick(own_grad.reshape(-1, 2, channels // 2), x, 1)

    conv_grad_low = jnp.concatenate(
        [first_grad, gated_grad * values_part, gated_grad * second_part], axis=1
    ).astype(bf16)
    back_shift = [(i + 2, i) for i in range(seq_count - 2)]
    following = lax.ppermute(conv_grad_low[:2], "seq", back_shift)
    conv_grad = conv_grad_low.astype(f32)
    grad_ext = jnp.concatenate([conv_grad_low, following], axis=0).astype(f32)
    projected_grad_low = (
        short_taps[0] * grad_ext[2:] + short_taps[1] * grad_ext[1 : rows + 1] + short_taps[2] * grad_ext[:rows]
    ).astype(bf16)
    short_weight_grad = jnp.stack(
        [jnp.sum(conv_grad * extended[tap : tap + rows], axis=0) for tap in range(3)]
    )
    short_bias_grad = jnp.sum(conv_grad, axis=0)
    input_bias_grad = jnp.sum(projected_grad_low.astype(f32), axis=0)
    input_grad = contract(normed_low, projected_grad_low, 0, 0)
    normed_one_part = contract(projected_grad_low, in_half, 1, 1)
    normed_one_grad = own_tokens(normed_one_part) + swap_core(other_tokens(normed_one_part))
    unit_own = own_tokens(unit_one)
    pre_gain_grad = jnp.sum(normed_one_grad * unit_own, axis=0)
    pre_offset_grad = jnp.sum(normed_one_grad, axis=0)
    tokens_grad = own_tokens(hidden_grad) + norm_backward(
        normed_one_grad, unit_own, own_tokens(inverse_one), pre_gain_full
    )

    in_low = input_grad.astype(bf16).reshape(z_count, 2, 2, 2, -1, 3 * half).transpose(0, 1, 3, 2, 4, 5)
    in_sum = jnp.stack(reduce_pair(in_low[:, :, :, 0], in_low[:, :, :, 1]))
    out_low = output_grad.astype(bf16).reshape(z_count, 2, 2, -1, width)
    split = out_low.shape[3] // 2
    out_sum = jnp.concatenate(reduce_pair(out_low[:, :, :, :split], out_low[:, :, :, split:]), axis=0)

    def whole_columns(value, groups, run):
        got = swap_core(pick(value, 1 - core, 0))
        mine_part = pick(value, core, 0)
        n = mine_part.shape[0]
        grid = both(mine_part, got, core).reshape(2, n, groups, chips, run)
        return grid.transpose(1, 2, 3, 0, 4).reshape(n, -1)

    in_rows = whole_columns(in_sum, 3, channels)
    up_rows_sum = whole_columns(up_sum, 1, hidden_own)

    chip_wide = [post_gain_grad, post_offset_grad, down_bias_grad, output_bias_grad]
    own_wide = [pre_gain_grad, pre_offset_grad, *trunk_grad]
    half_wide = [up_bias_grad.reshape(-1), input_bias_grad, short_weight_grad, short_bias_grad]
    own_flat, half_flat = to_rows(flatten(*own_wide)), to_rows(flatten(*half_wide))
    summed = sum_chips(jnp.concatenate([to_rows(flatten(*chip_wide)), own_flat, half_flat], axis=0))
    n_chip = to_rows(flatten(*chip_wide)).shape[0]
    chip_sum = summed[:n_chip].reshape(-1)
    got = swap_core(summed[n_chip:])
    own_sum = (summed[n_chip:] + got)[: own_flat.shape[0]].reshape(-1)
    half_sum = both(summed[n_chip + own_flat.shape[0] :], got[own_flat.shape[0] :], core).reshape(2, -1)
    chip_sums = unflatten(chip_sum, [v.shape for v in chip_wide])
    own_sums = unflatten(own_sum, [v.shape for v in own_wide])
    half_sums = [
        unflatten(half_sum[side], [v.shape for v in half_wide]) for side in range(2)
    ]

    def joined(index, groups, run):
        pair_of = jnp.stack([half_sums[side][index].reshape(groups, chips, run) for side in range(2)], axis=2)
        return pair_of.reshape(groups, -1)

    block_index = seq_index * 2 + x

    def own_block(value, axis=0):
        size = value.shape[axis] // (2 * seq_count)
        return lax.dynamic_slice_in_dim(value, block_index * size, size, axis)

    up_bias_sum = joined(0, 1, hidden_own).reshape(-1)
    input_bias_sum = joined(1, 3, channels).reshape(-1)
    short_weight_sum = joined(2, 9, channels).reshape(3, -1)
    short_bias_sum = joined(3, 3, channels).reshape(-1)
    return (
        result.astype(bf16)[None],
        tokens_grad.astype(bf16)[None],
        own_block(own_sums[0]),
        own_block(own_sums[1]),
        in_rows,
        own_block(input_bias_sum),
        own_block(short_weight_sum, 1),
        own_block(short_bias_sum),
        own_grad[units],
        *own_sums[2:],
        own_grad[:units],
        out_sum,
        own_block(chip_sums[3]),
        own_block(chip_sums[0]),
        own_block(chip_sums[1]),
        up_rows_sum,
        own_block(up_bias_sum),
        down_sum,
        own_block(chip_sums[2]),
    )


def after(earlier, value):
    return lax.optimization_barrier((earlier, value))[1]


def gather_z(piece):
    have = piece[None]
    for mask in z_masks(lax.axis_size("seq") // 4):
        have = jnp.concatenate([have, swap_z(have, mask)], axis=0)
    return have


def gather_near(have):
    half = have.shape[1] // 2
    first, second = have[:, :half], have[:, half:]
    return jnp.stack([first, swap_y(first)]), jnp.stack([second, swap_x(second)])


def gather_far(near):
    first, second = near
    return first, swap_x(first), second, swap_y(second)


def reduce_step(kept, got):
    return kept.astype(f32) + got.astype(f32)


def reduce_far(total):
    for mask in reversed(z_masks(lax.axis_size("seq") // 4)):
        half = total.shape[0] // 2
        total = total[:half] + swap_z(total[half:].astype(bf16), mask).astype(f32)
    return total[0]


def reduce_rows(kept, sent, first, second):
    total = reduce_step(kept, first(sent))
    total = total[0] + second(total[1].astype(bf16)).astype(f32)
    return reduce_far(total)


def place_pieces(out_ref, pieces, scalars, chips, span):
    first, first_far, second, second_far = pieces
    x = scalars[0]
    half = span // 2
    z_count = chips // 2
    for slot in range(z_count):
        for yr in range(2):
            base = scalars[2 + yr * z_count + slot] * (2 * span)
            source = second_far if yr else second
            for xr in range(2):
                at = pl.multiple_of(base + (x if xr == 0 else 1 - x) * span, span)
                out_ref[pl.ds(at, half), :] = (first_far if xr else first)[yr, slot]
                out_ref[pl.ds(pl.multiple_of(at + half, half), half), :] = source[xr, slot]


def route_rows(grad_ref, kept_ref, sent_ref, scalars, chips, inner, by_x):
    x = scalars[0]
    z_count = chips // 2
    rows = grad_ref.shape[0] // (2 * chips * inner)
    for slot in range(z_count):
        for yr in range(2):
            base = scalars[2 + yr * z_count + slot] * (2 * inner * rows)
            for xr in range(2):
                target, lead = ((sent_ref if xr else kept_ref), yr) if by_x else ((sent_ref if yr else kept_ref), xr)
                for part in range(inner):
                    at = pl.multiple_of(base + part * 2 * rows + (x if xr == 0 else 1 - x) * rows, rows)
                    target[lead, slot, part] = grad_ref[pl.ds(at, rows), :].astype(bf16)


HALO = 16


def short_conv(rows, taps, bias):
    two, one = pltpu.roll(rows, 2, 0), pltpu.roll(rows, 1, 0)
    return (taps[0:1] * two + taps[1:2] * one + taps[2:3] * rows + bias)[HALO:]


def pack_pairs(out_ref, index, pair, even, odd):
    half = LANES // 2
    lower = lax.broadcasted_iota(jnp.int32, even.shape, 1) < half
    out_ref[index, pair] = jnp.where(lower, even, pltpu.roll(odd, half, 1)).astype(bf16)
    out_ref[index + 1, pair] = jnp.where(lower, pltpu.roll(even, half, 1), odd).astype(bf16)


def pack_rows(out_ref, index, value):
    for pair in range(value.shape[0] // 256):
        rows = value[256 * pair : 256 * (pair + 1)]
        pack_pairs(out_ref, index, pair, rows[:LANES], rows[LANES:])


def unpack_rows(in_ref, index):
    half = LANES // 2
    out = []
    for pair in range(in_ref.shape[1]):
        one, two = in_ref[index, pair].astype(f32), in_ref[index + 1, pair].astype(f32)
        lower = lax.broadcasted_iota(jnp.int32, one.shape, 1) < half
        out.append(jnp.where(lower, one, pltpu.roll(two, half, 1)))
        out.append(jnp.where(lower, pltpu.roll(one, half, 1), two))
    return jnp.concatenate(out, axis=0)


def project_body(scalars, normed_ref, bias_ref, a_ref, ax_ref, b_ref, by_ref, out_ref, weight_ref):
    chips = 2 * a_ref.shape[1]
    place_pieces(weight_ref, (a_ref, ax_ref, b_ref, by_ref), scalars, chips, 2 * a_ref.shape[2])
    value = jnp.dot(normed_ref[...], weight_ref[...], preferred_element_type=f32) + bias_ref[...]
    row = lax.broadcasted_iota(jnp.int32, value.shape, 0)
    value = jnp.where(jnp.logical_and(row < HALO, scalars[1] == 0), 0.0, value)
    out_ref[...] = value.astype(bf16)


def grid_call(body, scalars, grid, ins, outs, scratch, flops, moved, transcendentals=0):
    return pl.pallas_call(
        body,
        grid_spec=pltpu.PrefetchScalarGridSpec(
            num_scalar_prefetch=1,
            grid=(grid,),
            in_specs=[pl.BlockSpec(block, index) for _, block, index in ins],
            out_specs=[pl.BlockSpec(block, index) for _, _, block, index in outs],
            scratch_shapes=scratch,
        ),
        out_shape=[jax.ShapeDtypeStruct(shape, dtype) for shape, dtype, _, _ in outs],
        compiler_params=pltpu.CompilerParams(vmem_limit_bytes=VMEM_BYTES),
        cost_estimate=pl.CostEstimate(flops=flops, bytes_accessed=moved, transcendentals=transcendentals),
    )(scalars, *[value for value, _, _ in ins])


def fixed(value):
    return (value, value.shape, lambda i, s, n=value.ndim: (0,) * n)


def fixed_out(shape, dtype):
    return (shape, dtype, shape, lambda i, s, n=len(shape): (0,) * n)


def project(scalars, normed, bias, pieces):
    rows, width = normed.shape
    columns = bias.shape[1]
    block = columns // 3
    lead = pieces[0].shape[:3]
    piece_specs = [(p, (*lead, block), lambda i, s: (0, 0, 0, i)) for p in pieces]
    return grid_call(
        project_body,
        scalars,
        3,
        [fixed(normed), (bias, (1, block), lambda i, s: (0, i)), *piece_specs],
        [
            ((rows, columns), bf16, (rows, block), lambda i, s: (0, i)),
            ((width, columns), bf16, (width, block), lambda i, s: (0, i)),
        ],
        [],
        2 * rows * width * columns,
        4 * width * columns + 2 * rows * (width + columns),
    )


def gate_body(scalars, second_ref, values_ref, t2_ref, t3_ref, b2_ref, b3_ref, out_ref):
    second = short_conv(second_ref[...].astype(f32), t2_ref[...], b2_ref[...])
    values = short_conv(values_ref[...].astype(f32), t3_ref[...], b3_ref[...])
    pack_rows(out_ref, 0, values * second)


def stream_tiles(projected, taps, bias, stream, tiles):
    rows = projected.shape[0]
    index = lambda i, s, at=stream * tiles: (0, at + i)
    return (
        (projected, (rows, LANES), index),
        (taps, (3, LANES), index),
        (bias, (1, LANES), index),
    )


def gate(scalars, projected, taps, bias, chips):
    rows, columns = projected.shape
    tiles = columns // 3 // LANES
    p2, t2, b2 = stream_tiles(projected, taps, bias, 1, tiles)
    p3, t3, b3 = stream_tiles(projected, taps, bias, 2, tiles)
    pairs = (rows - HALO) // 256
    (out,) = grid_call(
        gate_body,
        scalars,
        tiles,
        [p2, p3, t2, t3, b2, b3],
        [((chips, pairs, LANES, LANES), bf16, (2, pairs, LANES, LANES), lambda i, s: (i, 0, 0, 0))],
        [],
        20 * rows * columns,
        3 * rows * columns,
    )
    return out


def branch_body(
    scalars, mixed_ref, first_ref, taps_ref, bias_ref, a_ref, ax_ref, b_ref, by_ref, mixed_out, mix_out, weight_ref, out_ref
):
    chips = 2 * a_ref.shape[1]
    place_pieces(weight_ref, (a_ref, ax_ref, b_ref, by_ref), scalars, chips, 2 * a_ref.shape[2])
    for tile in range(chips // 2):
        cols = slice(tile * LANES, (tile + 1) * LANES)
        mixed = unpack_rows(mixed_ref, 2 * tile)
        first = short_conv(first_ref[:, cols].astype(f32), taps_ref[:, cols], bias_ref[:, cols])
        mixed_out[:, cols] = mixed.astype(bf16)
        mix_out[:, cols] = (mixed * first).astype(bf16)
    out_ref[...] = jnp.dot(mix_out[...], weight_ref[...], preferred_element_type=f32)


def first_stream(projected, taps, bias):
    rows, columns = projected.shape
    block = columns // 3
    return [
        (projected, (rows, block), lambda i, s: (0, 0)),
        (taps, (3, block), lambda i, s: (0, 0)),
        (bias, (1, block), lambda i, s: (0, 0)),
    ]


def branch_out(scalars, mixed, projected, taps, bias, pieces):
    rows = projected.shape[0] - HALO
    half = projected.shape[1] // 3
    width = pieces[0].shape[3]
    return grid_call(
        branch_body,
        scalars,
        1,
        [fixed(mixed), *first_stream(projected, taps, bias), *[fixed(p) for p in pieces]],
        [
            fixed_out((rows, half), bf16),
            fixed_out((rows, half), bf16),
            fixed_out((half, width), bf16),
            fixed_out((rows, width), f32),
        ],
        [],
        2 * rows * half * width,
        4 * rows * width + 6 * half * width,
    )


def tiled_feed_body(
    scalars,
    nt_ref,
    ct_ref,
    bias_ref,
    ua_ref,
    uax_ref,
    ub_ref,
    uby_ref,
    da_ref,
    dax_ref,
    db_ref,
    dby_ref,
    y_ref,
    gx_ref,
    gdown_kept,
    gdown_sent,
    gup_kept,
    gup_sent,
    gbias_ref,
    up_ref,
    down_ref,
    grad_ref,
):
    step = pl.program_id(0)
    z_count = ua_ref.shape[1]
    x = scalars[0]

    @pl.when(step == 0)
    def _():
        y_ref[...] = jnp.zeros_like(y_ref)
        gx_ref[...] = jnp.zeros_like(gx_ref)

    place_pieces(up_ref, (ua_ref, uax_ref, ub_ref, uby_ref), scalars, 2 * z_count, 2 * ua_ref.shape[2])
    span = down_ref.shape[0] // 2
    half = span // 2
    own, other = pl.multiple_of(x * span, span), pl.multiple_of((1 - x) * span, span)
    down_ref[pl.ds(own, half), :] = da_ref[0, 0]
    down_ref[pl.ds(other, half), :] = dax_ref[0, 0]

    def put_second(source):
        down_ref[pl.ds(pl.multiple_of(own + half, half), half), :] = source[0, 0]
        down_ref[pl.ds(pl.multiple_of(other + half, half), half), :] = source[1, 0]

    @pl.when(step < z_count)
    def _():
        put_second(db_ref)

    @pl.when(step >= z_count)
    def _():
        put_second(dby_ref)

    nt, ct, up, down = nt_ref[...], ct_ref[...], up_ref[...], down_ref[...]
    before = jnp.dot(nt, up, preferred_element_type=f32) + bias_ref[...]
    cdf = 0.5 * (1.0 + lax.erf(before * math.sqrt(0.5)))
    active = (before * cdf).astype(bf16)
    slope = cdf + before * (jnp.exp(-0.5 * before * before) * (1.0 / math.sqrt(2.0 * math.pi)))
    g_act = lax.dot_general(ct, down, (((1,), (1,)), ((), ())), preferred_element_type=f32)
    g_before = (g_act * slope).astype(bf16)
    y_ref[...] += jnp.dot(active, down, preferred_element_type=f32)
    gx_ref[...] += lax.dot_general(g_before, up, (((1,), (1,)), ((), ())), preferred_element_type=f32)
    gdown = lax.dot_general(active, ct, (((0,), (0,)), ((), ())), preferred_element_type=f32)
    one, two = gdown[:span], gdown[span:]
    gdown_kept[0, 0] = jnp.where(x == 0, one, two).astype(bf16)
    gdown_sent[0, 0] = jnp.where(x == 0, two, one).astype(bf16)
    grad_ref[...] = lax.dot_general(nt, g_before, (((0,), (0,)), ((), ())), preferred_element_type=f32)
    route_rows(grad_ref, gup_kept, gup_sent, scalars, 2 * z_count, 2, False)
    gbias_ref[...] = jnp.sum(g_before.astype(f32), axis=0, keepdims=True)


def tiled_feed(scalars, nt, ct, bias, up, down):
    rows, width = nt.shape
    hidden = bias.shape[1]
    z_count = up[0].shape[1]
    chips = 2 * z_count
    block = hidden // chips
    h = up[0].shape[2]
    hd = down[0].shape[2]
    column = lambda i, s: (0, s[2 + i])
    up_specs = [(p, (2, z_count, h, block), lambda i, s: (0, 0, 0, s[2 + i])) for p in up]
    near = lambda i, s: (i // z_count, i % z_count, 0, 0)
    far = lambda i, s: (0, i % z_count, 0, 0)
    down_specs = [(p, (1, 1, hd, width), near) for p in down[:2]] + [(p, (2, 1, hd, width), far) for p in down[2:]]
    down_block = (1, 1, 2 * hd, width)
    up_shape = (2, z_count, 2, h, hidden)
    up_block = (2, z_count, 2, h, block)
    up_index = lambda i, s: (0, 0, 0, 0, s[2 + i])
    return grid_call(
        tiled_feed_body,
        scalars,
        chips,
        [fixed(nt), fixed(ct), (bias, (1, block), column), *up_specs, *down_specs],
        [
            fixed_out((rows, width), f32),
            fixed_out((rows, width), f32),
            ((2, z_count, 2 * hd, width), bf16, down_block, near),
            ((2, z_count, 2 * hd, width), bf16, down_block, near),
            (up_shape, bf16, up_block, up_index),
            (up_shape, bf16, up_block, up_index),
            ((1, hidden), f32, (1, block), column),
        ],
        [pltpu.VMEM((width, block), bf16), pltpu.VMEM((block, width), bf16), pltpu.VMEM((width, block), f32)],
        12 * rows * width * hidden,
        8 * width * hidden + 12 * rows * width,
        2 * rows * hidden,
    )


def unbranch_body(
    scalars,
    g_ref,
    mix_ref,
    mixed_ref,
    first_ref,
    taps_ref,
    bias_ref,
    weight_ref,
    gmixed_ref,
    gfirst_ref,
    kept_ref,
    sent_ref,
    grad_ref,
):
    chips = gmixed_ref.shape[0]
    g = g_ref[...]
    gate_grad = lax.dot_general(g, weight_ref[...], (((1,), (1,)), ((), ())), preferred_element_type=f32)
    for tile in range(chips // 2):
        cols = slice(tile * LANES, (tile + 1) * LANES)
        first = short_conv(first_ref[:, cols].astype(f32), taps_ref[:, cols], bias_ref[:, cols])
        gfirst_ref[:, cols] = (gate_grad[:, cols] * mixed_ref[:, cols].astype(f32)).astype(bf16)
        pack_rows(gmixed_ref, 2 * tile, gate_grad[:, cols] * first)
    grad_ref[...] = lax.dot_general(mix_ref[...], g, (((0,), (0,)), ((), ())), preferred_element_type=f32)
    route_rows(grad_ref, kept_ref, sent_ref, scalars, chips, 1, False)


def unbranch(scalars, g, mix, mixed, projected, taps, bias, weight, chips):
    rows, width = g.shape
    half = weight.shape[0]
    grad_shape = (2, chips // 2, 1, half // (2 * chips), width)
    return grid_call(
        unbranch_body,
        scalars,
        1,
        [fixed(g), fixed(mix), fixed(mixed), *first_stream(projected, taps, bias), fixed(weight)],
        [
            fixed_out((chips, rows // 256, LANES, LANES), bf16),
            fixed_out((rows, half), bf16),
            fixed_out(grad_shape, bf16),
            fixed_out(grad_shape, bf16),
        ],
        [pltpu.VMEM((half, width), f32)],
        4 * rows * half * width,
        4 * rows * width + 6 * half * width,
    )


def ungate_body(scalars, gated_ref, second_ref, values_ref, t2_ref, t3_ref, b2_ref, b3_ref, gsecond_ref, gvalues_ref):
    grad = unpack_rows(gated_ref, 0)
    second = short_conv(second_ref[...].astype(f32), t2_ref[...], b2_ref[...])
    values = short_conv(values_ref[...].astype(f32), t3_ref[...], b3_ref[...])
    gsecond_ref[...] = (grad * values).astype(bf16)
    gvalues_ref[...] = (grad * second).astype(bf16)


def ungate(scalars, gated, projected, taps, bias):
    rows, columns = projected.shape
    half = columns // 3
    tiles = half // LANES
    p2, t2, b2 = stream_tiles(projected, taps, bias, 1, tiles)
    p3, t3, b3 = stream_tiles(projected, taps, bias, 2, tiles)
    out = ((rows - HALO, half), bf16, (rows - HALO, LANES), lambda i, s: (0, i))
    return grid_call(
        ungate_body,
        scalars,
        tiles,
        [(gated, (2, *gated.shape[1:]), lambda i, s: (i, 0, 0, 0)), p2, p3, t2, t3, b2, b3],
        [out, out],
        [],
        20 * rows * columns,
        3 * rows * columns,
    )


def stream_body(
    by_x, scalars, grad_ref, follow_ref, rows_ref, taps_ref, normed_ref, gproj_ref, kept_ref, sent_ref, sums_ref, work_ref
):
    count, columns = grad_ref.shape
    chips = 2 * kept_ref.shape[1]
    for at in range(0, columns, LANES):
        cols = slice(at, at + LANES)
        taps = taps_ref[:, cols]
        grad = grad_ref[:, cols].astype(f32)
        ext = jnp.concatenate([grad, follow_ref[:, cols].astype(f32)], axis=0)
        total = count + HALO
        one, two = pltpu.roll(ext, total - 1, 0)[:count], pltpu.roll(ext, total - 2, 0)[:count]
        low = (taps[0:1] * two + taps[1:2] * one + taps[2:3] * grad).astype(bf16)
        gproj_ref[:, cols] = low
        rows = rows_ref[:, cols].astype(f32)
        sums = [
            jnp.sum(grad * pltpu.roll(rows, 2, 0)[HALO:], axis=0, keepdims=True),
            jnp.sum(grad * pltpu.roll(rows, 1, 0)[HALO:], axis=0, keepdims=True),
            jnp.sum(grad * rows[HALO:], axis=0, keepdims=True),
            jnp.sum(grad, axis=0, keepdims=True),
            jnp.sum(low.astype(f32), axis=0, keepdims=True),
            jnp.zeros((3, LANES), f32),
        ]
        sums_ref[:, cols] = jnp.concatenate(sums, axis=0)
    work_ref[...] = lax.dot_general(
        normed_ref[...], gproj_ref[...], (((0,), (0,)), ((), ())), preferred_element_type=f32
    )
    route_rows(work_ref, kept_ref, sent_ref, scalars, chips, 2, by_x)


def stream_back(scalars, grad, follow, projected, taps, normed, stream, chips, by_x):
    count, columns = grad.shape
    width = normed.shape[1]
    rows = projected.shape[0]
    index = lambda i, s: (0, stream)
    shape = (2, chips // 2, 2, width // (4 * chips), columns)
    return grid_call(
        partial(stream_body, by_x),
        scalars,
        1,
        [
            fixed(grad),
            fixed(follow),
            (projected, (rows, columns), index),
            (taps, (3, columns), index),
            fixed(normed),
        ],
        [
            fixed_out((count, columns), bf16),
            fixed_out(shape, bf16),
            fixed_out(shape, bf16),
            fixed_out((8, columns), f32),
        ],
        [pltpu.VMEM((width, columns), f32)],
        2 * count * columns * width,
        4 * count * columns + 2 * count * width + 2 * width * columns,
    )


def filter_features(seq_index, tok_count, length):
    positions = (seq_index * tok_count + jnp.arange(tok_count, dtype=jnp.int32)).astype(f32)
    relative = positions / (length - 1)
    phases = positions * (2.0 * math.pi / length)
    band_count = (FEATURES - 1) // 2
    band_freq = jnp.linspace(0.0001, band_count - 1, band_count).astype(f32)
    angles = phases[:, None] * band_freq[None, :]
    return jnp.concatenate([relative[:, None], jnp.cos(angles), -jnp.sin(angles)], axis=1)


def tiled_device(
    tokens,
    cotangent,
    pre_gain,
    pre_offset,
    input_weight,
    input_bias,
    short_weight,
    short_bias,
    skip_weight,
    embed_weight,
    embed_bias,
    hidden_weight,
    hidden_bias,
    last_weight,
    last_bias,
    frequency,
    filter_weight,
    output_weight,
    output_bias,
    post_gain,
    post_offset,
    up_weight,
    up_bias,
    down_weight,
    down_bias,
):
    seq_count = lax.axis_size("seq")
    seq_index = lax.axis_index("seq")
    z, y, core, x = place()
    chips = seq_count // 2
    z_count = seq_count // 4
    tok_count, width = tokens.shape[1:]
    length = tok_count * seq_count
    channels = width // seq_count
    ff = up_weight.shape[1]
    hidden_own = ff // seq_count
    half = width // 2
    pairs = length // 256
    rows = 2 * tok_count
    chip_at = [(z ^ rel) * 2 + (y ^ yr) for yr in range(2) for rel in z_order(z_count)]
    scalars = jnp.stack([x, seq_index // 2, *chip_at]).astype(jnp.int32)

    def half_columns(value, groups, run):
        grid = value.reshape(value.shape[0], groups, chips, 2, run)
        return [grid[:, :, :, side].reshape(value.shape[0], groups * chips * run) for side in range(2)]

    def own_rows(value, groups, run):
        sides = half_columns(value, groups, run)
        keep = jnp.where(core == 0, sides[0], sides[1])
        got = swap_core(jnp.where(core == 0, sides[1], sides[0]))
        return jnp.where(core == x, keep, got)

    in_have = gather_z(own_rows(input_weight, 3, channels))
    mine = jnp.stack([tokens[0], cotangent[0]])
    pair = both(mine, swap_core(mine), core)
    tok = pair[:, 0].reshape(rows, width)
    cot = pair[:, 1].reshape(rows, width)
    shift = [(i, i + 2) for i in range(seq_count - 2)]
    tok_ext = jnp.concatenate([lax.ppermute(tok[rows - HALO :], "seq", shift), tok], axis=0)
    vectors = [
        pre_gain,
        pre_offset,
        input_bias,
        short_weight,
        short_bias,
        output_bias,
        post_gain,
        post_offset,
        up_bias,
        down_bias,
    ]
    small = to_rows(flatten(*vectors).astype(f32))
    small_all = gather_small(small).reshape(seq_count, -1)
    up_piece = own_rows(up_weight, 1, hidden_own)
    in_near = gather_near(in_have)
    up_have = gather_z(after(in_have, up_piece))
    in_pieces = gather_far(in_near)
    out_piece = pick(output_weight.reshape(2, -1, width), x, 0)
    out_have = gather_z(after(in_have, out_piece))
    out_pieces = gather_far(gather_near(after(in_pieces, out_have)))
    down_piece = pick(down_weight.reshape(2, -1, width), x, 0)
    down_have = gather_z(after(up_have, down_piece))
    up_near = gather_near(after(in_pieces, up_have))
    up_pieces = gather_far(up_near)
    down_near = gather_near(after(up_near, down_have))
    down_pieces = gather_far(after(up_pieces, down_near))

    columns, at = [], 0
    for vector in vectors:
        columns.append(small_all[:, at : at + vector.size])
        at += vector.size

    def halved(value, run):
        lead = value.shape[:-1]
        return pick(value.reshape(*lead, -1, 2, run), core, len(lead) + 1).reshape(*lead, -1)

    pre_gain_full, pre_offset_full = columns[0].reshape(-1), columns[1].reshape(-1)
    input_bias_own = halved(columns[2].reshape(3, width), channels).reshape(1, -1)
    short_full = columns[3].reshape(seq_count, 3, -1).transpose(1, 0, 2).reshape(3, 3, width)
    taps = halved(short_full, channels).reshape(3, -1)
    short_bias_own = halved(columns[4].reshape(3, width), channels).reshape(1, -1)
    output_bias_full = columns[5].reshape(-1)
    post_gain_full, post_offset_full = columns[6].reshape(-1), columns[7].reshape(-1)
    up_bias_own = halved(columns[8].reshape(-1), hidden_own)[None]
    down_bias_full = columns[9].reshape(-1)

    trunk = (embed_weight, embed_bias, hidden_weight, hidden_bias, last_weight, last_bias, frequency)
    features = filter_features(seq_index, tok_count, length)
    hidden_rows, trunk_pull = jax.vjp(partial(trunk_hidden, features=features), trunk)
    units = hidden_rows.shape[1]
    own_pairs = tok_count // 256
    packed = hidden_rows.reshape(own_pairs, 2, LANES, units).transpose(0, 2, 1, 3)
    packed = packed.reshape(own_pairs, LANES, 2 * units)
    filter_hidden = lax.all_gather(packed, "seq", axis=0, tiled=True)
    filter_own = filter_weight.astype(f32)
    zero = jnp.zeros_like(filter_own)
    filter_pair = jnp.concatenate(
        [jnp.concatenate([filter_own, zero], axis=1), jnp.concatenate([zero, filter_own], axis=1)], axis=0
    )
    deltas = jnp.linspace(math.log(0.01) / 1.5, math.log(0.01) / 0.3, width).astype(f32)
    delta_own = jnp.abs(lax.dynamic_slice_in_dim(deltas, seq_index * channels, channels))
    delta_pair = jnp.concatenate([delta_own, delta_own])[None]
    skip_own = skip_weight.astype(f32)
    skip_pair = jnp.concatenate([skip_own, skip_own])[None]
    tables = tuple(jnp.asarray(t) for t in conv_tables(pairs))
    kernel_spec = conv_filter(filter_hidden, filter_pair, delta_pair, tables)

    normed_one, unit_one, inverse_one = norm_forward(tok_ext.astype(f32), pre_gain_full, pre_offset_full)
    normed_ext = normed_one.astype(bf16)
    normed_low = normed_ext[HALO:]
    projected, in_half = project(scalars, normed_ext, input_bias_own, in_pieces)
    gated_ch = chip_exchange(gate(scalars, projected, taps, short_bias_own, chips)).reshape(pairs, LANES, LANES)
    mixed_ch, gated_spec = conv_forward(gated_ch, kernel_spec, skip_pair, tables)
    chip_shape = (chips, rows // 256, LANES, LANES)
    mixed_back = chip_exchange(mixed_ch.reshape(chip_shape))
    mixed_tok, mix_low, out_half, branch_part = branch_out(
        scalars, mixed_back, projected, taps, short_bias_own, out_pieces
    )
    hidden = tok.astype(f32) + (branch_part + swap_core(branch_part) + output_bias_full)

    normed_two, unit_two, inverse_two = norm_forward(hidden, post_gain_full, post_offset_full)
    down_part, back_part, gdown_kept, gdown_sent, gup_kept, gup_sent, up_bias_grad = tiled_feed(
        scalars, normed_two.astype(bf16), cot, up_bias_own, up_pieces, down_pieces
    )

    def own_tokens(value):
        return lax.dynamic_slice_in_dim(value, core * tok_count, tok_count, 0)

    def other_tokens(value):
        return lax.dynamic_slice_in_dim(value, (1 - core) * tok_count, tok_count, 0)

    normed_two_grad = back_part + swap_core(back_part)
    cot_f = cot.astype(f32)
    hidden_grad = cot_f + norm_backward(normed_two_grad, unit_two, inverse_two, post_gain_full)
    branch_low = hidden_grad.astype(bf16)
    gmixed, gfirst, gout_kept, gout_sent = unbranch(
        scalars, branch_low, mix_low, mixed_tok, projected, taps, short_bias_own, out_half, chips
    )
    mixed_grad_ch = chip_exchange(gmixed).reshape(pairs, LANES, LANES)
    gated_back, hidden_back, filter_square, skip_line = conv_backward(
        mixed_grad_ch, gated_ch, gated_spec, kernel_spec, skip_pair, filter_hidden, filter_pair, delta_pair, tables
    )
    gated_grad = chip_exchange(gated_back.reshape(chip_shape))

    down_sum = reduce_rows(gdown_kept, gdown_sent, swap_x, swap_y)
    up_sum = reduce_rows(gup_kept, gup_sent, swap_y, swap_x)
    result = own_tokens(hidden) + (
        own_tokens(down_part) + swap_core(other_tokens(down_part)) + down_bias_full
    )
    down_bias_grad = jnp.sum(cot_f, axis=0)
    post_gain_grad = jnp.sum(normed_two_grad * unit_two, axis=0)
    post_offset_grad = jnp.sum(normed_two_grad, axis=0)
    output_bias_grad = jnp.sum(branch_low.astype(f32), axis=0)

    back_shift = [(i + 2, i) for i in range(seq_count - 2)]
    gfirst_next = lax.ppermute(gfirst[:HALO], "seq", back_shift)
    first_proj, first_kept, first_sent, first_sums = stream_back(
        scalars, gfirst, gfirst_next, projected, taps, normed_low, 0, chips, True
    )
    first_sum = reduce_rows(first_kept, first_sent, swap_x, swap_y)
    out_sum = reduce_rows(gout_kept, gout_sent, swap_y, swap_x)[0]
    gsecond, gvalues = ungate(scalars, gated_grad, projected, taps, short_bias_own)
    follow = lax.ppermute(jnp.stack([gsecond[:HALO], gvalues[:HALO]]), "seq", back_shift)
    second_proj, second_kept, second_sent, second_sums = stream_back(
        scalars, gsecond, follow[0], projected, taps, normed_low, 1, chips, True
    )
    values_proj, values_kept, values_sent, values_sums = stream_back(
        scalars, gvalues, follow[1], projected, taps, normed_low, 2, chips, False
    )
    second_sum = reduce_rows(second_kept, second_sent, swap_x, swap_y)
    values_sum = reduce_rows(values_kept, values_sent, swap_y, swap_x)
    normed_one_part = sum(
        contract(part, in_half[:, i * half : (i + 1) * half], 1, 1)
        for i, part in enumerate((first_proj, second_proj, values_proj))
    )
    normed_one_grad = own_tokens(normed_one_part) + swap_core(other_tokens(normed_one_part))
    unit_own = own_tokens(unit_one[HALO:])
    pre_gain_grad = jnp.sum(normed_one_grad * unit_own, axis=0)
    pre_offset_grad = jnp.sum(normed_one_grad, axis=0)
    tokens_grad = own_tokens(hidden_grad) + norm_backward(
        normed_one_grad, unit_own, own_tokens(inverse_one[HALO:]), pre_gain_full
    )

    hidden_got = lax.all_to_all(
        hidden_back.reshape(seq_count, own_pairs * LANES, 2 * units), "seq", split_axis=0, concat_axis=0, tiled=True
    )
    hidden_sum = jnp.sum(hidden_got.astype(f32), axis=0)
    hidden_sum = hidden_sum.reshape(own_pairs, LANES, 2, units).transpose(0, 2, 1, 3).reshape(tok_count, units)
    (trunk_grad,) = trunk_pull(hidden_sum)
    filter_grad = filter_square[:units, :channels] + filter_square[units:, channels:]
    skip_grad = skip_line[:, :channels] + skip_line[:, channels:]
    own_grad = jnp.concatenate([filter_grad, skip_grad], axis=0)
    own_grad = own_grad + swap_x(own_grad)
    own_grad = pick(own_grad.reshape(-1, 2, channels // 2), x, 1)

    def whole_columns(value, groups, run):
        got = swap_core(pick(value, 1 - core, 0))
        mine_part = pick(value, core, 0)
        n = mine_part.shape[0]
        grid = both(mine_part, got, core).reshape(2, n, groups, chips, run)
        return grid.transpose(1, 2, 3, 0, 4).reshape(n, -1)

    in_rows = whole_columns(jnp.concatenate([first_sum, second_sum, values_sum], axis=2), 3, channels)
    up_rows_sum = whole_columns(up_sum, 1, hidden_own)

    all_sums = jnp.stack([first_sums, second_sums, values_sums])
    chip_wide = [post_gain_grad, post_offset_grad, down_bias_grad, output_bias_grad]
    own_wide = [pre_gain_grad, pre_offset_grad, *trunk_grad]
    half_wide = [up_bias_grad.reshape(-1), all_sums[:, :5]]
    chip_flat, own_flat, half_flat = (to_rows(flatten(*group)) for group in (chip_wide, own_wide, half_wide))
    summed = sum_chips(jnp.concatenate([chip_flat, own_flat, half_flat], axis=0))
    n_chip, n_own = chip_flat.shape[0], own_flat.shape[0]
    got = swap_core(summed[n_chip:])
    own_sum = (summed[n_chip:] + got)[:n_own].reshape(-1)
    half_sum = both(summed[n_chip + n_own :], got[n_own:], core).reshape(2, -1)
    chip_sums = unflatten(summed[:n_chip].reshape(-1), [v.shape for v in chip_wide])
    own_sums = unflatten(own_sum, [v.shape for v in own_wide])
    half_sums = [unflatten(half_sum[side], [v.shape for v in half_wide]) for side in range(2)]
    block_index = seq_index * 2 + x

    def own_block(value, axis=0):
        size = value.shape[axis] // (2 * seq_count)
        return lax.dynamic_slice_in_dim(value, block_index * size, size, axis)

    up_bias_sum = jnp.stack([s[0].reshape(chips, hidden_own) for s in half_sums], axis=1).reshape(-1)
    streams = jnp.stack([s[1].reshape(3, 5, chips, channels) for s in half_sums], axis=3)
    streams = streams.transpose(1, 0, 2, 3, 4).reshape(5, 3 * width)
    return (
        result.astype(bf16)[None],
        tokens_grad.astype(bf16)[None],
        own_block(own_sums[0]),
        own_block(own_sums[1]),
        in_rows,
        own_block(streams[4]),
        own_block(streams[:3], 1),
        own_block(streams[3]),
        own_grad[units],
        *own_sums[2:],
        own_grad[:units],
        out_sum,
        own_block(chip_sums[3]),
        own_block(chip_sums[0]),
        own_block(chip_sums[1]),
        up_rows_sum,
        own_block(up_bias_sum),
        down_sum,
        own_block(chip_sums[2]),
    )


def per_device(tokens, *others):
    channels = tokens.shape[2] // lax.axis_size("seq")
    tiled = 2 * channels == LANES and tokens.shape[1] % 256 == 0
    return (tiled_device if tiled else plain_device)(tokens, *others)


def solution(mesh):
    placed = (
        P("dp", "seq", None),
        P("dp", "seq", None),
        P("seq"),
        P("seq"),
        P("seq", None),
        P("seq"),
        P(None, "seq"),
        P("seq"),
        P("seq"),
        P(),
        P(),
        P(),
        P(),
        P(),
        P(),
        P(),
        P(None, "seq"),
        P("seq", None),
        P("seq"),
        P("seq"),
        P("seq"),
        P("seq", None),
        P("seq"),
        P("seq", None),
        P("seq"),
    )
    split = P(("seq", "dp"))
    split_rows = P(("seq", "dp"), None)
    split_columns = P(None, ("seq", "dp"))
    return jax.shard_map(
        per_device,
        mesh=mesh,
        in_specs=placed,
        out_specs=(
            P("dp", "seq", None),
            P("dp", "seq", None),
            split,
            split,
            split_rows,
            split,
            split_columns,
            split,
            split,
            P(),
            P(),
            P(),
            P(),
            P(),
            P(),
            P(),
            split_columns,
            split_rows,
            split,
            split,
            split,
            split_rows,
            split,
            split_rows,
            split,
        ),
        check_vma=False,
    )
```

time: 1940 us -> 617 us (0.32)
  waiting for transfers between devices: 1390 us -> 234 us
  matrix products: 201 us -> 14.6 us
  blocking collectives: 163 us -> 0 us
  Pallas kernels: 0 us -> 82 us
  starting transfers between devices: 57.2 us -> 108 us
  other arithmetic: 20.2 us -> 65 us
    reduce_scatter x5 -> x0, waiting for transfers between devices: 1150 us -> none  [the longest x1 362 us: per_device(): lax.psum_scatter(down_weight_grad, ('seq', 'dp'), scatter_dimension=0, ti...]
    ppermute x2 -> x70, waiting for transfers between devices: 0.78 us -> 234 us  [the longest x51 154 us: swap_seq(): return lax.ppermute(value, 'seq', [(i, i ^ mask) for i in range(count)])]
    unnamed x13 -> x1, waiting for transfers between devices: 224 us -> 0.02 us
    dot_general x49 -> x8, matrix products: 135 us -> 7.43 us  [the longest x3 3.26 us: trunk_hidden(): jnp.dot(layer_out, last_weight, precision=highest) + last_bias]
    all_gather x3 -> x0, blocking collectives: 95.3 us -> none  [the longest x1 37.5 us: per_device(): lax.all_gather(short_weight, 'seq', axis=1, tiled=True)]
    pallas_call x0 -> x12, Pallas kernels: none -> 82 us  [the longest x9 51.4 us: grid_call(): pl.pallas_call(body, grid_spec=pltpu.PrefetchScalarGridSpec(num_scalar_pr...]
    ppermute x2 -> x70, starting transfers between devices: 18.1 us -> 81 us  [the longest x51 56.5 us: swap_seq(): return lax.ppermute(value, 'seq', [(i, i ^ mask) for i in range(count)])]
    dot_general x10 -> x3, matrix products: 65.4 us -> 7.2 us  [contract(): lax.dot_general(left_side, right_side, (((left_dim,), (right_dim,)), ((),...]
  transfers between devices with their start and end apart: 18 -> 76, of which waited for: 10 -> 36; matrix products, arithmetic and copies ran while one was open for 11% -> 21% of each run, Pallas kernels for 0% -> 10%
where the time goes in v1:
time: 617 us; the launch traced here: 606 us
  waiting for transfers between devices  234 us (38%)
  starting transfers between devices  108 us (18%)
  local copies, waits for them, and re-layouts  85.7 us (14%)
  Pallas kernels  82 us (13%)
  other arithmetic  65 us (11%)
  between operations  16.4 us (3%)
  matrix products  14.6 us (2%)
    ppermute x51, waiting for transfers between devices, swap_seq(): return lax.ppermute(value, 'seq', [(i, i ^ mask) for i in range(count)])  154 us
    ppermute x16, waiting for transfers between devices, swap_x(): return lax.ppermute(value, 'dp', [(i, i ^ 1) for i in range(count)])  70.3 us
    ppermute x51, starting transfers between devices, swap_seq(): return lax.ppermute(value, 'seq', [(i, i ^ mask) for i in range(count)])  56.5 us
    pallas_call x9, Pallas kernels, grid_call(): pl.pallas_call(body, grid_spec=pltpu.PrefetchScalarGridSpec(num_scalar_pr...  51.4 us
    pallas_call x3, Pallas kernels, whole_call(): pl.pallas_call(body, out_shape=outs, scratch_shapes=scratch, compiler_par...  30.6 us
    unnamed x225, local copies, waits for them, and re-layouts  27.8 us
    all_to_all x4, starting transfers between devices, chip_exchange(): lax.all_to_all(value, 'seq', split_axis=0, concat_axis=0, tiled=True, axi...  19.2 us
    ppermute x16, starting transfers between devices, swap_x(): return lax.ppermute(value, 'dp', [(i, i ^ 1) for i in range(count)])  14.7 us
  transfers between devices with their start and end apart: 76, of which 36 were waited for; matrix products, arithmetic and copies ran while one was open for 21% of the time, Pallas kernels for 10%

profile of v1, /device:TPU:9, one launch (start us, length us, event | category | flops | bytes accessed | tf_op | source)
XLA Modules:
  0.0 605.7 jit_solution(2588831893892642147)
XLA Ops:
  8.1 6.1 %concatenate.121 = bf16[1600]{0:T(1024)(128)(2,1)S(1)} concatenate(bf16[64]{0:T(256)(128)(2,1)} %param.31, bf16[64]{0:T(256)(128)(2,1)} %param.32, bf16[192]{0:T(256)(128)(2,1)} %param.34, bf16[576]{0:T(1024)(128)(2,1)S(1)} %reshape.480, bf16[192]{0:T(256)(128)(2,1)} %param.36, bf16[64]{0:T(256)(128)(2,1)} %param.47, bf16[64]{0:T(256)(128)(2,1)} %param.48, bf16[64]{0:T(256)(128)(2,1)} %param.49, ...), dimensions={0} | concatenate | bytes 6400 | tf_op jit(solution)/shard_map/concatenate | solution.py:735
  33.7 2.1 collective-permute-start.4
  38.6 2.7 collective-permute-done.5
  43.9 9.9 %collective-permute-done.7 = bf16[1,64,1536]{2,1,0:T(8,128)(2,1)S(1)} collective-permute-done((bf16[1,64,1536]{2,1,0:T(8,128)(2,1)S(1)}, bf16[1,64,1536]{2,1,0:T(8,128)(2,1)S(1)}, u32[]{:S(2)}, u32[]{:S(2)}) %collective-permute-start.7) | collective-permute-done | bytes 196640 | tf_op jit(solution)/shard_map/ppermute | solution.py:21
  54.8 10.0 %collective-permute-done.8 = bf16[2,64,1536]{2,1,0:T(8,128)(2,1)S(1)} collective-permute-done((bf16[2,64,1536]{2,1,0:T(8,128)(2,1)S(1)}, bf16[2,64,1536]{2,1,0:T(8,128)(2,1)S(1)}, u32[]{:S(2)}, u32[]{:S(2)}) %collective-permute-start.8) | collective-permute-done | bytes 393248 | tf_op jit(solution)/shard_map/ppermute | solution.py:21
  69.4 3.4 collective-permute-start.1
  80.9 2.3 fusion
  83.1 8.7 %collective-permute-done.10.ax_ref = bf16[2,4,32,1536]{3,2,1,0:T(8,128)(2,1)S(1)} collective-permute-done((bf16[2,4,32,1536]{3,2,1,0:T(8,128)(2,1)S(1)}, bf16[2,4,32,1536]{3,2,1,0:T(8,128)(2,1)S(1)}, u32[]{:S(2)}, u32[]{:S(2)}) %collective-permute-start.10) | collective-permute-done | bytes 786464 | tf_op jit(solution)/shard_map/ppermute | solution.py:38
  91.8 2.5 collective-permute-done.12.by_ref
  94.3 5.3 shard_map.468
  101.0 2.9 shard_map.469
  103.9 4.5 all-to-all-start
  111.8 22.1 %collective-permute-done.13 = bf16[1,32,1024]{2,1,0:T(8,128)(2,1)S(1)} collective-permute-done((bf16[1,32,1024]{2,1,0:T(8,128)(2,1)S(1)}, bf16[1,32,1024]{2,1,0:T(8,128)(2,1)S(1)}, u32[]{:S(2)}, u32[]{:S(2)}) %collective-permute-start.13) | collective-permute-done | bytes 65568 | tf_op jit(solution)/shard_map/ppermute | solution.py:21
  139.1 5.4 shard_map.470.kernel_ref
  145.8 9.1 %shard_map.471 = (bf16[16,128,128]{2,1,0:T(8,128)(2,1)}, f32[256,2176]{1,0:T(8,128)S(1)}) custom-call(bf16[16,128,128]{2,1,0:T(8,128)(2,1)S(1)} %bitcast.304, f32[256,2176]{1,0:T(8,128)} %copy-done.4, f32[1,128]{1,0:T(1,128)S(1)} %fusion.56.skip_ref, f32[17,2,128]{2,1,0:T(2,128)S(1)} %copy-done.25, f32[17,2,128,128]{3,2,1,0:T(8,128)} %constant.175.clone.turn_ref, ...), custom_call_target="tpu_custom_call" | custom-call | flops 2000000000 | bytes 10000000 | tf_op jit(solution)/shard_map/pallas_call | solution.py:450
  156.3 4.6 all-to-all-start.1
  162.5 2.1 pad_maximum_fusion.1
  166.0 2.4 collective-permute-start.16
  168.6 15.0 %collective-permute-done.27 = bf16[1,128,1024]{2,1,0:T(8,128)(2,1)S(1)} collective-permute-done((bf16[1,128,1024]{2,1,0:T(8,128)(2,1)}, bf16[1,128,1024]{2,1,0:T(8,128)(2,1)S(1)}, u32[]{:S(2)}, u32[]{:S(2)}) %collective-permute-start.27) | collective-permute-done | bytes 262176 | tf_op jit(solution)/shard_map/ppermute | solution.py:21
  185.5 4.2 shard_map.472
  189.7 2.9 collective-permute-start.19
  197.5 8.9 %collective-permute-done.23 = bf16[4,32,2048]{2,1,0:T(8,128)(2,1)S(1)} collective-permute-done((bf16[4,32,2048]{2,1,0:T(8,128)(2,1)S(1)}, bf16[4,32,2048]{2,1,0:T(8,128)(2,1)S(1)}, u32[]{:S(2)}, u32[]{:S(2)}) %collective-permute-start.23) | collective-permute-done | bytes 524320 | tf_op jit(solution)/shard_map/ppermute | solution.py:21
  214.1 27.7 %collective-permute-done.30 = bf16[4,64,1024]{2,1,0:T(8,128)(2,1)} collective-permute-done((bf16[4,64,1024]{2,1,0:T(8,128)(2,1)}, bf16[4,64,1024]{2,1,0:T(8,128)(2,1)}, u32[]{:S(2)}, u32[]{:S(2)}) %collective-permute-start.30) | collective-permute-done | bytes 524320 | tf_op jit(solution)/shard_map/ppermute | solution.py:38
  246.7 2.1 fusion.61
  250.2 17.5 %collective-permute-done.31.dax_ref = bf16[2,4,64,1024]{3,2,1,0:T(8,128)(2,1)S(1)} collective-permute-done((bf16[2,4,64,1024]{3,2,1,0:T(8,128)(2,1)S(1)}, bf16[2,4,64,1024]{3,2,1,0:T(8,128)(2,1)S(1)}, u32[]{:S(2)}, u32[]{:S(2)}) %collective-permute-start.31) | collective-permute-done | bytes 1048608 | tf_op jit(solution)/shard_map/ppermute | solution.py:38
  269.1 22.4 %shard_map.473 = (f32[512,1024]{1,0:T(8,128)}, f32[512,1024]{1,0:T(8,128)}, bf16[2,4,128,1024]{3,2,1,0:T(8,128)(2,1)}, bf16[2,4,128,1024]{3,2,1,0:T(8,128)(2,1)}...) custom-call(s32[10]{0:T(128)S(1)} %stack.264.scalars, ...), custom_call_target="tpu_custom_call" | custom-call | flops 12884901888 | bytes 23068672 | tf_op jit(solution)/shard_map/pallas_call | solution.py:1169
  292.9 2.3 constant_dynamic-slice_fusion.4
  295.2 3.1 collective-permute-start.33
  305.2 2.4 fusion.16
  307.6 28.4 %collective-permute-done.61 = bf16[2,4,2,32,2048]{4,3,2,1,0:T(8,128)(2,1)} collective-permute-done((bf16[2,4,2,32,2048]{4,3,2,1,0:T(8,128)(2,1)}, bf16[2,4,2,32,2048]{4,3,2,1,0:T(8,128)(2,1)}, u32[]{:S(2)}, u32[]{:S(2)}) %collective-permute-start.61) | collective-permute-done | bytes 2097184 | tf_op jit(solution)/shard_map/ppermute | solution.py:21
  336.0 2.3 convert_add_fusion.1
  340.4 5.6 collective-permute-done.66
  346.0 2.5 convert_add_fusion
  353.0 2.5 convert_reduce_fusion.1
  355.6 3.8 shard_map.474
  360.9 5.2 all-to-all-start.2
  366.1 3.1 collective-permute-start.35
  371.9 8.9 %collective-permute-done.35.follow_ref = bf16[16,512]{1,0:T(8,128)(2,1)S(1)} collective-permute-done((bf16[16,512]{1,0:T(8,128)(2,1)S(1)}, bf16[16,512]{1,0:T(8,128)(2,1)S(1)}, u32[]{:S(2)}, u32[]{:S(2)}) %collective-permute-start.35) | collective-permute-done | bytes 16416 | tf_op jit(solution)/shard_map/ppermute | solution.py:1721
  380.7 3.3 shard_map.475
  385.0 3.3 fusion.13
  388.3 3.6 collective-permute-done.57
  394.4 6.2 %collective-permute-done.58 = bf16[4,1,32,1024]{3,2,0,1:T(8,128)(2,1)S(1)} collective-permute-done((bf16[4,1,32,1024]{3,2,0,1:T(8,128)(2,1)S(1)}, bf16[4,1,32,1024]{3,2,0,1:T(8,128)(2,1)S(1)}, u32[]{:S(2)}, u32[]{:S(2)}) %collective-permute-start.58) | collective-permute-done | bytes 262176 | tf_op jit(solution)/shard_map/ppermute | solution.py:38
  405.0 16.1 %shard_map.476 = (bf16[16,128,128]{2,1,0:T(8,128)(2,1)}, bf16[16,128,128]{2,1,0:T(8,128)(2,1)S(1)}, f32[128,128]{1,0:T(8,128)S(1)}, f32[1,128]{1,0:T(1,128)S(1)}) custom-call(bf16[16,128,128]{2,1,0:T(8,128)(2,1)S(1)} %bitcast.306, bf16[16,128,128]{2,1,0:T(8,128)(2,1)S(1)} %bitcast.305, f32[256,2176]{1,0:T(8,128)} %copy-done.39, f32[256,2176]{1,0:T(8,128)} %copy-done.4, ...), custom_call_target="tpu_custom_call" | custom-call | flops 4000000000 | bytes 16000000 | tf_op jit(solution)/shard_map/pallas_call | solution.py:450
  422.7 5.0 all-to-all-start.3
  434.5 8.1 %collective-permute-done.60 = bf16[1,1,32,1024]{3,2,0,1:T(8,128)(2,1)S(1)} collective-permute-done((bf16[1,1,32,1024]{3,2,0,1:T(8,128)(2,1)S(1)}, bf16[1,1,32,1024]{3,2,0,1:T(8,128)(2,1)S(1)}, u32[]{:S(2)}, u32[]{:S(2)}) %collective-permute-start.60) | collective-permute-done | bytes 65568 | tf_op jit(solution)/shard_map/ppermute | solution.py:21
  443.3 2.3 fusion.4
  449.7 5.2 collective-permute-done.63
  455.1 11.0 %collective-permute-done.68 = bf16[2,128,1024]{2,1,0:T(8,128)(2,1)S(1)} collective-permute-done((bf16[2,128,1024]{2,1,0:T(8,128)(2,1)S(1)}, bf16[2,128,1024]{2,1,0:T(8,128)(2,1)S(1)}, u32[]{:S(2)}, u32[]{:S(2)}) %collective-permute-start.68) | collective-permute-done | bytes 524320 | tf_op jit(solution)/shard_map/ppermute | solution.py:21
  467.8 12.6 %collective-permute-start.65 = (f32[32,2048]{1,0:T(8,128)}, f32[32,2048]{1,0:T(8,128)}, u32[]{:S(2)}, u32[]{:S(2)}) collective-permute-start(f32[32,2048]{1,0:T(8,128)} %get-tuple-element.161), channel_id=1, source_target_pairs={{0,2},{2,0},{4,6},{6,4},{8,10},{10,8},{12,14},{14,12},{16,18},{18,... | collective-permute-start | bytes 786440 | tf_op jit(solution)/shard_map/ppermute | solution.py:21
  480.4 7.3 %all-to-all-start.4 = ((bf16[16,128,128]{2,1,0:T(8,128)(2,1)}), bf16[16,128,128]{2,1,0:T(8,128)(2,1)}, u32[]{:S(2)}, u32[]{:S(2)}) async-start(bf16[16,128,128]{2,1,0:T(8,128)(2,1)} %copy-done.12), calls=%async_computation.4 | async-start | bytes 1048576 | tf_op jit(solution)/shard_map/all_to_all | solution.py:1749
  491.4 3.4 collective-permute-start.36
  497.7 4.1 shard_map.479
  502.6 5.1 collective-permute-start.51
  507.8 3.3 shard_map.478
  537.8 3.4 collective-permute-done.52
  541.3 2.3 collective-permute-done.48
  545.7 2.7 collective-permute-done.49
  549.1 4.1 collective-permute-done.50
  554.5 2.6 collective-permute-start.55
  557.1 2.6 multiply_reduce_fusion.4
  564.7 6.5 %collective-permute-done.38 = f32[216,128]{1,0:T(8,128)S(1)} collective-permute-done((f32[216,128]{1,0:T(8,128)}, f32[216,128]{1,0:T(8,128)S(1)}, u32[]{:S(2)}, u32[]{:S(2)}) %collective-permute-start.38) | collective-permute-done | bytes 110624 | tf_op jit(solution)/shard_map/ppermute | solution.py:21
  572.9 2.9 collective-permute-done.39
  576.5 2.3 fusion.17
  585.9 3.5 collective-permute-start.42
  (581 shorter events, 179.5 us)
Async XLA Ops:
  7.2 130.6 %all-gather.2.cloned.1.call-start = ((), (), s32[]{:S(2)}) async-start(), calls=%async_computation.5 | async-start | bytes 1114112 | tf_op jit(solution)/shard_map/all_gather | solution.py:1659
  14.2 16.4 %collective-permute-start.2 = (f32[1,16,128]{2,1,0:T(8,128)S(1)}, f32[1,16,128]{2,1,0:T(8,128)S(1)}, u32[]{:S(2)}, u32[]{:S(2)}) collective-permute-start(f32[1,16,128]{2,1,0:T(8,128)S(1)} %get-tuple-element.217), channel_id=1, source_target_pairs={{0,2},{2,0},{4,6},{6,4},{8,10},{10,8},{12,14},{14,12},{16,18},{18,... | collective-permute-start | bytes 24584 | tf_op jit(solution)/shard_map/ppermute | solution.py:21
  24.5 83.9 %collective-permute-start.20 = (bf16[64,2048]{1,0:T(8,128)(2,1)}, bf16[64,2048]{1,0:T(8,128)(2,1)}, u32[]{:S(2)}, u32[]{:S(2)}) collective-permute-start(bf16[64,2048]{1,0:T(8,128)(2,1)} %bitcast.158), channel_id=1, source_target_pairs={{0,2},{2,0},{4,6},{6,4},{8,10},{10,8},{12,14},{14,12},{16,18},{18,... | collective-permute-start | bytes 786440 | tf_op jit(solution)/shard_map/ppermute | solution.py:21
  26.6 15.1 %collective-permute-start.6 = (bf16[64,1536]{1,0:T(8,128)(2,1)S(1)}, bf16[64,1536]{1,0:T(8,128)(2,1)}, u32[]{:S(2)}, u32[]{:S(2)}) collective-permute-start(bf16[64,1536]{1,0:T(8,128)(2,1)S(1)} %select_n.289), channel_id=1, source_target_pairs={{0,2},{2,0},{4,6},{6,4},{8,10},{10,8},{12,14},{14,12},{16,18},{18,... | collective-permute-start | bytes 589832 | tf_op jit(solution)/shard_map/ppermute | solution.py:21
  28.3 37.6 %collective-permute-start = (bf16[2,256,1024]{2,1,0:T(8,128)(2,1)S(1)}, bf16[2,256,1024]{2,1,0:T(8,128)(2,1)}, u32[]{:S(2)}, u32[]{:S(2)}) collective-permute-start(bf16[2,256,1024]{2,1,0:T(8,128)(2,1)S(1)} %constant_dynamic-update-slice_fusion), channel_id=1, source_target_pairs={{0,2},{2,0},{4,6},{6,4},{8,10},{10,8},{12,14},{14,12},{16,18},{18,... | collective-permute-start | bytes 3145736 | tf_op jit(solution)/shard_map/ppermute | solution.py:21
  42.6 11.2 %collective-permute-start.7 = (bf16[1,64,1536]{2,1,0:T(8,128)(2,1)S(1)}, bf16[1,64,1536]{2,1,0:T(8,128)(2,1)S(1)}, u32[]{:S(2)}, u32[]{:S(2)}) collective-permute-start(bf16[1,64,1536]{2,1,0:T(8,128)(2,1)S(1)} %select_bitcast_fusion), channel_id=1, source_target_pairs={{0,24},{2,26},{4,28},{6,30},{8,16},{10,18},{12,20},{14,22},{16,8},... | collective-permute-start | bytes 589832 | tf_op jit(solution)/shard_map/ppermute | solution.py:21
  53.9 11.0 %collective-permute-start.8 = (bf16[2,64,1536]{2,1,0:T(8,128)(2,1)S(1)}, bf16[2,64,1536]{2,1,0:T(8,128)(2,1)S(1)}, u32[]{:S(2)}, u32[]{:S(2)}) collective-permute-start(bf16[2,64,1536]{2,1,0:T(8,128)(2,1)S(1)} %pad_maximum_fusion.12), channel_id=1, source_target_pairs={{0,8},{2,10},{4,12},{6,14},{8,0},{10,2},{12,4},{14,6},{16,24},{18,... | collective-permute-start | bytes 1179656 | tf_op jit(solution)/shard_map/ppermute | solution.py:21
  65.9 12.1 %collective-permute-start.11 = (bf16[4,32,1536]{2,1,0:T(8,128)(2,1)}, bf16[4,32,1536]{2,1,0:T(8,128)(2,1)}, u32[]{:S(2)}, u32[]{:S(2)}) collective-permute-start(bf16[4,32,1536]{2,1,0:T(8,128)(2,1)} %get-tuple-element.156), channel_id=1, source_target_pairs={{0,1},{1,0},{2,3},{3,2},{4,5},{5,4},{6,7},{7,6},{8,9},{9,8},{10,11... | collective-permute-start | bytes 1179656 | tf_op jit(solution)/shard_map/ppermute | solution.py:38
  65.9 9.4 %collective-permute-start.9 = (bf16[4,32,1536]{2,1,0:T(8,128)(2,1)}, bf16[4,32,1536]{2,1,0:T(8,128)(2,1)}, u32[]{:S(2)}, u32[]{:S(2)}) collective-permute-start(bf16[4,32,1536]{2,1,0:T(8,128)(2,1)} %get-tuple-element.157), channel_id=1, source_target_pairs={{0,4},{2,6},{4,0},{6,2},{8,12},{10,14},{12,8},{14,10},{16,20},{18,... | collective-permute-start | bytes 1179656 | tf_op jit(solution)/shard_map/ppermute | solution.py:21
  69.4 5.7 collective-permute-start.1
  76.5 15.4 %collective-permute-start.10 = (bf16[2,4,32,1536]{3,2,1,0:T(8,128)(2,1)S(1)}, bf16[2,4,32,1536]{3,2,1,0:T(8,128)(2,1)S(1)}, u32[]{:S(2)}, u32[]{:S(2)}) collective-permute-start(bf16[2,4,32,1536]{3,2,1,0:T(8,128)(2,1)S(1)} %pad_maximum_fusion.8.a_ref), channel_id=1, source_target_pairs={{0,1},{1,0},{2,3},{3,2},{4,5},{5,4},{6,7},{7,6},{8,9},{9,8},{10,11... | collective-permute-start | bytes 2359304 | tf_op jit(solution)/shard_map/ppermute | solution.py:38
  79.1 15.3 %collective-permute-start.12 = (bf16[2,4,32,1536]{3,2,1,0:T(8,128)(2,1)S(1)}, bf16[2,4,32,1536]{3,2,1,0:T(8,128)(2,1)S(1)}, u32[]{:S(2)}, u32[]{:S(2)}) collective-permute-start(bf16[2,4,32,1536]{3,2,1,0:T(8,128)(2,1)S(1)} %pad_maximum_fusion.9.b_ref), channel_id=1, source_target_pairs={{0,4},{2,6},{4,0},{6,2},{8,12},{10,14},{12,8},{14,10},{16,20},{18,... | collective-permute-start | bytes 2359304 | tf_op jit(solution)/shard_map/ppermute | solution.py:21
  103.9 41.9 %all-to-all-start = ((bf16[8,2,128,128]{3,2,1,0:T(8,128)(2,1)}), bf16[8,2,128,128]{3,2,1,0:T(8,128)(2,1)S(1)}, u32[]{:S(2)}, u32[]{:S(2)}) async-start(bf16[8,2,128,128]{3,2,1,0:T(8,128)(2,1)} %shard_map.469), calls=%async_computation | async-start | bytes 1048576 | tf_op jit(solution)/shard_map/all_to_all | solution.py:64
  109.4 24.5 %collective-permute-start.21 = (bf16[1,64,2048]{2,1,0:T(8,128)(2,1)S(1)}, bf16[1,64,2048]{2,1,0:T(8,128)(2,1)S(1)}, u32[]{:S(2)}, u32[]{:S(2)}) collective-permute-start(bf16[1,64,2048]{2,1,0:T(8,128)(2,1)S(1)} %bitcast.317), channel_id=1, source_target_pairs={{0,24},{2,26},{4,28},{6,30},{8,16},{10,18},{12,20},{14,22},{16,8},... | collective-permute-start | bytes 786440 | tf_op jit(solution)/shard_map/ppermute | solution.py:21
  111.4 22.4 %collective-permute-start.13 = (bf16[1,32,1024]{2,1,0:T(8,128)(2,1)S(1)}, bf16[1,32,1024]{2,1,0:T(8,128)(2,1)S(1)}, u32[]{:S(2)}, u32[]{:S(2)}) collective-permute-start(bf16[1,32,1024]{2,1,0:T(8,128)(2,1)S(1)} %bitcast.338), channel_id=1, source_target_pairs={{0,24},{2,26},{4,28},{6,30},{8,16},{10,18},{12,20},{14,22},{16,8},... | collective-permute-start | bytes 196616 | tf_op jit(solution)/shard_map/ppermute | solution.py:21
  134.8 27.6 %collective-permute-start.22 = (bf16[2,64,2048]{2,1,0:T(8,128)(2,1)}, bf16[2,64,2048]{2,1,0:T(8,128)(2,1)}, u32[]{:S(2)}, u32[]{:S(2)}) collective-permute-start(bf16[2,64,2048]{2,1,0:T(8,128)(2,1)} %pad_maximum_fusion.10), channel_id=1, source_target_pairs={{0,8},{2,10},{4,12},{6,14},{8,0},{10,2},{12,4},{14,6},{16,24},{18,... | collective-permute-start | bytes 1572872 | tf_op jit(solution)/shard_map/ppermute | solution.py:21
  156.3 29.2 %all-to-all-start.1 = ((bf16[8,2,128,128]{3,2,1,0:T(8,128)(2,1)}), bf16[8,2,128,128]{3,2,1,0:T(8,128)(2,1)S(1)}, u32[]{:S(2)}, u32[]{:S(2)}) async-start(bf16[8,2,128,128]{3,2,1,0:T(8,128)(2,1)} %bitcast.38), calls=%async_computation.1 | async-start | bytes 1048576 | tf_op jit(solution)/shard_map/all_to_all | solution.py:64
  160.9 7.6 %collective-permute-start.17 = (bf16[4,16,1024]{2,1,0:T(8,128)(2,1)S(1)}, bf16[4,16,1024]{2,1,0:T(8,128)(2,1)S(1)}, u32[]{:S(2)}, u32[]{:S(2)}) collective-permute-start(bf16[4,16,1024]{2,1,0:T(8,128)(2,1)S(1)} %get-tuple-element.168), channel_id=1, source_target_pairs={{0,1},{1,0},{2,3},{3,2},{4,5},{5,4},{6,7},{7,6},{8,9},{9,8},{10,11... | collective-permute-start | bytes 393224 | tf_op jit(solution)/shard_map/ppermute | solution.py:38
  164.6 18.9 %collective-permute-start.27 = (bf16[1,128,1024]{2,1,0:T(8,128)(2,1)}, bf16[1,128,1024]{2,1,0:T(8,128)(2,1)S(1)}, u32[]{:S(2)}, u32[]{:S(2)}) collective-permute-start(bf16[1,128,1024]{2,1,0:T(8,128)(2,1)} %bitcast.55), channel_id=1, source_target_pairs={{0,24},{2,26},{4,28},{6,30},{8,16},{10,18},{12,20},{14,22},{16,8},... | collective-permute-start | bytes 786440 | tf_op jit(solution)/shard_map/ppermute | solution.py:21
  166.0 19.4 %collective-permute-start.16 = (bf16[2,4,16,1024]{3,2,1,0:T(8,128)(2,1)S(1)}, bf16[2,4,16,1024]{3,2,1,0:T(8,128)(2,1)S(1)}, u32[]{:S(2)}, u32[]{:S(2)}) collective-permute-start(bf16[2,4,16,1024]{3,2,1,0:T(8,128)(2,1)S(1)} %pad_maximum_fusion.15.a_ref), channel_id=1, source_target_pairs={{0,1},{1,0},{2,3},{3,2},{4,5},{5,4},{6,7},{7,6},{8,9},{9,8},{10,11... | collective-permute-start | bytes 786440 | tf_op jit(solution)/shard_map/ppermute | solution.py:38
  168.5 17.0 %collective-permute-start.18 = (bf16[2,4,16,1024]{3,2,1,0:T(8,128)(2,1)S(1)}, bf16[2,4,16,1024]{3,2,1,0:T(8,128)(2,1)S(1)}, u32[]{:S(2)}, u32[]{:S(2)}) collective-permute-start(bf16[2,4,16,1024]{3,2,1,0:T(8,128)(2,1)S(1)} %pad_maximum_fusion.16.b_ref), channel_id=1, source_target_pairs={{0,4},{2,6},{4,0},{6,2},{8,12},{10,14},{12,8},{14,10},{16,20},{18,... | collective-permute-start | bytes 786440 | tf_op jit(solution)/shard_map/ppermute | solution.py:21
  185.4 10.9 %collective-permute-start.28 = (bf16[2,128,1024]{2,1,0:T(8,128)(2,1)}, bf16[2,128,1024]{2,1,0:T(8,128)(2,1)}, u32[]{:S(2)}, u32[]{:S(2)}) collective-permute-start(bf16[2,128,1024]{2,1,0:T(8,128)(2,1)} %pad_maximum_fusion.11), channel_id=1, source_target_pairs={{0,8},{2,10},{4,12},{6,14},{8,0},{10,2},{12,4},{14,6},{16,24},{18,... | collective-permute-start | bytes 1572872 | tf_op jit(solution)/shard_map/ppermute | solution.py:21
  189.7 57.0 %collective-permute-start.19 = (f32[512,1024]{1,0:T(8,128)}, f32[512,1024]{1,0:T(8,128)}, u32[]{:S(2)}, u32[]{:S(2)}) collective-permute-start(f32[512,1024]{1,0:T(8,128)} %get-tuple-element.74), channel_id=1, source_target_pairs={{0,2},{2,0},{4,6},{6,4},{8,10},{10,8},{12,14},{14,12},{16,18},{18,... | collective-permute-start | bytes 6291464 | tf_op jit(solution)/shard_map/ppermute | solution.py:21
  192.9 13.6 %collective-permute-start.23 = (bf16[4,32,2048]{2,1,0:T(8,128)(2,1)S(1)}, bf16[4,32,2048]{2,1,0:T(8,128)(2,1)S(1)}, u32[]{:S(2)}, u32[]{:S(2)}) collective-permute-start(bf16[4,32,2048]{2,1,0:T(8,128)(2,1)S(1)} %get-tuple-element.151), channel_id=1, source_target_pairs={{0,4},{2,6},{4,0},{6,2},{8,12},{10,14},{12,8},{14,10},{16,20},{18,... | collective-permute-start | bytes 1572872 | tf_op jit(solution)/shard_map/ppermute | solution.py:21
  194.1 13.2 %collective-permute-start.25 = (bf16[4,32,2048]{2,1,0:T(8,128)(2,1)S(1)}, bf16[4,32,2048]{2,1,0:T(8,128)(2,1)S(1)}, u32[]{:S(2)}, u32[]{:S(2)}) collective-permute-start(bf16[4,32,2048]{2,1,0:T(8,128)(2,1)S(1)} %get-tuple-element.150), channel_id=1, source_target_pairs={{0,1},{1,0},{2,3},{3,2},{4,5},{5,4},{6,7},{7,6},{8,9},{9,8},{10,11... | collective-permute-start | bytes 1572872 | tf_op jit(solution)/shard_map/ppermute | solution.py:38
  206.6 38.3 %collective-permute-start.24 = (bf16[2,4,32,2048]{3,2,1,0:T(8,128)(2,1)S(1)}, bf16[2,4,32,2048]{3,2,1,0:T(8,128)(2,1)}, u32[]{:S(2)}, u32[]{:S(2)}) collective-permute-start(bf16[2,4,32,2048]{3,2,1,0:T(8,128)(2,1)S(1)} %pad_maximum_fusion.2.ua_ref), channel_id=1, source_target_pairs={{0,1},{1,0},{2,3},{3,2},{4,5},{5,4},{6,7},{7,6},{8,9},{9,8},{10,11... | collective-permute-start | bytes 3145736 | tf_op jit(solution)/shard_map/ppermute | solution.py:38
  208.4 36.5 %collective-permute-start.26 = (bf16[2,4,32,2048]{3,2,1,0:T(8,128)(2,1)}, bf16[2,4,32,2048]{3,2,1,0:T(8,128)(2,1)}, u32[]{:S(2)}, u32[]{:S(2)}) collective-permute-start(bf16[2,4,32,2048]{3,2,1,0:T(8,128)(2,1)} %pad_maximum_fusion.3.ub_ref), channel_id=1, source_target_pairs={{0,4},{2,6},{4,0},{6,2},{8,12},{10,14},{12,8},{14,10},{16,20},{18,... | collective-permute-start | bytes 3145736 | tf_op jit(solution)/shard_map/ppermute | solution.py:21
  210.5 31.4 %collective-permute-start.30 = (bf16[4,64,1024]{2,1,0:T(8,128)(2,1)}, bf16[4,64,1024]{2,1,0:T(8,128)(2,1)}, u32[]{:S(2)}, u32[]{:S(2)}) collective-permute-start(bf16[4,64,1024]{2,1,0:T(8,128)(2,1)} %get-tuple-element.146), channel_id=1, source_target_pairs={{0,1},{1,0},{2,3},{3,2},{4,5},{5,4},{6,7},{7,6},{8,9},{9,8},{10,11... | collective-permute-start | bytes 1572872 | tf_op jit(solution)/shard_map/ppermute | solution.py:38
  211.6 31.8 %collective-permute-start.29 = (bf16[4,64,1024]{2,1,0:T(8,128)(2,1)}, bf16[4,64,1024]{2,1,0:T(8,128)(2,1)}, u32[]{:S(2)}, u32[]{:S(2)}) collective-permute-start(bf16[4,64,1024]{2,1,0:T(8,128)(2,1)} %get-tuple-element.147), channel_id=1, source_target_pairs={{0,4},{2,6},{4,0},{6,2},{8,12},{10,14},{12,8},{14,10},{16,20},{18,... | collective-permute-start | bytes 1572872 | tf_op jit(solution)/shard_map/ppermute | solution.py:21
  244.9 22.9 %collective-permute-start.31 = (bf16[2,4,64,1024]{3,2,1,0:T(8,128)(2,1)S(1)}, bf16[2,4,64,1024]{3,2,1,0:T(8,128)(2,1)S(1)}, u32[]{:S(2)}, u32[]{:S(2)}) collective-permute-start(bf16[2,4,64,1024]{3,2,1,0:T(8,128)(2,1)S(1)} %pad_maximum_fusion.5.da_ref), channel_id=1, source_target_pairs={{0,1},{1,0},{2,3},{3,2},{4,5},{5,4},{6,7},{7,6},{8,9},{9,8},{10,11... | collective-permute-start | bytes 3145736 | tf_op jit(solution)/shard_map/ppermute | solution.py:38
  245.5 22.4 %collective-permute-start.32 = (bf16[2,4,64,1024]{3,2,1,0:T(8,128)(2,1)S(1)}, bf16[2,4,64,1024]{3,2,1,0:T(8,128)(2,1)S(1)}, u32[]{:S(2)}, u32[]{:S(2)}) collective-permute-start(bf16[2,4,64,1024]{3,2,1,0:T(8,128)(2,1)S(1)} %pad_maximum_fusion.6.db_ref), channel_id=1, source_target_pairs={{0,4},{2,6},{4,0},{6,2},{8,12},{10,14},{12,8},{14,10},{16,20},{18,... | collective-permute-start | bytes 3145736 | tf_op jit(solution)/shard_map/ppermute | solution.py:21
  291.5 44.5 %collective-permute-start.61 = (bf16[2,4,2,32,2048]{4,3,2,1,0:T(8,128)(2,1)}, bf16[2,4,2,32,2048]{4,3,2,1,0:T(8,128)(2,1)}, u32[]{:S(2)}, u32[]{:S(2)}) collective-permute-start(bf16[2,4,2,32,2048]{4,3,2,1,0:T(8,128)(2,1)} %get-tuple-element.112), channel_id=1, source_target_pairs={{0,4},{2,6},{4,0},{6,2},{8,12},{10,14},{12,8},{14,10},{16,20},{18,... | collective-permute-start | bytes 6291464 | tf_op jit(solution)/shard_map/ppermute | solution.py:21
  295.2 9.5 %collective-permute-start.33 = (f32[256,1024]{1,0:T(8,128)}, f32[256,1024]{1,0:T(8,128)}, u32[]{:S(2)}, u32[]{:S(2)}) collective-permute-start(f32[256,1024]{1,0:T(8,128)} %constant_dynamic-slice_fusion.4), channel_id=1, source_target_pairs={{0,2},{2,0},{4,6},{6,4},{8,10},{10,8},{12,14},{14,12},{16,18},{18,... | collective-permute-start | bytes 3145736 | tf_op jit(solution)/shard_map/ppermute | solution.py:21
  298.4 47.6 %collective-permute-start.66 = (bf16[2,4,128,1024]{3,2,1,0:T(8,128)(2,1)}, bf16[2,4,128,1024]{3,2,1,0:T(8,128)(2,1)}, u32[]{:S(2)}, u32[]{:S(2)}) collective-permute-start(bf16[2,4,128,1024]{3,2,1,0:T(8,128)(2,1)} %get-tuple-element.114), channel_id=1, source_target_pairs={{0,1},{1,0},{2,3},{3,2},{4,5},{5,4},{6,7},{7,6},{8,9},{9,8},{10,11... | collective-permute-start | bytes 6291464 | tf_op jit(solution)/shard_map/ppermute | solution.py:38
  304.5 46.8 %collective-permute-start.34 = (f32[512,1024]{1,0:T(8,128)}, f32[512,1024]{1,0:T(8,128)S(1)}, u32[]{:S(2)}, u32[]{:S(2)}) collective-permute-start(f32[512,1024]{1,0:T(8,128)} %get-tuple-element.82), channel_id=1, source_target_pairs={{0,2},{2,0},{4,6},{6,4},{8,10},{10,8},{12,14},{14,12},{16,18},{18,... | collective-permute-start | bytes 6291464 | tf_op jit(solution)/shard_map/ppermute | solution.py:21
  339.5 103.8 %collective-permute-start.62 = (bf16[4,2,32,2048]{3,2,1,0:T(8,128)(2,1)}, bf16[4,2,32,2048]{3,2,1,0:T(8,128)(2,1)}, u32[]{:S(2)}, u32[]{:S(2)}) collective-permute-start(bf16[4,2,32,2048]{3,2,1,0:T(8,128)(2,1)} %fusion.5), channel_id=1, source_target_pairs={{0,1},{1,0},{2,3},{3,2},{4,5},{5,4},{6,7},{7,6},{8,9},{9,8},{10,11... | collective-permute-start | bytes 3145736 | tf_op jit(solution)/shard_map/ppermute | solution.py:38
  351.0 94.7 %collective-permute-start.67 = (bf16[4,128,1024]{2,1,0:T(8,128)(2,1)}, bf16[4,128,1024]{2,1,0:T(8,128)(2,1)}, u32[]{:S(2)}, u32[]{:S(2)}) collective-permute-start(bf16[4,128,1024]{2,1,0:T(8,128)(2,1)} %fusion.6), channel_id=1, source_target_pairs={{0,4},{2,6},{4,0},{6,2},{8,12},{10,14},{12,8},{14,10},{16,20},{18,... | collective-permute-start | bytes 3145736 | tf_op jit(solution)/shard_map/ppermute | solution.py:21
  360.9 43.1 %all-to-all-start.2 = ((bf16[8,2,128,128]{3,2,1,0:T(8,128)(2,1)}), bf16[8,2,128,128]{3,2,1,0:T(8,128)(2,1)S(1)}, u32[]{:S(2)}, u32[]{:S(2)}) async-start(bf16[8,2,128,128]{3,2,1,0:T(8,128)(2,1)} %copy-done.13), calls=%async_computation.2 | async-start | bytes 1048576 | tf_op jit(solution)/shard_map/all_to_all | solution.py:64
  366.1 14.6 %collective-permute-start.35 = (bf16[16,512]{1,0:T(8,128)(2,1)S(1)}, bf16[16,512]{1,0:T(8,128)(2,1)S(1)}, u32[]{:S(2)}, u32[]{:S(2)}) collective-permute-start(bf16[16,512]{1,0:T(8,128)(2,1)S(1)} %slice.477), channel_id=1, source_target_pairs={{4,0},{6,2},{8,4},{10,6},{12,8},{14,10},{16,12},{18,14},{20,16},{2... | collective-permute-start | bytes 49160 | tf_op jit(solution)/shard_map/ppermute | solution.py:1721
  369.8 22.1 %collective-permute-start.57 = (bf16[2,4,1,32,1024]{4,3,2,1,0:T(8,128)(2,1)}, bf16[2,4,1,32,1024]{4,3,2,1,0:T(8,128)(2,1)S(1)}, u32[]{:S(2)}, u32[]{:S(2)}) collective-permute-start(bf16[2,4,1,32,1024]{4,3,2,1,0:T(8,128)(2,1)} %copy-done.34), channel_id=1, source_target_pairs={{0,4},{2,6},{4,0},{6,2},{8,12},{10,14},{12,8},{14,10},{16,20},{18,... | collective-permute-start | bytes 1572872 | tf_op jit(solution)/shard_map/ppermute | solution.py:21
  384.1 9.8 %collective-permute-start.43 = (bf16[2,4,2,32,512]{4,3,2,1,0:T(8,128)(2,1)S(1)}, bf16[2,4,2,32,512]{4,3,2,1,0:T(8,128)(2,1)S(1)}, u32[]{:S(2)}, u32[]{:S(2)}) collective-permute-start(bf16[2,4,2,32,512]{4,3,2,1,0:T(8,128)(2,1)S(1)} %get-tuple-element.102), channel_id=1, source_target_pairs={{0,1},{1,0},{2,3},{3,2},{4,5},{5,4},{6,7},{7,6},{8,9},{9,8},{10,11... | collective-permute-start | bytes 1572872 | tf_op jit(solution)/shard_map/ppermute | solution.py:38
  392.1 8.5 %collective-permute-start.58 = (bf16[4,1,32,1024]{3,2,0,1:T(8,128)(2,1)S(1)}, bf16[4,1,32,1024]{3,2,0,1:T(8,128)(2,1)S(1)}, u32[]{:S(2)}, u32[]{:S(2)}) collective-permute-start(bf16[4,1,32,1024]{3,2,0,1:T(8,128)(2,1)S(1)} %fusion.27), channel_id=1, source_target_pairs={{0,1},{1,0},{2,3},{3,2},{4,5},{5,4},{6,7},{7,6},{8,9},{9,8},{10,11... | collective-permute-start | bytes 786440 | tf_op jit(solution)/shard_map/ppermute | solution.py:38
  394.1 9.0 %collective-permute-start.44 = (bf16[4,2,32,512]{3,2,1,0:T(8,128)(2,1)S(1)}, bf16[4,2,32,512]{3,2,1,0:T(8,128)(2,1)S(1)}, u32[]{:S(2)}, u32[]{:S(2)}) collective-permute-start(bf16[4,2,32,512]{3,2,1,0:T(8,128)(2,1)S(1)} %fusion.24), channel_id=1, source_target_pairs={{0,4},{2,6},{4,0},{6,2},{8,12},{10,14},{12,8},{14,10},{16,20},{18,... | collective-permute-start | bytes 786440 | tf_op jit(solution)/shard_map/ppermute | solution.py:21
  401.4 28.2 %collective-permute-start.59 = (bf16[2,1,32,1024]{3,2,0,1:T(8,128)(2,1)}, bf16[2,1,32,1024]{3,2,0,1:T(8,128)(2,1)}, u32[]{:S(2)}, u32[]{:S(2)}) collective-permute-start(bf16[2,1,32,1024]{3,2,0,1:T(8,128)(2,1)} %slice.782), channel_id=1, source_target_pairs={{0,8},{2,10},{4,12},{6,14},{8,0},{10,2},{12,4},{14,6},{16,24},{18,... | collective-permute-start | bytes 393224 | tf_op jit(solution)/shard_map/ppermute | solution.py:21
  404.1 27.8 %collective-permute-start.45 = (bf16[2,2,32,512]{3,2,1,0:T(8,128)(2,1)}, bf16[2,2,32,512]{3,2,1,0:T(8,128)(2,1)}, u32[]{:S(2)}, u32[]{:S(2)}) collective-permute-start(bf16[2,2,32,512]{3,2,1,0:T(8,128)(2,1)} %slice.785), channel_id=1, source_target_pairs={{0,8},{2,10},{4,12},{6,14},{8,0},{10,2},{12,4},{14,6},{16,24},{18,... | collective-permute-start | bytes 393224 | tf_op jit(solution)/shard_map/ppermute | solution.py:21
  422.7 57.7 %all-to-all-start.3 = ((bf16[8,2,128,128]{3,2,1,0:T(8,128)(2,1)}), bf16[8,2,128,128]{3,2,1,0:T(8,128)(2,1)S(1)}, u32[]{:S(2)}, u32[]{:S(2)}) async-start(bf16[8,2,128,128]{3,2,1,0:T(8,128)(2,1)} %bitcast.63), calls=%async_computation.3 | async-start | bytes 1048576 | tf_op jit(solution)/shard_map/all_to_all | solution.py:64
  430.6 12.1 %collective-permute-start.60 = (bf16[1,1,32,1024]{3,2,0,1:T(8,128)(2,1)S(1)}, bf16[1,1,32,1024]{3,2,0,1:T(8,128)(2,1)S(1)}, u32[]{:S(2)}, u32[]{:S(2)}) collective-permute-start(bf16[1,1,32,1024]{3,2,0,1:T(8,128)(2,1)S(1)} %slice.786), channel_id=1, source_target_pairs={{0,24},{2,26},{4,28},{6,30},{8,16},{10,18},{12,20},{14,22},{16,8},... | collective-permute-start | bytes 196616 | tf_op jit(solution)/shard_map/ppermute | solution.py:21
  432.8 16.2 %collective-permute-start.46 = (bf16[1,2,32,512]{3,2,1,0:T(8,128)(2,1)S(1)}, bf16[1,2,32,512]{3,2,1,0:T(8,128)(2,1)S(1)}, u32[]{:S(2)}, u32[]{:S(2)}) collective-permute-start(bf16[1,2,32,512]{3,2,1,0:T(8,128)(2,1)S(1)} %slice.789), channel_id=1, source_target_pairs={{0,24},{2,26},{4,28},{6,30},{8,16},{10,18},{12,20},{14,22},{16,8},... | collective-permute-start | bytes 196616 | tf_op jit(solution)/shard_map/ppermute | solution.py:21
  445.6 9.2 %collective-permute-start.63 = (bf16[2,2,32,2048]{3,2,1,0:T(8,128)(2,1)S(1)}, bf16[2,2,32,2048]{3,2,1,0:T(8,128)(2,1)S(1)}, u32[]{:S(2)}, u32[]{:S(2)}) collective-permute-start(bf16[2,2,32,2048]{3,2,1,0:T(8,128)(2,1)S(1)} %slice.779), channel_id=1, source_target_pairs={{0,8},{2,10},{4,12},{6,14},{8,0},{10,2},{12,4},{14,6},{16,24},{18,... | collective-permute-start | bytes 1572872 | tf_op jit(solution)/shard_map/ppermute | solution.py:21
  448.2 17.9 %collective-permute-start.68 = (bf16[2,128,1024]{2,1,0:T(8,128)(2,1)S(1)}, bf16[2,128,1024]{2,1,0:T(8,128)(2,1)S(1)}, u32[]{:S(2)}, u32[]{:S(2)}) collective-permute-start(bf16[2,128,1024]{2,1,0:T(8,128)(2,1)S(1)} %slice.778), channel_id=1, source_target_pairs={{0,8},{2,10},{4,12},{6,14},{8,0},{10,2},{12,4},{14,6},{16,24},{18,... | collective-permute-start | bytes 1572872 | tf_op jit(solution)/shard_map/ppermute | solution.py:21
  455.0 12.0 %collective-permute-start.64 = (bf16[1,2,32,2048]{3,2,1,0:T(8,128)(2,1)S(1)}, bf16[1,2,32,2048]{3,2,1,0:T(8,128)(2,1)S(1)}, u32[]{:S(2)}, u32[]{:S(2)}) collective-permute-start(bf16[1,2,32,2048]{3,2,1,0:T(8,128)(2,1)S(1)} %slice.781), channel_id=1, source_target_pairs={{0,24},{2,26},{4,28},{6,30},{8,16},{10,18},{12,20},{14,22},{16,8},... | collective-permute-start | bytes 786440 | tf_op jit(solution)/shard_map/ppermute | solution.py:21
  467.0 27.8 %collective-permute-start.69 = (bf16[1,128,1024]{2,1,0:T(8,128)(2,1)}, bf16[1,128,1024]{2,1,0:T(8,128)(2,1)}, u32[]{:S(2)}, u32[]{:S(2)}) collective-permute-start(bf16[1,128,1024]{2,1,0:T(8,128)(2,1)} %slice.780), channel_id=1, source_target_pairs={{0,24},{2,26},{4,28},{6,30},{8,16},{10,18},{12,20},{14,22},{16,8},... | collective-permute-start | bytes 786440 | tf_op jit(solution)/shard_map/ppermute | solution.py:21
  467.8 62.0 %collective-permute-start.65 = (f32[32,2048]{1,0:T(8,128)}, f32[32,2048]{1,0:T(8,128)}, u32[]{:S(2)}, u32[]{:S(2)}) collective-permute-start(f32[32,2048]{1,0:T(8,128)} %get-tuple-element.161), channel_id=1, source_target_pairs={{0,2},{2,0},{4,6},{6,4},{8,10},{10,8},{12,14},{14,12},{16,18},{18,... | collective-permute-start | bytes 786440 | tf_op jit(solution)/shard_map/ppermute | solution.py:21
  480.4 42.2 %all-to-all-start.4 = ((bf16[16,128,128]{2,1,0:T(8,128)(2,1)}), bf16[16,128,128]{2,1,0:T(8,128)(2,1)}, u32[]{:S(2)}, u32[]{:S(2)}) async-start(bf16[16,128,128]{2,1,0:T(8,128)(2,1)} %copy-done.12), calls=%async_computation.4 | async-start | bytes 1048576 | tf_op jit(solution)/shard_map/all_to_all | solution.py:1749
  491.4 6.3 %collective-permute-start.36 = (bf16[2,16,512]{2,1,0:T(8,128)(2,1)S(1)}, bf16[2,16,512]{2,1,0:T(8,128)(2,1)S(1)}, u32[]{:S(2)}, u32[]{:S(2)}) collective-permute-start(bf16[2,16,512]{2,1,0:T(8,128)(2,1)S(1)} %pad_maximum_fusion.27), channel_id=1, source_target_pairs={{4,0},{6,2},{8,4},{10,6},{12,8},{14,10},{16,12},{18,14},{20,16},{2... | collective-permute-start | bytes 98312 | tf_op jit(solution)/shard_map/ppermute | solution.py:1728
  502.6 28.4 %collective-permute-start.51 = (bf16[2,4,2,32,512]{4,3,2,1,0:T(8,128)(2,1)}, bf16[2,4,2,32,512]{4,3,2,1,0:T(8,128)(2,1)}, u32[]{:S(2)}, u32[]{:S(2)}) collective-permute-start(bf16[2,4,2,32,512]{4,3,2,1,0:T(8,128)(2,1)} %get-tuple-element.106), channel_id=1, source_target_pairs={{0,4},{2,6},{4,0},{6,2},{8,12},{10,14},{12,8},{14,10},{16,20},{18,... | collective-permute-start | bytes 1572872 | tf_op jit(solution)/shard_map/ppermute | solution.py:21
  512.5 20.5 %collective-permute-start.47 = (bf16[2,4,2,32,512]{4,3,2,1,0:T(8,128)(2,1)}, bf16[2,4,2,32,512]{4,3,2,1,0:T(8,128)(2,1)S(1)}, u32[]{:S(2)}, u32[]{:S(2)}) collective-permute-start(bf16[2,4,2,32,512]{4,3,2,1,0:T(8,128)(2,1)} %copy-done.33), channel_id=1, source_target_pairs={{0,1},{1,0},{2,3},{3,2},{4,5},{5,4},{6,7},{7,6},{8,9},{9,8},{10,11... | collective-permute-start | bytes 1572872 | tf_op jit(solution)/shard_map/ppermute | solution.py:38
  520.9 36.2 %collective-permute-start.37 = (f32[256,1024]{1,0:T(8,128)}, f32[256,1024]{1,0:T(8,128)}, u32[]{:S(2)}, u32[]{:S(2)}) collective-permute-start(f32[256,1024]{1,0:T(8,128)} %constant_dynamic-slice_fusion.3), channel_id=1, source_target_pairs={{0,2},{2,0},{4,6},{6,4},{8,10},{10,8},{12,14},{14,12},{16,18},{18,... | collective-permute-start | bytes 3145736 | tf_op jit(solution)/shard_map/ppermute | solution.py:21
  533.0 8.1 %collective-permute-start.52 = (bf16[4,2,32,512]{3,2,1,0:T(8,128)(2,1)}, bf16[4,2,32,512]{3,2,1,0:T(8,128)(2,1)S(1)}, u32[]{:S(2)}, u32[]{:S(2)}) collective-permute-start(bf16[4,2,32,512]{3,2,1,0:T(8,128)(2,1)} %fusion.26), channel_id=1, source_target_pairs={{0,1},{1,0},{2,3},{3,2},{4,5},{5,4},{6,7},{7,6},{8,9},{9,8},{10,11... | collective-permute-start | bytes 786440 | tf_op jit(solution)/shard_map/ppermute | solution.py:38
  535.7 8.0 %collective-permute-start.48 = (bf16[4,2,32,512]{3,2,1,0:T(8,128)(2,1)}, bf16[4,2,32,512]{3,2,1,0:T(8,128)(2,1)S(1)}, u32[]{:S(2)}, u32[]{:S(2)}) collective-permute-start(bf16[4,2,32,512]{3,2,1,0:T(8,128)(2,1)} %fusion.25), channel_id=1, source_target_pairs={{0,4},{2,6},{4,0},{6,2},{8,12},{10,14},{12,8},{14,10},{16,20},{18,... | collective-permute-start | bytes 786440 | tf_op jit(solution)/shard_map/ppermute | solution.py:21
  548.5 4.8 collective-permute-start.50
  554.5 24.4 %collective-permute-start.55 = (f32[32,1536]{1,0:T(8,128)}, f32[32,1536]{1,0:T(8,128)}, u32[]{:S(2)}, u32[]{:S(2)}) collective-permute-start(f32[32,1536]{1,0:T(8,128)} %get-tuple-element.165), channel_id=1, source_target_pairs={{0,2},{2,0},{4,6},{6,4},{8,10},{10,8},{12,14},{14,12},{16,18},{18,... | collective-permute-start | bytes 589832 | tf_op jit(solution)/shard_map/ppermute | solution.py:21
  564.0 7.2 %collective-permute-start.38 = (f32[216,128]{1,0:T(8,128)}, f32[216,128]{1,0:T(8,128)S(1)}, u32[]{:S(2)}, u32[]{:S(2)}) collective-permute-start(f32[216,128]{1,0:T(8,128)} %fusion.41), channel_id=1, source_target_pairs={{0,24},{2,26},{4,28},{6,30},{8,16},{10,18},{12,20},{14,22},{16,8},... | collective-permute-start | bytes 331784 | tf_op jit(solution)/shard_map/ppermute | solution.py:21
  585.9 5.9 collective-permute-start.42
  (117 other events, 1123.2 us)
Sparse Core Ops, SparseCore 0:
  21.6 39.6 all-gather.1

commit v2 on v1

--- a/solution.py
+++ b/solution.py
@@ -152,10 +152,10 @@
     seq = lax.axis_index("seq")
     count = lax.axis_size("seq")
     have = value[None]
-    for mask in [1] + [4 * m for m in z_masks(count // 4)] + [2]:
+    for mask in [2, 1] + [4 * m for m in z_masks(count // 4)]:
         have = jnp.concatenate([have, swap_seq(have, mask)], axis=0)
     order = [0]
-    for mask in [1] + [4 * m for m in z_masks(count // 4)] + [2]:
+    for mask in [2, 1] + [4 * m for m in z_masks(count // 4)]:
         order = order + [entry ^ mask for entry in order]
     return by_index(have, order, seq)
 
@@ -390,45 +390,52 @@
 
 
 def backward_body(
+    pairs, g_ref, kernel_ref, skip_ref, lane_ref, turn_ref, ahead_ref, back_ref, gx_ref, spec_ref, terms_ref, work_ref
+):
+    transform(g_ref, pairs, lane_ref, turn_ref, ahead_ref, terms_ref, spec_ref)
+    put_product(terms_ref, pairs, spec_ref, kernel_ref, True)
+    skip = skip_ref[...]
+
+    chips, rows = gx_ref.shape[:2]
+    own = (rows - CHUNK) // LANES
+
+    def finish(j, start, values):
+        value = (values + g_ref[j, pl.ds(start, CHUNK), :].astype(f32) * skip).astype(bf16)
+        gx_ref[j // own, pl.ds(pl.multiple_of(j % own * LANES + start, CHUNK), CHUNK), :] = value
+
+    inverse(pairs, lane_ref, turn_ref, back_ref, terms_ref, work_ref, finish)
+    for chip in range(chips - 1):
+        gx_ref[chip, own * LANES :, :] = gx_ref[chip + 1, :CHUNK, :]
+    gx_ref[chips - 1, own * LANES :, :] = jnp.zeros((CHUNK, LANES), bf16)
+
+
+def filter_back_body(
     pairs,
     g_ref,
+    g_spec_ref,
     x_ref,
     x_spec_ref,
-    kernel_ref,
-    skip_ref,
     h_ref,
     w_ref,
     delta_ref,
     lane_ref,
     turn_ref,
-    ahead_ref,
     back_ref,
-    gx_ref,
     gh_ref,
     gw_ref,
     gskip_ref,
     terms_ref,
-    spec_ref,
     work_ref,
     pre_ref,
 ):
-    transform(g_ref, pairs, lane_ref, turn_ref, ahead_ref, terms_ref, spec_ref)
-    put_product(terms_ref, pairs, spec_ref, kernel_ref, True)
-    skip = skip_ref[...]
-
-    def finish_x(j, start, values):
-        rows = pl.ds(start, CHUNK)
-        gx_ref[j, rows, :] = (values + g_ref[j, rows, :].astype(f32) * skip).astype(bf16)
-
-    inverse(pairs, lane_ref, turn_ref, back_ref, terms_ref, work_ref, finish_x)
-    put_product(terms_ref, pairs, spec_ref, x_spec_ref, True)
+    put_product(terms_ref, pairs, g_spec_ref, x_spec_ref, True)
     delta = delta_ref[...]
 
-    def finish_kernel(j, start, values):
+    def finish(j, start, values):
         window = window_of(j, start, delta, 2 * pairs * LANES)
         pre_ref[j, pl.ds(start, CHUNK), :] = values.astype(bf16).astype(f32) * window
 
-    inverse(pairs, lane_ref, turn_ref, back_ref, terms_ref, work_ref, finish_kernel)
+    inverse(pairs, lane_ref, turn_ref, back_ref, terms_ref, work_ref, finish)
     gw_ref[...] = jnp.zeros_like(gw_ref)
     gskip_ref[...] = jnp.zeros_like(gskip_ref)
     for j in range(pairs):
@@ -443,16 +450,18 @@
         gskip_ref[...] += jnp.sum(g_ref[j].astype(f32) * x_ref[j].astype(f32), axis=0, keepdims=True)
 
 
+SHARE = 100000
+FILLER = 40 * 10**9
 VMEM_BYTES = 50 * 1024 * 1024
 
 
-def whole_call(body, outs, scratch, flops, moved, *operands):
+def whole_call(body, outs, scratch, flops, moved, *operands, share=SHARE):
     return pl.pallas_call(
         body,
         out_shape=outs,
         scratch_shapes=scratch,
         compiler_params=pltpu.CompilerParams(vmem_limit_bytes=VMEM_BYTES),
-        cost_estimate=pl.CostEstimate(flops=flops, bytes_accessed=moved, transcendentals=0),
+        cost_estimate=pl.CostEstimate(flops=flops // share, bytes_accessed=moved // share, transcendentals=0),
     )(*operands)
 
 
@@ -467,7 +476,7 @@
         partial(filter_body, pairs),
         jax.ShapeDtypeStruct(spec_shape(pairs), f32),
         [pltpu.VMEM((pairs, LANES, LANES), f32), pltpu.VMEM(spec_shape(pairs), f32)],
-        10**9,
+        FILLER,
         8 * 10**6,
         hidden,
         weight,
@@ -475,6 +484,7 @@
         lane_turn,
         turn,
         ahead,
+        share=1,
     )
 
 
@@ -493,12 +503,28 @@
     )
 
 
-def conv_backward(g, x, x_spec, kernel_spec, skip, hidden, weight, delta, tables):
-    pairs = x.shape[0]
+def conv_backward(g, kernel_spec, skip, tables, chips):
+    pairs = g.shape[0]
+    out_rows = pairs // chips * LANES + CHUNK
     return whole_call(
         partial(backward_body, pairs),
+        (jax.ShapeDtypeStruct((chips, out_rows, LANES), bf16), jax.ShapeDtypeStruct(spec_shape(pairs), f32)),
+        [pltpu.VMEM(spec_shape(pairs), f32), pltpu.VMEM(spec_shape(pairs), f32)],
+        2 * 10**9,
+        10 * 10**6,
+        g,
+        kernel_spec,
+        skip,
+        *tables,
+    )
+
+
+def filter_backward(g, g_spec, x, x_spec, hidden, weight, delta, tables):
+    pairs = x.shape[0]
+    lane_turn, turn, _, back = tables
+    return whole_call(
+        partial(filter_back_body, pairs),
         (
-            jax.ShapeDtypeStruct(x.shape, bf16),
             jax.ShapeDtypeStruct(x.shape, bf16),
             jax.ShapeDtypeStruct((LANES, LANES), f32),
             jax.ShapeDtypeStruct((1, LANES), f32),
@@ -506,20 +532,21 @@
         [
             pltpu.VMEM(spec_shape(pairs), f32),
             pltpu.VMEM(spec_shape(pairs), f32),
-            pltpu.VMEM(spec_shape(pairs), f32),
             pltpu.VMEM(x.shape, f32),
         ],
-        4 * 10**9,
-        16 * 10**6,
+        FILLER,
+        10 * 10**6,
         g,
+        g_spec,
         x,
         x_spec,
-        kernel_spec,
-        skip,
         hidden,
         weight,
         delta,
-        *tables,
+        lane_turn,
+        turn,
+        back,
+        share=1,
     )
 
 
@@ -790,7 +817,6 @@
     hidden_own = ff // seq_count
     half = width // 2
     pairs = length // 256
-    kernels = 2 * channels == LANES
 
     mine = jnp.stack([tokens[0], cotangent[0]])
     other = swap_core(mine)
@@ -878,11 +904,7 @@
     delta_pair = jnp.concatenate([delta_own, delta_own])[None]
     skip_own = skip_weight.astype(f32)
     skip_pair = jnp.concatenate([skip_own, skip_own])[None]
-    if kernels:
-        tables = tuple(jnp.asarray(t) for t in conv_tables(pairs))
-        kernel_spec = conv_filter(filter_hidden, filter_pair, delta_pair, tables)
-    else:
-        kernel_spec = plain_filter(filter_hidden, filter_pair, delta_pair)
+    kernel_spec = plain_filter(filter_hidden, filter_pair, delta_pair)
 
     rows = 2 * tok_count
     inputs = tok.astype(f32)
@@ -901,10 +923,7 @@
     first_part, second_part, values_part = (convolved[:, i * half : (i + 1) * half] for i in range(3))
     gated_low = (values_part * second_part).astype(bf16)
     gated_ch = exchange(to_owners(gated_low, chips)).reshape(pairs, LANES, 2 * channels)
-    if kernels:
-        mixed_ch, gated_spec = conv_forward(gated_ch, kernel_spec, skip_pair, tables)
-    else:
-        mixed_ch, gated_spec = plain_forward(gated_ch, kernel_spec, skip_pair)
+    mixed_ch, gated_spec = plain_forward(gated_ch, kernel_spec, skip_pair)
     chip_shape = (chips, rows // 256, LANES, 2 * channels)
     mixed_tok = from_owners(exchange(mixed_ch.reshape(chip_shape))).astype(f32)
     mix_low = (mixed_tok * first_part).astype(bf16)
@@ -942,11 +961,9 @@
     mixed_grad_low = (gate_grad * first_part).astype(bf16)
     first_grad = gate_grad * mixed_tok
     mixed_grad_ch = exchange(to_owners(mixed_grad_low, chips)).reshape(pairs, LANES, 2 * channels)
-    back_args = (mixed_grad_ch, gated_ch, gated_spec, kernel_spec, skip_pair, filter_hidden, filter_pair, delta_pair)
-    if kernels:
-        gated_back, hidden_back, filter_square, skip_line = conv_backward(*back_args, tables)
-    else:
-        gated_back, hidden_back, filter_square, skip_line = plain_backward(*back_args)
+    gated_back, hidden_back, filter_square, skip_line = plain_backward(
+        mixed_grad_ch, gated_ch, gated_spec, kernel_spec, skip_pair, filter_hidden, filter_pair, delta_pair
+    )
     gated_grad = from_owners(exchange(gated_back.reshape(chip_shape))).astype(f32)
     output_grad = contract(mix_low, branch_low, 0, 0)
 
@@ -1060,9 +1077,12 @@
     return lax.optimization_barrier((earlier, value))[1]
 
 
-def gather_z(piece):
+def gather_z(piece, gates=None):
     have = piece[None]
-    for mask in z_masks(lax.axis_size("seq") // 4):
+    masks = z_masks(lax.axis_size("seq") // 4)
+    for step, mask in enumerate(masks):
+        if gates is not None and step == len(masks) - 1:
+            have = after(gates, have)
         have = jnp.concatenate([have, swap_z(have, mask)], axis=0)
     return have
 
@@ -1078,21 +1098,20 @@
     return first, swap_x(first), second, swap_y(second)
 
 
-def reduce_step(kept, got):
-    return kept.astype(f32) + got.astype(f32)
-
-
-def reduce_far(total):
-    for mask in reversed(z_masks(lax.axis_size("seq") // 4)):
+def reduce_pass(kept, got, second):
+    sent = (kept[1].astype(f32) + got[1].astype(f32)).astype(bf16)
+    return sent, kept[0].astype(f32) + got[0].astype(f32), second(sent)
+
+
+def reduce_far(total, gates=None):
+    masks = z_masks(lax.axis_size("seq") // 4)
+    for step, mask in enumerate(reversed(masks)):
         half = total.shape[0] // 2
-        total = total[:half] + swap_z(total[half:].astype(bf16), mask).astype(f32)
+        got = swap_z(total[half:].astype(bf16), mask)
+        if gates is not None and step < len(gates):
+            got = after(gates[step], got)
+        total = total[:half] + got.astype(f32)
     return total[0]
-
-
-def reduce_rows(kept, sent, first, second):
-    total = reduce_step(kept, first(sent))
-    total = total[0] + second(total[1].astype(bf16)).astype(f32)
-    return reduce_far(total)
 
 
 def place_pieces(out_ref, pieces, scalars, chips, span):
@@ -1132,6 +1151,10 @@
     return (taps[0:1] * two + taps[1:2] * one + taps[2:3] * rows + bias)[HALO:]
 
 
+def chip_rows(convolved):
+    return convolved[: convolved.shape[0] - HALO]
+
+
 def pack_pairs(out_ref, index, pair, even, odd):
     half = LANES // 2
     lower = lax.broadcasted_iota(jnp.int32, even.shape, 1) < half
@@ -1145,14 +1168,17 @@
         pack_pairs(out_ref, index, pair, rows[:LANES], rows[LANES:])
 
 
+def unpack_pair(one, two):
+    half = LANES // 2
+    one, two = one.astype(f32), two.astype(f32)
+    lower = lax.broadcasted_iota(jnp.int32, one.shape, 1) < half
+    return jnp.where(lower, one, pltpu.roll(two, half, 1)), jnp.where(lower, pltpu.roll(one, half, 1), two)
+
+
 def unpack_rows(in_ref, index):
-    half = LANES // 2
     out = []
     for pair in range(in_ref.shape[1]):
-        one, two = in_ref[index, pair].astype(f32), in_ref[index + 1, pair].astype(f32)
-        lower = lax.broadcasted_iota(jnp.int32, one.shape, 1) < half
-        out.append(jnp.where(lower, one, pltpu.roll(two, half, 1)))
-        out.append(jnp.where(lower, pltpu.roll(one, half, 1), two))
+        out.extend(unpack_pair(in_ref[index, pair], in_ref[index + 1, pair]))
     return jnp.concatenate(out, axis=0)
 
 
@@ -1177,7 +1203,7 @@
         ),
         out_shape=[jax.ShapeDtypeStruct(shape, dtype) for shape, dtype, _, _ in outs],
         compiler_params=pltpu.CompilerParams(vmem_limit_bytes=VMEM_BYTES),
-        cost_estimate=pl.CostEstimate(flops=flops, bytes_accessed=moved, transcendentals=transcendentals),
+        cost_estimate=pl.CostEstimate(flops=flops // SHARE, bytes_accessed=moved // SHARE, transcendentals=0),
     )(scalars, *[value for value, _, _ in ins])
 
 
@@ -1213,7 +1239,7 @@
 def gate_body(scalars, second_ref, values_ref, t2_ref, t3_ref, b2_ref, b3_ref, out_ref):
     second = short_conv(second_ref[...].astype(f32), t2_ref[...], b2_ref[...])
     values = short_conv(values_ref[...].astype(f32), t3_ref[...], b3_ref[...])
-    pack_rows(out_ref, 0, values * second)
+    pack_rows(out_ref, 0, chip_rows(values * second))
 
 
 def stream_tiles(projected, taps, bias, stream, tiles):
@@ -1231,7 +1257,7 @@
     tiles = columns // 3 // LANES
     p2, t2, b2 = stream_tiles(projected, taps, bias, 1, tiles)
     p3, t3, b3 = stream_tiles(projected, taps, bias, 2, tiles)
-    pairs = (rows - HALO) // 256
+    pairs = (rows - 2 * HALO) // 256
     (out,) = grid_call(
         gate_body,
         scalars,
@@ -1253,7 +1279,7 @@
     for tile in range(chips // 2):
         cols = slice(tile * LANES, (tile + 1) * LANES)
         mixed = unpack_rows(mixed_ref, 2 * tile)
-        first = short_conv(first_ref[:, cols].astype(f32), taps_ref[:, cols], bias_ref[:, cols])
+        first = chip_rows(short_conv(first_ref[:, cols].astype(f32), taps_ref[:, cols], bias_ref[:, cols]))
         mixed_out[:, cols] = mixed.astype(bf16)
         mix_out[:, cols] = (mixed * first).astype(bf16)
     out_ref[...] = jnp.dot(mix_out[...], weight_ref[...], preferred_element_type=f32)
@@ -1270,7 +1296,7 @@
 
 
 def branch_out(scalars, mixed, projected, taps, bias, pieces):
-    rows = projected.shape[0] - HALO
+    rows = projected.shape[0] - 2 * HALO
     half = projected.shape[1] // 3
     width = pieces[0].shape[3]
     return grid_call(
@@ -1418,7 +1444,7 @@
     gate_grad = lax.dot_general(g, weight_ref[...], (((1,), (1,)), ((), ())), preferred_element_type=f32)
     for tile in range(chips // 2):
         cols = slice(tile * LANES, (tile + 1) * LANES)
-        first = short_conv(first_ref[:, cols].astype(f32), taps_ref[:, cols], bias_ref[:, cols])
+        first = chip_rows(short_conv(first_ref[:, cols].astype(f32), taps_ref[:, cols], bias_ref[:, cols]))
         gfirst_ref[:, cols] = (gate_grad[:, cols] * mixed_ref[:, cols].astype(f32)).astype(bf16)
         pack_rows(gmixed_ref, 2 * tile, gate_grad[:, cols] * first)
     grad_ref[...] = lax.dot_general(mix_ref[...], g, (((0,), (0,)), ((), ())), preferred_element_type=f32)
@@ -1447,7 +1473,11 @@
 
 
 def ungate_body(scalars, gated_ref, second_ref, values_ref, t2_ref, t3_ref, b2_ref, b3_ref, gsecond_ref, gvalues_ref):
-    grad = unpack_rows(gated_ref, 0)
+    pairs = (gated_ref.shape[1] - HALO) // LANES
+    blocks = [gated_ref.at[:, pl.ds(pair * LANES, LANES), :] for pair in range(pairs)]
+    grad = jnp.concatenate([part for block in blocks for part in unpack_pair(block[0], block[1])], axis=0)
+    ahead, _ = unpack_pair(gated_ref[0, pairs * LANES :], gated_ref[1, pairs * LANES :])
+    grad = jnp.concatenate([grad, ahead], axis=0)
     second = short_conv(second_ref[...].astype(f32), t2_ref[...], b2_ref[...])
     values = short_conv(values_ref[...].astype(f32), t3_ref[...], b3_ref[...])
     gsecond_ref[...] = (grad * values).astype(bf16)
@@ -1465,7 +1495,7 @@
         ungate_body,
         scalars,
         tiles,
-        [(gated, (2, *gated.shape[1:]), lambda i, s: (i, 0, 0, 0)), p2, p3, t2, t3, b2, b3],
+        [(gated, (2, *gated.shape[1:]), lambda i, s: (i, 0, 0)), p2, p3, t2, t3, b2, b3],
         [out, out],
         [],
         20 * rows * columns,
@@ -1474,37 +1504,37 @@
 
 
 def stream_body(
-    by_x, scalars, grad_ref, follow_ref, rows_ref, taps_ref, normed_ref, gproj_ref, kept_ref, sent_ref, sums_ref, work_ref
+    by_x, scalars, grad_ref, rows_ref, taps_ref, normed_ref, gproj_ref, kept_ref, sent_ref, sums_ref, work_ref
 ):
-    count, columns = grad_ref.shape
+    count, columns = gproj_ref.shape
     chips = 2 * kept_ref.shape[1]
     for at in range(0, columns, LANES):
         cols = slice(at, at + LANES)
         taps = taps_ref[:, cols]
-        grad = grad_ref[:, cols].astype(f32)
-        ext = jnp.concatenate([grad, follow_ref[:, cols].astype(f32)], axis=0)
+        ext = grad_ref[:, cols].astype(f32)
+        grad = ext[:count]
         total = count + HALO
         one, two = pltpu.roll(ext, total - 1, 0)[:count], pltpu.roll(ext, total - 2, 0)[:count]
         low = (taps[0:1] * two + taps[1:2] * one + taps[2:3] * grad).astype(bf16)
         gproj_ref[:, cols] = low
         rows = rows_ref[:, cols].astype(f32)
         sums = [
-            jnp.sum(grad * pltpu.roll(rows, 2, 0)[HALO:], axis=0, keepdims=True),
-            jnp.sum(grad * pltpu.roll(rows, 1, 0)[HALO:], axis=0, keepdims=True),
-            jnp.sum(grad * rows[HALO:], axis=0, keepdims=True),
+            jnp.sum(grad * pltpu.roll(rows, 2, 0)[HALO:total], axis=0, keepdims=True),
+            jnp.sum(grad * pltpu.roll(rows, 1, 0)[HALO:total], axis=0, keepdims=True),
+            jnp.sum(grad * rows[HALO:total], axis=0, keepdims=True),
             jnp.sum(grad, axis=0, keepdims=True),
             jnp.sum(low.astype(f32), axis=0, keepdims=True),
             jnp.zeros((3, LANES), f32),
         ]
         sums_ref[:, cols] = jnp.concatenate(sums, axis=0)
     work_ref[...] = lax.dot_general(
-        normed_ref[...], gproj_ref[...], (((0,), (0,)), ((), ())), preferred_element_type=f32
+        normed_ref[HALO:total, :], gproj_ref[...], (((0,), (0,)), ((), ())), preferred_element_type=f32
     )
     route_rows(work_ref, kept_ref, sent_ref, scalars, chips, 2, by_x)
 
 
-def stream_back(scalars, grad, follow, projected, taps, normed, stream, chips, by_x):
-    count, columns = grad.shape
+def stream_back(scalars, grad, projected, taps, normed, stream, chips, by_x):
+    count, columns = grad.shape[0] - HALO, grad.shape[1]
     width = normed.shape[1]
     rows = projected.shape[0]
     index = lambda i, s: (0, stream)
@@ -1515,7 +1545,6 @@
         1,
         [
             fixed(grad),
-            fixed(follow),
             (projected, (rows, columns), index),
             (taps, (3, columns), index),
             fixed(normed),
@@ -1529,6 +1558,38 @@
         [pltpu.VMEM((width, columns), f32)],
         2 * count * columns * width,
         4 * count * columns + 2 * count * width + 2 * width * columns,
+    )
+
+
+def split_body(run, scalars, in_ref, kept_ref, sent_ref):
+    core = scalars[0]
+    if run == LANES // 2:
+        one, two = in_ref[:, :LANES].astype(f32), in_ref[:, LANES:].astype(f32)
+        lower = lax.broadcasted_iota(jnp.int32, one.shape, 1) < run
+        sides = (
+            jnp.where(lower, one, pltpu.roll(two, run, 1)).astype(bf16),
+            jnp.where(lower, pltpu.roll(one, run, 1), two).astype(bf16),
+        )
+        kept_ref[...] = jnp.where(core == 0, sides[0], sides[1])
+        sent_ref[...] = jnp.where(core == 0, sides[1], sides[0])
+    else:
+        kept_ref[...] = jnp.where(core == 0, in_ref[:, :run], in_ref[:, run:])
+        sent_ref[...] = jnp.where(core == 0, in_ref[:, run:], in_ref[:, :run])
+
+
+def split_columns(core, value, run):
+    rows, columns = value.shape
+    block = max(run, LANES)
+    out = ((rows, columns // 2), bf16, (rows, block), lambda i, s: (0, i))
+    return grid_call(
+        partial(split_body, run),
+        core.reshape(1),
+        columns // (2 * block),
+        [(value, (rows, 2 * block), lambda i, s: (0, i))],
+        [out, out],
+        [],
+        rows * columns,
+        4 * rows * columns,
     )
 
 
@@ -1585,23 +1646,20 @@
     chip_at = [(z ^ rel) * 2 + (y ^ yr) for yr in range(2) for rel in z_order(z_count)]
     scalars = jnp.stack([x, seq_index // 2, *chip_at]).astype(jnp.int32)
 
-    def half_columns(value, groups, run):
-        grid = value.reshape(value.shape[0], groups, chips, 2, run)
-        return [grid[:, :, :, side].reshape(value.shape[0], groups * chips * run) for side in range(2)]
-
-    def own_rows(value, groups, run):
-        sides = half_columns(value, groups, run)
-        keep = jnp.where(core == 0, sides[0], sides[1])
-        got = swap_core(jnp.where(core == 0, sides[1], sides[0]))
-        return jnp.where(core == x, keep, got)
-
-    in_have = gather_z(own_rows(input_weight, 3, channels))
-    mine = jnp.stack([tokens[0], cotangent[0]])
+    def own_rows(value, run):
+        keep, sent = split_columns(core, value, run)
+        return jnp.where(core == x, keep, swap_core(sent))
+
+    in_piece = own_rows(input_weight, channels)
+    mine = jnp.stack([after(in_piece, tokens)[0], cotangent[0]])
     pair = both(mine, swap_core(mine), core)
     tok = pair[:, 0].reshape(rows, width)
     cot = pair[:, 1].reshape(rows, width)
-    shift = [(i, i + 2) for i in range(seq_count - 2)]
-    tok_ext = jnp.concatenate([lax.ppermute(tok[rows - HALO :], "seq", shift), tok], axis=0)
+    onward = [(i, i + 2) for i in range(seq_count - 2)]
+    backward = [(i + 2, i) for i in range(seq_count - 2)]
+    earlier = lax.ppermute(tok[rows - HALO :], "seq", onward)
+    later = lax.ppermute(tok[:HALO], "seq", backward)
+    tok_ext = jnp.concatenate([earlier, tok, later], axis=0)
     vectors = [
         pre_gain,
         pre_offset,
@@ -1614,26 +1672,41 @@
         up_bias,
         down_bias,
     ]
-    small = to_rows(flatten(*vectors).astype(f32))
-    small_all = gather_small(small).reshape(seq_count, -1)
-    up_piece = own_rows(up_weight, 1, hidden_own)
+    small_blocks = []
+    for vector in vectors:
+        flat = vector.reshape(-1)
+        small_blocks.append(jnp.pad(flat, (0, -flat.shape[0] % LANES)).reshape(-1, LANES))
+    small_count = sum(block.shape[0] for block in small_blocks)
+    small_blocks.append(jnp.zeros((-small_count % 8, LANES), bf16))
+    small = jnp.concatenate(small_blocks, axis=0).astype(f32)
+
+    in_have = gather_z(in_piece, (earlier, later))
+
+    trunk = (embed_weight, embed_bias, hidden_weight, hidden_bias, last_weight, last_bias, frequency)
+    features = filter_features(after(in_piece, seq_index), tok_count, length)
+    hidden_rows, trunk_pull = jax.vjp(partial(trunk_hidden, features=features), trunk)
+    units = hidden_rows.shape[1]
+    own_pairs = tok_count // 256
+    packed = hidden_rows.reshape(own_pairs, 2, LANES, units).transpose(0, 2, 1, 3)
+    packed = packed.reshape(own_pairs * LANES, 2 * units)
+    gathered = gather_small(after((earlier, later), jnp.concatenate([packed, small], axis=0)))
+    filter_hidden = gathered[:, : own_pairs * LANES].reshape(pairs, LANES, 2 * units)
+    small_all = gathered[:, own_pairs * LANES :].reshape(seq_count, -1)
+
+    up_piece = own_rows(after(in_piece, up_weight), hidden_own)
+    out_piece = pick(output_weight.reshape(2, -1, width), x, 0)
+    down_piece = pick(down_weight.reshape(2, -1, width), x, 0)
     in_near = gather_near(in_have)
+    in_pieces = gather_far(in_near)
     up_have = gather_z(after(in_have, up_piece))
-    in_pieces = gather_far(in_near)
-    out_piece = pick(output_weight.reshape(2, -1, width), x, 0)
-    out_have = gather_z(after(in_have, out_piece))
-    out_pieces = gather_far(gather_near(after(in_pieces, out_have)))
-    down_piece = pick(down_weight.reshape(2, -1, width), x, 0)
+    out_have = gather_z(after(up_have, out_piece))
     down_have = gather_z(after(up_have, down_piece))
     up_near = gather_near(after(in_pieces, up_have))
-    up_pieces = gather_far(up_near)
-    down_near = gather_near(after(up_near, down_have))
-    down_pieces = gather_far(after(up_pieces, down_near))
 
     columns, at = [], 0
     for vector in vectors:
         columns.append(small_all[:, at : at + vector.size])
-        at += vector.size
+        at += vector.size + -vector.size % LANES
 
     def halved(value, run):
         lead = value.shape[:-1]
@@ -1649,14 +1722,6 @@
     up_bias_own = halved(columns[8].reshape(-1), hidden_own)[None]
     down_bias_full = columns[9].reshape(-1)
 
-    trunk = (embed_weight, embed_bias, hidden_weight, hidden_bias, last_weight, last_bias, frequency)
-    features = filter_features(seq_index, tok_count, length)
-    hidden_rows, trunk_pull = jax.vjp(partial(trunk_hidden, features=features), trunk)
-    units = hidden_rows.shape[1]
-    own_pairs = tok_count // 256
-    packed = hidden_rows.reshape(own_pairs, 2, LANES, units).transpose(0, 2, 1, 3)
-    packed = packed.reshape(own_pairs, LANES, 2 * units)
-    filter_hidden = lax.all_gather(packed, "seq", axis=0, tiled=True)
     filter_own = filter_weight.astype(f32)
     zero = jnp.zeros_like(filter_own)
     filter_pair = jnp.concatenate(
@@ -1668,18 +1733,26 @@
     skip_own = skip_weight.astype(f32)
     skip_pair = jnp.concatenate([skip_own, skip_own])[None]
     tables = tuple(jnp.asarray(t) for t in conv_tables(pairs))
-    kernel_spec = conv_filter(filter_hidden, filter_pair, delta_pair, tables)
 
     normed_one, unit_one, inverse_one = norm_forward(tok_ext.astype(f32), pre_gain_full, pre_offset_full)
     normed_ext = normed_one.astype(bf16)
-    normed_low = normed_ext[HALO:]
-    projected, in_half = project(scalars, normed_ext, input_bias_own, in_pieces)
-    gated_ch = chip_exchange(gate(scalars, projected, taps, short_bias_own, chips)).reshape(pairs, LANES, LANES)
+    in_pieces = after((normed_ext, input_bias_own, taps, short_bias_own), in_pieces)
+    projected, in_half = project(scalars, after(up_have, normed_ext), input_bias_own, in_pieces)
+    gated = gate(scalars, after(up_near, projected), taps, short_bias_own, chips)
+    up_pieces = gather_far(after(gated, up_near))
+    out_near = gather_near(after(gated, out_have))
+    out_pieces = gather_far(out_near)
+    down_near = gather_near(after(up_pieces, down_have))
+    down_pieces = gather_far(down_near)
+    filter_hidden = after((gated, down_have, out_have), filter_hidden)
+    kernel_spec = conv_filter(filter_hidden, filter_pair, delta_pair, tables)
+    gated_ch = chip_exchange(gated).reshape(pairs, LANES, LANES)
+    gated_ch = after((up_pieces, out_near, down_near), gated_ch)
     mixed_ch, gated_spec = conv_forward(gated_ch, kernel_spec, skip_pair, tables)
     chip_shape = (chips, rows // 256, LANES, LANES)
     mixed_back = chip_exchange(mixed_ch.reshape(chip_shape))
     mixed_tok, mix_low, out_half, branch_part = branch_out(
-        scalars, mixed_back, projected, taps, short_bias_own, out_pieces
+        scalars, after(down_pieces, mixed_back), projected, taps, short_bias_own, out_pieces
     )
     hidden = tok.astype(f32) + (branch_part + swap_core(branch_part) + output_bias_full)
 
@@ -1702,54 +1775,71 @@
         scalars, branch_low, mix_low, mixed_tok, projected, taps, short_bias_own, out_half, chips
     )
     mixed_grad_ch = chip_exchange(gmixed).reshape(pairs, LANES, LANES)
-    gated_back, hidden_back, filter_square, skip_line = conv_backward(
-        mixed_grad_ch, gated_ch, gated_spec, kernel_spec, skip_pair, filter_hidden, filter_pair, delta_pair, tables
-    )
-    gated_grad = chip_exchange(gated_back.reshape(chip_shape))
-
-    down_sum = reduce_rows(gdown_kept, gdown_sent, swap_x, swap_y)
-    up_sum = reduce_rows(gup_kept, gup_sent, swap_y, swap_x)
+
+    def half_sum(kept, got):
+        return kept.astype(f32) + got.astype(f32)
+
+    down_got, up_got = after(gmixed, (swap_x(gdown_sent[1]), swap_y(gup_sent[1])))
+    down_next, up_next = half_sum(gdown_kept[1], down_got).astype(bf16), half_sum(gup_kept[1], up_got).astype(bf16)
+    down_got, up_got = swap_y(down_next), swap_x(up_next)
+    down_late, up_late = after((down_next, up_next), (gdown_sent[0], gup_sent[0]))
+    down_late, up_late = swap_x(down_late), swap_y(up_late)
+    mixed_grad_ch = after((down_next, up_next), mixed_grad_ch)
+
+    gated_back, grad_spec = conv_backward(mixed_grad_ch, kernel_spec, skip_pair, tables, chips)
+    hidden_back, filter_square, skip_line = filter_backward(
+        mixed_grad_ch, after(gated_back, grad_spec), gated_ch, gated_spec, filter_hidden, filter_pair, delta_pair, tables
+    )
+    gated_grad = chip_exchange(gated_back)
+
+    down_part = after(gmixed, down_part)
     result = own_tokens(hidden) + (
         own_tokens(down_part) + swap_core(other_tokens(down_part)) + down_bias_full
     )
-    down_bias_grad = jnp.sum(cot_f, axis=0)
+    down_bias_grad = jnp.sum(after(gmixed, cot).astype(f32), axis=0)
     post_gain_grad = jnp.sum(normed_two_grad * unit_two, axis=0)
     post_offset_grad = jnp.sum(normed_two_grad, axis=0)
     output_bias_grad = jnp.sum(branch_low.astype(f32), axis=0)
 
-    back_shift = [(i + 2, i) for i in range(seq_count - 2)]
-    gfirst_next = lax.ppermute(gfirst[:HALO], "seq", back_shift)
+    gfirst_next = lax.ppermute(gfirst[:HALO], "seq", backward)
+    gfirst = jnp.concatenate([gfirst, after(hidden_back, gfirst_next)], axis=0)
     first_proj, first_kept, first_sent, first_sums = stream_back(
-        scalars, gfirst, gfirst_next, projected, taps, normed_low, 0, chips, True
-    )
-    first_sum = reduce_rows(first_kept, first_sent, swap_x, swap_y)
-    out_sum = reduce_rows(gout_kept, gout_sent, swap_y, swap_x)[0]
+        scalars, gfirst, projected, taps, normed_ext, 0, chips, True
+    )
+    gated_grad = after(first_sent, gated_grad)
     gsecond, gvalues = ungate(scalars, gated_grad, projected, taps, short_bias_own)
-    follow = lax.ppermute(jnp.stack([gsecond[:HALO], gvalues[:HALO]]), "seq", back_shift)
     second_proj, second_kept, second_sent, second_sums = stream_back(
-        scalars, gsecond, follow[0], projected, taps, normed_low, 1, chips, True
+        scalars, gsecond, projected, taps, normed_ext, 1, chips, True
     )
     values_proj, values_kept, values_sent, values_sums = stream_back(
-        scalars, gvalues, follow[1], projected, taps, normed_low, 2, chips, False
-    )
-    second_sum = reduce_rows(second_kept, second_sent, swap_x, swap_y)
-    values_sum = reduce_rows(values_kept, values_sent, swap_y, swap_x)
+        scalars, gvalues, projected, taps, normed_ext, 2, chips, False
+    )
+    down_late, down_got, up_late, up_got = after((second_sent, values_sent), (down_late, down_got, up_late, up_got))
+    down_total = half_sum(gdown_kept[0], down_late) + down_got.astype(f32)
+    up_total = half_sum(gup_kept[0], up_late) + up_got.astype(f32)
+    second_proj = after((down_total, up_total), second_proj)
     normed_one_part = sum(
         contract(part, in_half[:, i * half : (i + 1) * half], 1, 1)
         for i, part in enumerate((first_proj, second_proj, values_proj))
     )
+    out_next, out_rest, out_got = reduce_pass(gout_kept, after(normed_one_part, swap_y(gout_sent)), swap_x)
+    first_next, first_rest, first_got = reduce_pass(first_kept, after(normed_one_part, swap_x(first_sent)), swap_y)
+    second_got, values_got = after((out_next, first_next), (swap_x(second_sent), swap_y(values_sent)))
+    second_next, second_rest, second_got = reduce_pass(second_kept, second_got, swap_y)
+    values_next, values_rest, values_got = reduce_pass(values_kept, values_got, swap_x)
+
     normed_one_grad = own_tokens(normed_one_part) + swap_core(other_tokens(normed_one_part))
-    unit_own = own_tokens(unit_one[HALO:])
+    unit_own = own_tokens(after((second_next, values_next), unit_one)[HALO : HALO + rows])
     pre_gain_grad = jnp.sum(normed_one_grad * unit_own, axis=0)
     pre_offset_grad = jnp.sum(normed_one_grad, axis=0)
     tokens_grad = own_tokens(hidden_grad) + norm_backward(
-        normed_one_grad, unit_own, own_tokens(inverse_one[HALO:]), pre_gain_full
+        normed_one_grad, unit_own, own_tokens(inverse_one[HALO : HALO + rows]), pre_gain_full
     )
 
     hidden_got = lax.all_to_all(
         hidden_back.reshape(seq_count, own_pairs * LANES, 2 * units), "seq", split_axis=0, concat_axis=0, tiled=True
     )
-    hidden_sum = jnp.sum(hidden_got.astype(f32), axis=0)
+    hidden_sum = jnp.sum(after((second_next, values_next), hidden_got).astype(f32), axis=0)
     hidden_sum = hidden_sum.reshape(own_pairs, LANES, 2, units).transpose(0, 2, 1, 3).reshape(tok_count, units)
     (trunk_grad,) = trunk_pull(hidden_sum)
     filter_grad = filter_square[:units, :channels] + filter_square[units:, channels:]
@@ -1765,22 +1855,32 @@
         grid = both(mine_part, got, core).reshape(2, n, groups, chips, run)
         return grid.transpose(1, 2, 3, 0, 4).reshape(n, -1)
 
-    in_rows = whole_columns(jnp.concatenate([first_sum, second_sum, values_sum], axis=2), 3, channels)
-    up_rows_sum = whole_columns(up_sum, 1, hidden_own)
-
-    all_sums = jnp.stack([first_sums, second_sums, values_sums])
+
     chip_wide = [post_gain_grad, post_offset_grad, down_bias_grad, output_bias_grad]
     own_wide = [pre_gain_grad, pre_offset_grad, *trunk_grad]
-    half_wide = [up_bias_grad.reshape(-1), all_sums[:, :5]]
-    chip_flat, own_flat, half_flat = (to_rows(flatten(*group)) for group in (chip_wide, own_wide, half_wide))
-    summed = sum_chips(jnp.concatenate([chip_flat, own_flat, half_flat], axis=0))
-    n_chip, n_own = chip_flat.shape[0], own_flat.shape[0]
+    half_wide = [up_bias_grad.reshape(-1), jnp.stack([first_sums[:5], second_sums[:5], values_sums[:5]])]
+    flats = [to_rows(flatten(*group)) for group in (chip_wide, own_wide, half_wide)]
+    n_chip, n_own = flats[0].shape[0], flats[1].shape[0]
+    small = jnp.concatenate(flats, axis=0)
+    summed = sum_chips(small)
     got = swap_core(summed[n_chip:])
     own_sum = (summed[n_chip:] + got)[:n_own].reshape(-1)
     half_sum = both(summed[n_chip + n_own :], got[n_own:], core).reshape(2, -1)
     chip_sums = unflatten(summed[:n_chip].reshape(-1), [v.shape for v in chip_wide])
     own_sums = unflatten(own_sum, [v.shape for v in own_wide])
     half_sums = [unflatten(half_sum[side], [v.shape for v in half_wide]) for side in range(2)]
+    second_got, values_got = after(small, (second_got, values_got))
+    last_total = jnp.stack([second_rest + second_got.astype(f32), values_rest + values_got.astype(f32)], axis=1)
+    out_total = out_rest + after(last_total, out_got).astype(f32)
+    first_total = first_rest + after(last_total, first_got).astype(f32)
+    ends = (last_total, (out_total, first_total))
+    down_sum = reduce_far(down_total, ends)
+    up_sum = reduce_far(up_total, ends)
+    second_sum, values_sum = reduce_far(last_total, ((out_total, first_total),))
+    out_sum = reduce_far(out_total)[0]
+    first_sum = reduce_far(first_total)
+    in_rows = whole_columns(jnp.concatenate([first_sum, second_sum, values_sum], axis=2), 3, channels)
+    up_rows_sum = whole_columns(up_sum, 1, hidden_own)
     block_index = seq_index * 2 + x
 
     def own_block(value, axis=0):

time: 617 us -> 498 us (0.81)
  waiting for transfers between devices: 234 us -> 130 us
  local copies, waits for them, and re-layouts: 85.7 us -> 68.3 us
  starting transfers between devices: 108 us -> 123 us
  between operations: 16.4 us -> 3.06 us
    ppermute x16 -> x17, waiting for transfers between devices: 70.3 us -> 14.7 us  [swap_x(): return lax.ppermute(value, 'dp', [(i, i ^ 1) for i in range(count)])]
    ppermute x51 -> x50, waiting for transfers between devices: 154 us -> 105 us  [swap_seq(): return lax.ppermute(value, 'seq', [(i, i ^ mask) for i in range(count)])]
    convert_element_type x0 -> x7, other arithmetic: none -> 11.6 us  [the longest x4 6.03 us: reduce_pass(): sent = (kept[1].astype(f32) + got[1].astype(f32)).astype(bf16)]
    unnamed x225 -> x213, local copies, waits for them, and re-layouts: 27.8 us -> 18.5 us
    all_to_all x4, waiting for transfers between devices: 0.01 us -> 8.41 us  [chip_exchange(): lax.all_to_all(value, 'seq', split_axis=0, concat_axis=0, tiled=True, axi...]
    ppermute x3, waiting for transfers between devices: 10.1 us -> 2.12 us  [the longest x1 2.12 us: tiled_device(): earlier = lax.ppermute(tok[rows - HALO:], 'seq', onward)]
    concatenate x2 -> x1, local copies, waits for them, and re-layouts: 7.56 us -> 0.08 us  [flatten(): return jnp.concatenate([value.reshape(-1) for value in values])]
    ppermute x3, starting transfers between devices: 9.82 us -> 17.2 us  [the longest x1 11.9 us: tiled_device(): gfirst_next = lax.ppermute(gfirst[:HALO], 'seq', backward)]
  transfers between devices with their start and end apart: 76 -> 75, of which waited for: 36 -> 25; matrix products, arithmetic and copies ran while one was open for 21% -> 25% of each run, Pallas kernels for 10% -> 12%
where the time goes in v2:
time: 498 us; the launch traced here: 489 us
  waiting for transfers between devices  130 us (26%)
  starting transfers between devices  123 us (25%)
  Pallas kernels  86.1 us (17%)
  local copies, waits for them, and re-layouts  68.3 us (14%)
  other arithmetic  64.7 us (13%)
  matrix products  13 us (3%)
    ppermute x50, waiting for transfers between devices, swap_seq(): return lax.ppermute(value, 'seq', [(i, i ^ mask) for i in range(count)])  105 us
    ppermute x50, starting transfers between devices, swap_seq(): return lax.ppermute(value, 'seq', [(i, i ^ mask) for i in range(count)])  62.6 us
    pallas_call x11, Pallas kernels, grid_call(): pl.pallas_call(body, grid_spec=pltpu.PrefetchScalarGridSpec(num_scalar_pr...  54.7 us
    pallas_call x4, Pallas kernels, whole_call(): pl.pallas_call(body, out_shape=outs, scratch_shapes=scratch, compiler_par...  31.4 us
    all_to_all x4, starting transfers between devices, chip_exchange(): lax.all_to_all(value, 'seq', split_axis=0, concat_axis=0, tiled=True, axi...  20 us
    unnamed x213, local copies, waits for them, and re-layouts  18.5 us
    ppermute x17, waiting for transfers between devices, swap_x(): return lax.ppermute(value, 'dp', [(i, i ^ 1) for i in range(count)])  14.7 us
    ppermute x17, starting transfers between devices, swap_x(): return lax.ppermute(value, 'dp', [(i, i ^ 1) for i in range(count)])  14.4 us
  transfers between devices with their start and end apart: 75, of which 25 were waited for; matrix products, arithmetic and copies ran while one was open for 25% of the time, Pallas kernels for 12%

profile of v2, /device:TPU:9, one launch (start us, length us, event | category | flops | bytes accessed | tf_op | source)
XLA Modules:
  0.0 488.6 jit_solution(16520545806942743548)
XLA Ops:
  15.6 2.0 multiply_sine_fusion
  18.3 4.7 collective-permute-done.4
  28.0 3.4 collective-permute-start.2
  31.4 2.1 collective-permute-done.2
  37.2 3.2 collective-permute-start.16
  41.5 4.7 collective-permute-start.17
  47.8 18.0 %collective-permute-done.17 = f32[4,152,128]{2,1,0:T(8,128)S(1)} collective-permute-done((f32[4,152,128]{2,1,0:T(8,128)S(1)}, f32[4,152,128]{2,1,0:T(8,128)S(1)}, u32[]{:S(2)}, u32[]{:S(2)}) %collective-permute-start.17) | collective-permute-done | bytes 311328 | tf_op jit(solution)/shard_map/ppermute | solution.py:21
  66.0 5.5 %collective-permute-done.11 = bf16[1,64,2048]{2,1,0:T(8,128)(2,1)S(1)} collective-permute-done((bf16[1,64,2048]{2,1,0:T(8,128)(2,1)S(1)}, bf16[1,64,2048]{2,1,0:T(8,128)(2,1)S(1)}, u32[]{:S(2)}, u32[]{:S(2)}) %collective-permute-start.11) | collective-permute-done | bytes 262176 | tf_op jit(solution)/shard_map/ppermute | solution.py:21
  73.9 7.1 %collective-permute-done.18 = f32[8,152,128]{2,1,0:T(8,128)S(1)} collective-permute-done((f32[8,152,128]{2,1,0:T(8,128)S(1)}, f32[8,152,128]{2,1,0:T(8,128)S(1)}, u32[]{:S(2)}, u32[]{:S(2)}) %collective-permute-start.18) | collective-permute-done | bytes 622624 | tf_op jit(solution)/shard_map/ppermute | solution.py:21
  84.9 7.3 %collective-permute-done.12 = bf16[2,64,2048]{2,1,0:T(8,128)(2,1)} collective-permute-done((bf16[2,64,2048]{2,1,0:T(8,128)(2,1)}, bf16[2,64,2048]{2,1,0:T(8,128)(2,1)}, u32[]{:S(2)}, u32[]{:S(2)}) %collective-permute-start.12) | collective-permute-done | bytes 524320 | tf_op jit(solution)/shard_map/ppermute | solution.py:21
  102.7 3.5 fusion
  107.7 5.7 %shard_map.470 = (bf16[544,1536]{1,0:T(8,128)(2,1)}, bf16[1024,1536]{1,0:T(8,128)(2,1)}) custom-call(s32[10]{0:T(128)S(1)} %stack.244.scalars, bf16[544,1024]{1,0:T(8,128)(2,1)} %get-tuple-element.130.normed_ref, f32[1,1536]{1,0:T(1,128)S(1)} %reshape_reshape.25.bias_ref, bf16[2,4,32,1536]{3,2,1,0:T(8,128)(2,1)S(1)} %pad_maximum_fusion.12.a_ref, ...), custom_call_target="tpu_custom_call" | custom-call | flops 17112 | bytes 90 | tf_op jit(solution)/shard_map/pallas_call | solution.py:1195
  113.4 2.3 pad_maximum_fusion.8.ub_ref
  116.8 2.9 shard_map.471
  121.4 2.2 collective-permute-start.22
  125.7 9.9 %collective-permute-done.28 = bf16[2,32,1024]{2,1,0:T(8,128)(2,1)S(1)} collective-permute-done((bf16[2,32,1024]{2,1,0:T(8,128)(2,1)S(1)}, bf16[2,32,1024]{2,1,0:T(8,128)(2,1)S(1)}, u32[]{:S(2)}, u32[]{:S(2)}) %collective-permute-start.28) | collective-permute-done | bytes 131104 | tf_op jit(solution)/shard_map/ppermute | solution.py:21
  136.8 4.9 all-to-all-start
  146.3 5.3 %shard_map.472.kernel_ref = f32[256,2176]{1,0:T(8,128)S(1)} custom-call(f32[16,128,128]{2,1,0:T(8,128)S(1)} %copy-done.8, f32[128,128]{1,0:T(8,128)S(1)} %select_maximum_fusion.w_ref, f32[1,128]{1,0:T(1,128)S(1)} %maximum_bitcast_fusion.2.delta_ref, f32[17,2,128]{2,1,0:T(2,128)S(1)} %copy-done.27, f32[17,2,128,128]{3,2,1,0:T(8,128)} %constant.176.clone.turn_ref, ...), custom_call_target="tpu_custom_call" | custom-call | flops 40000000000 | bytes 8000000 | tf_op jit(solution)/shard_map/pallas_call | solution.py:459
  151.6 10.5 %collective-permute-done.23 = bf16[4,64,1024]{2,1,0:T(8,128)(2,1)S(1)} collective-permute-done((bf16[4,64,1024]{2,1,0:T(8,128)(2,1)S(1)}, bf16[4,64,1024]{2,1,0:T(8,128)(2,1)S(1)}, u32[]{:S(2)}, u32[]{:S(2)}) %collective-permute-start.23) | collective-permute-done | bytes 524320 | tf_op jit(solution)/shard_map/ppermute | solution.py:21
  167.2 8.2 %shard_map.473 = (bf16[16,128,128]{2,1,0:T(8,128)(2,1)S(1)}, f32[256,2176]{1,0:T(8,128)S(1)}) custom-call(bf16[16,128,128]{2,1,0:T(8,128)(2,1)S(1)} %bitcast.279, f32[256,2176]{1,0:T(8,128)} %copy-done.5, f32[1,128]{1,0:T(1,128)S(1)} %fusion.51.skip_ref, f32[17,2,128]{2,1,0:T(2,128)S(1)} %copy-done.27, f32[17,2,128,128]{3,2,1,0:T(8,128)} %constant.176.clone.turn_ref, ...), custom_call_target="tpu_custom_call" | custom-call | flops 20000 | bytes 100 | tf_op jit(solution)/shard_map/pallas_call | solution.py:459
  177.5 4.5 all-to-all-start.1
  183.2 8.4 %all-to-all-done.1.mixed_ref = bf16[8,2,128,128]{3,2,1,0:T(8,128)(2,1)S(1)} async-done(((bf16[8,2,128,128]{3,2,1,0:T(8,128)(2,1)}), bf16[8,2,128,128]{3,2,1,0:T(8,128)(2,1)S(1)}, u32[]{:S(2)}, u32[]{:S(2)}) %all-to-all-start.1) | async-done | bytes 524320 | tf_op jit(solution)/shard_map/all_to_all | solution.py:64
  191.6 7.7 %collective-permute-done.32.by_ref = bf16[2,4,16,1024]{3,2,1,0:T(8,128)(2,1)} collective-permute-done((bf16[2,4,16,1024]{3,2,1,0:T(8,128)(2,1)S(1)}, bf16[2,4,16,1024]{3,2,1,0:T(8,128)(2,1)}, u32[]{:S(2)}, u32[]{:S(2)}) %collective-permute-start.32) | collective-permute-done | bytes 262176 | tf_op jit(solution)/shard_map/ppermute | solution.py:21
  199.3 4.4 shard_map.474
  206.3 3.9 collective-permute-start.33
  211.2 3.2 collective-permute-done.33
  214.3 2.9 fusion.55
  218.6 22.2 %shard_map.475 = (f32[512,1024]{1,0:T(8,128)}, f32[512,1024]{1,0:T(8,128)}, bf16[2,4,128,1024]{3,2,1,0:T(8,128)(2,1)}, bf16[2,4,128,1024]{3,2,1,0:T(8,128)(2,1)}...) custom-call(s32[10]{0:T(128)S(1)} %stack.244.scalars, ...), custom_call_target="tpu_custom_call" | custom-call | flops 128849 | bytes 230 | tf_op jit(solution)/shard_map/pallas_call | solution.py:1195
  242.0 3.2 slice_bitcast_fusion.1
  248.2 2.7 multiply_reduce_fusion
  251.0 2.5 convert_reduce_fusion.1
  253.5 3.8 shard_map.476
  259.7 4.8 all-to-all-start.2
  264.7 5.5 %collective-permute-done.36 = bf16[4,128,1024]{2,1,0:T(8,128)(2,1)} collective-permute-done((bf16[4,128,1024]{2,1,0:T(8,128)(2,1)}, bf16[4,128,1024]{2,1,0:T(8,128)(2,1)}, u32[]{:S(2)}, u32[]{:S(2)}) %collective-permute-start.36) | collective-permute-done | bytes 1048608 | tf_op jit(solution)/shard_map/ppermute | solution.py:38
  270.2 4.2 collective-permute-done.37
  275.0 11.9 %collective-permute-start.38 = (bf16[16,512]{1,0:T(8,128)(2,1)}, bf16[16,512]{1,0:T(8,128)(2,1)S(1)}, u32[]{:S(2)}, u32[]{:S(2)}) collective-permute-start(bf16[16,512]{1,0:T(8,128)(2,1)} %slice.501), channel_id=1, source_target_pairs={{4,0},{6,2},{8,4},{10,6},{12,8},{14,10},{16,12},{18,14},{20,16},{2... | collective-permute-start | bytes 49160 | tf_op jit(solution)/shard_map/ppermute | solution.py:1804
  286.9 2.9 fusion.5
  291.3 2.6 fusion.6
  295.0 2.9 collective-permute-start.35
  300.5 8.3 %shard_map.477 = (bf16[8,272,128]{2,1,0:T(8,128)(2,1)S(1)}, f32[256,2176]{1,0:T(8,128)S(1)}) custom-call(bf16[16,128,128]{2,1,0:T(8,128)(2,1)S(1)} %bitcast.281, f32[256,2176]{1,0:T(8,128)} %copy-done.5, f32[1,128]{1,0:T(1,128)S(1)} %fusion.51.skip_ref, f32[17,2,128]{2,1,0:T(2,128)S(1)} %copy-done.27, f32[17,2,128,128]{3,2,1,0:T(8,128)} %constant.176.clone.turn_ref, ...), custom_call_target="tpu_custom_call" | custom-call | flops 20000 | bytes 100 | tf_op jit(solution)/shard_map/pallas_call | solution.py:459
  310.3 9.6 %shard_map.478 = (bf16[16,128,128]{2,1,0:T(8,128)(2,1)S(1)}, f32[128,128]{1,0:T(8,128)S(1)}, f32[1,128]{1,0:T(1,128)S(1)}) custom-call(bf16[16,128,128]{2,1,0:T(8,128)(2,1)S(1)} %bitcast.282, f32[256,2176]{1,0:T(8,128)} %copy-done.29, bf16[16,128,128]{2,1,0:T(8,128)(2,1)S(1)} %bitcast.280, f32[256,2176]{1,0:T(8,128)} %copy-done.28, ...), custom_call_target="tpu_custom_call" | custom-call | flops 40000000000 | bytes 10000000 | tf_op jit(solution)/shard_map/pallas_call | solution.py:459
  321.5 5.8 %all-to-all-start.3 = ((bf16[8,272,128]{2,1,0:T(8,128)(2,1)}), bf16[8,272,128]{2,1,0:T(8,128)(2,1)S(1)}, u32[]{:S(2)}, u32[]{:S(2)}) async-start(bf16[8,272,128]{2,1,0:T(8,128)(2,1)} %copy-done.13), calls=%async_computation.3 | async-start | bytes 1114112 | tf_op jit(solution)/shard_map/all_to_all | solution.py:64
  327.3 3.3 shard_map.479
  331.4 4.4 collective-permute-done.62
  335.9 3.3 fusion.10
  342.1 3.0 fusion.13
  345.1 9.2 %all-to-all-start.4 = ((bf16[16,128,128]{2,1,0:T(8,128)(2,1)}), bf16[16,128,128]{2,1,0:T(8,128)(2,1)}, u32[]{:S(2)}, u32[]{:S(2)}) async-start(bf16[16,128,128]{2,1,0:T(8,128)(2,1)} %copy-done.19), calls=%async_computation.4 | async-start | bytes 1048576 | tf_op jit(solution)/shard_map/all_to_all | solution.py:1839
  354.3 2.3 shard_map.480
  356.6 4.1 shard_map.481
  360.7 4.4 shard_map.482
  367.8 2.0 fusion.3
  371.4 2.3 fusion.4
  376.1 2.1 add_add_fusion
  384.6 2.3 constant_dynamic-slice_fusion.3
  386.9 2.7 collective-permute-done.46
  389.6 2.0 collective-permute-start.43
  397.2 3.2 slice.517
  406.2 2.9 multiply_reduce_fusion.4
  416.2 5.2 %collective-permute-done.68 = bf16[2,128,1024]{2,1,0:T(8,128)(2,1)S(1)} collective-permute-done((bf16[2,128,1024]{2,1,0:T(8,128)(2,1)}, bf16[2,128,1024]{2,1,0:T(8,128)(2,1)S(1)}, u32[]{:S(2)}, u32[]{:S(2)}) %collective-permute-start.68) | collective-permute-done | bytes 524320 | tf_op jit(solution)/shard_map/ppermute | solution.py:21
  429.3 2.0 collective-permute-done.63
  435.2 11.9 %collective-permute-done.64 = bf16[1,1,32,1024]{3,2,0,1:T(8,128)(2,1)S(1)} collective-permute-done((bf16[1,1,32,1024]{3,2,0,1:T(8,128)(2,1)S(1)}, bf16[1,1,32,1024]{3,2,0,1:T(8,128)(2,1)S(1)}, u32[]{:S(2)}, u32[]{:S(2)}) %collective-permute-start.64) | collective-permute-done | bytes 65568 | tf_op jit(solution)/shard_map/ppermute | solution.py:21
  447.0 4.7 collective-permute-start.57
  452.4 2.9 collective-permute-done.57
  457.9 8.4 %collective-permute-start.67 = (f32[32,2048]{1,0:T(8,128)S(1)}, f32[32,2048]{1,0:T(8,128)S(1)}, u32[]{:S(2)}, u32[]{:S(2)}) collective-permute-start(f32[32,2048]{1,0:T(8,128)S(1)} %get-tuple-element.268), channel_id=1, source_target_pairs={{0,2},{2,0},{4,6},{6,4},{8,10},{10,8},{12,14},{14,12},{16,18},{18,... | collective-permute-start | bytes 786440 | tf_op jit(solution)/shard_map/ppermute | solution.py:21
  (556 shorter events, 155.5 us)
Async XLA Ops:
  3.1 8.9 %collective-permute-start = (bf16[64,1536]{1,0:T(8,128)(2,1)S(1)}, bf16[64,1536]{1,0:T(8,128)(2,1)S(1)}, u32[]{:S(2)}, u32[]{:S(2)}) collective-permute-start(bf16[64,1536]{1,0:T(8,128)(2,1)S(1)} %get-tuple-element.120), channel_id=1, source_target_pairs={{0,2},{2,0},{4,6},{6,4},{8,10},{10,8},{12,14},{14,12},{16,18},{18,... | collective-permute-start | bytes 589832 | tf_op jit(solution)/shard_map/ppermute | solution.py:21
  12.1 10.8 %collective-permute-start.4 = (bf16[1,64,1536]{2,1,0:T(8,128)(2,1)S(1)}, bf16[1,64,1536]{2,1,0:T(8,128)(2,1)}, u32[]{:S(2)}, u32[]{:S(2)}) collective-permute-start(bf16[1,64,1536]{2,1,0:T(8,128)(2,1)S(1)} %bitcast.318), channel_id=1, source_target_pairs={{0,24},{2,26},{4,28},{6,30},{8,16},{10,18},{12,20},{14,22},{16,8},... | collective-permute-start | bytes 589832 | tf_op jit(solution)/shard_map/ppermute | solution.py:21
  13.6 10.4 %collective-permute-start.1 = (bf16[2,256,1024]{2,1,0:T(8,128)(2,1)S(1)}, bf16[2,256,1024]{2,1,0:T(8,128)(2,1)}, u32[]{:S(2)}, u32[]{:S(2)}) collective-permute-start(bf16[2,256,1024]{2,1,0:T(8,128)(2,1)S(1)} %constant_dynamic-update-slice_fusion), channel_id=1, source_target_pairs={{0,2},{2,0},{4,6},{6,4},{8,10},{10,8},{12,14},{14,12},{16,18},{18,... | collective-permute-start | bytes 3145736 | tf_op jit(solution)/shard_map/ppermute | solution.py:21
  18.0 13.3 %collective-permute-start.10 = (bf16[64,2048]{1,0:T(8,128)(2,1)S(1)}, bf16[64,2048]{1,0:T(8,128)(2,1)S(1)}, u32[]{:S(2)}, u32[]{:S(2)}) collective-permute-start(bf16[64,2048]{1,0:T(8,128)(2,1)S(1)} %get-tuple-element.125), channel_id=1, source_target_pairs={{0,2},{2,0},{4,6},{6,4},{8,10},{10,8},{12,14},{14,12},{16,18},{18,... | collective-permute-start | bytes 786440 | tf_op jit(solution)/shard_map/ppermute | solution.py:21
  33.5 12.6 %collective-permute-start.5 = (bf16[2,64,1536]{2,1,0:T(8,128)(2,1)S(1)}, bf16[2,64,1536]{2,1,0:T(8,128)(2,1)S(1)}, u32[]{:S(2)}, u32[]{:S(2)}) collective-permute-start(bf16[2,64,1536]{2,1,0:T(8,128)(2,1)S(1)} %pad_maximum_fusion.18), channel_id=1, source_target_pairs={{0,8},{2,10},{4,12},{6,14},{8,0},{10,2},{12,4},{14,6},{16,24},{18,... | collective-permute-start | bytes 1179656 | tf_op jit(solution)/shard_map/ppermute | solution.py:21
  41.5 24.4 %collective-permute-start.17 = (f32[4,152,128]{2,1,0:T(8,128)S(1)}, f32[4,152,128]{2,1,0:T(8,128)S(1)}, u32[]{:S(2)}, u32[]{:S(2)}) collective-permute-start(f32[4,152,128]{2,1,0:T(8,128)S(1)} %pad_maximum_fusion.20), channel_id=1, source_target_pairs={{0,24},{2,26},{4,28},{6,30},{8,16},{10,18},{12,20},{14,22},{16,8},... | collective-permute-start | bytes 933896 | tf_op jit(solution)/shard_map/ppermute | solution.py:21
  46.4 25.1 %collective-permute-start.11 = (bf16[1,64,2048]{2,1,0:T(8,128)(2,1)S(1)}, bf16[1,64,2048]{2,1,0:T(8,128)(2,1)S(1)}, u32[]{:S(2)}, u32[]{:S(2)}) collective-permute-start(bf16[1,64,2048]{2,1,0:T(8,128)(2,1)S(1)} %bitcast.306), channel_id=1, source_target_pairs={{0,24},{2,26},{4,28},{6,30},{8,16},{10,18},{12,20},{14,22},{16,8},... | collective-permute-start | bytes 786440 | tf_op jit(solution)/shard_map/ppermute | solution.py:21
  46.5 25.9 %collective-permute-start.6 = (bf16[4,32,1536]{2,1,0:T(8,128)(2,1)S(1)}, bf16[4,32,1536]{2,1,0:T(8,128)(2,1)S(1)}, u32[]{:S(2)}, u32[]{:S(2)}) collective-permute-start(bf16[4,32,1536]{2,1,0:T(8,128)(2,1)S(1)} %get-tuple-element.266), channel_id=1, source_target_pairs={{0,4},{2,6},{4,0},{6,2},{8,12},{10,14},{12,8},{14,10},{16,20},{18,... | collective-permute-start | bytes 1179656 | tf_op jit(solution)/shard_map/ppermute | solution.py:21
  46.5 27.2 %collective-permute-start.8 = (bf16[4,32,1536]{2,1,0:T(8,128)(2,1)S(1)}, bf16[4,32,1536]{2,1,0:T(8,128)(2,1)S(1)}, u32[]{:S(2)}, u32[]{:S(2)}) collective-permute-start(bf16[4,32,1536]{2,1,0:T(8,128)(2,1)S(1)} %get-tuple-element.265), channel_id=1, source_target_pairs={{0,1},{1,0},{2,3},{3,2},{4,5},{5,4},{6,7},{7,6},{8,9},{9,8},{10,11... | collective-permute-start | bytes 1179656 | tf_op jit(solution)/shard_map/ppermute | solution.py:38
  65.9 15.1 %collective-permute-start.18 = (f32[8,152,128]{2,1,0:T(8,128)S(1)}, f32[8,152,128]{2,1,0:T(8,128)S(1)}, u32[]{:S(2)}, u32[]{:S(2)}) collective-permute-start(f32[8,152,128]{2,1,0:T(8,128)S(1)} %pad_maximum_fusion.14), channel_id=1, source_target_pairs={{0,8},{2,10},{4,12},{6,14},{8,0},{10,2},{12,4},{14,6},{16,24},{18,... | collective-permute-start | bytes 1867784 | tf_op jit(solution)/shard_map/ppermute | solution.py:21
  72.3 19.9 %collective-permute-start.12 = (bf16[2,64,2048]{2,1,0:T(8,128)(2,1)}, bf16[2,64,2048]{2,1,0:T(8,128)(2,1)}, u32[]{:S(2)}, u32[]{:S(2)}) collective-permute-start(bf16[2,64,2048]{2,1,0:T(8,128)(2,1)} %pad_maximum_fusion.16), channel_id=1, source_target_pairs={{0,8},{2,10},{4,12},{6,14},{8,0},{10,2},{12,4},{14,6},{16,24},{18,... | collective-permute-start | bytes 1572872 | tf_op jit(solution)/shard_map/ppermute | solution.py:21
  72.4 21.1 %collective-permute-start.7 = (bf16[2,4,32,1536]{3,2,1,0:T(8,128)(2,1)S(1)}, bf16[2,4,32,1536]{3,2,1,0:T(8,128)(2,1)S(1)}, u32[]{:S(2)}, u32[]{:S(2)}) collective-permute-start(bf16[2,4,32,1536]{3,2,1,0:T(8,128)(2,1)S(1)} %pad_maximum_fusion.12.a_ref), channel_id=1, source_target_pairs={{0,1},{1,0},{2,3},{3,2},{4,5},{5,4},{6,7},{7,6},{8,9},{9,8},{10,11... | collective-permute-start | bytes 2359304 | tf_op jit(solution)/shard_map/ppermute | solution.py:38
  73.8 19.7 %collective-permute-start.9 = (bf16[2,4,32,1536]{3,2,1,0:T(8,128)(2,1)S(1)}, bf16[2,4,32,1536]{3,2,1,0:T(8,128)(2,1)}, u32[]{:S(2)}, u32[]{:S(2)}) collective-permute-start(bf16[2,4,32,1536]{3,2,1,0:T(8,128)(2,1)S(1)} %pad_maximum_fusion.13.b_ref), channel_id=1, source_target_pairs={{0,4},{2,6},{4,0},{6,2},{8,12},{10,14},{12,8},{14,10},{16,20},{18,... | collective-permute-start | bytes 2359304 | tf_op jit(solution)/shard_map/ppermute | solution.py:21
  95.1 18.3 %collective-permute-start.14 = (bf16[4,32,2048]{2,1,0:T(8,128)(2,1)}, bf16[4,32,2048]{2,1,0:T(8,128)(2,1)}, u32[]{:S(2)}, u32[]{:S(2)}) collective-permute-start(bf16[4,32,2048]{2,1,0:T(8,128)(2,1)} %get-tuple-element.259), channel_id=1, source_target_pairs={{0,1},{1,0},{2,3},{3,2},{4,5},{5,4},{6,7},{7,6},{8,9},{9,8},{10,11... | collective-permute-start | bytes 1572872 | tf_op jit(solution)/shard_map/ppermute | solution.py:38
  102.6 13.2 %collective-permute-start.13 = (bf16[4,32,2048]{2,1,0:T(8,128)(2,1)}, bf16[4,32,2048]{2,1,0:T(8,128)(2,1)S(1)}, u32[]{:S(2)}, u32[]{:S(2)}) collective-permute-start(bf16[4,32,2048]{2,1,0:T(8,128)(2,1)} %get-tuple-element.260), channel_id=1, source_target_pairs={{0,4},{2,6},{4,0},{6,2},{8,12},{10,14},{12,8},{14,10},{16,20},{18,... | collective-permute-start | bytes 1572872 | tf_op jit(solution)/shard_map/ppermute | solution.py:21
  106.2 18.1 %collective-permute-start.27 = (bf16[1,32,1024]{2,1,0:T(8,128)(2,1)S(1)}, bf16[1,32,1024]{2,1,0:T(8,128)(2,1)S(1)}, u32[]{:S(2)}, u32[]{:S(2)}) collective-permute-start(bf16[1,32,1024]{2,1,0:T(8,128)(2,1)S(1)} %bitcast.320), channel_id=1, source_target_pairs={{0,24},{2,26},{4,28},{6,30},{8,16},{10,18},{12,20},{14,22},{16,8},... | collective-permute-start | bytes 196616 | tf_op jit(solution)/shard_map/ppermute | solution.py:21
  106.9 14.5 %collective-permute-start.21 = (bf16[1,128,1024]{2,1,0:T(8,128)(2,1)S(1)}, bf16[1,128,1024]{2,1,0:T(8,128)(2,1)S(1)}, u32[]{:S(2)}, u32[]{:S(2)}) collective-permute-start(bf16[1,128,1024]{2,1,0:T(8,128)(2,1)S(1)} %bitcast.303), channel_id=1, source_target_pairs={{0,24},{2,26},{4,28},{6,30},{8,16},{10,18},{12,20},{14,22},{16,8},... | collective-permute-start | bytes 786440 | tf_op jit(solution)/shard_map/ppermute | solution.py:21
  119.7 24.7 %collective-permute-start.19 = (bf16[2,4,32,2048]{3,2,1,0:T(8,128)(2,1)}, bf16[2,4,32,2048]{3,2,1,0:T(8,128)(2,1)}, u32[]{:S(2)}, u32[]{:S(2)}) collective-permute-start(bf16[2,4,32,2048]{3,2,1,0:T(8,128)(2,1)} %pad_maximum_fusion.7.ua_ref), channel_id=1, source_target_pairs={{0,1},{1,0},{2,3},{3,2},{4,5},{5,4},{6,7},{7,6},{8,9},{9,8},{10,11... | collective-permute-start | bytes 3145736 | tf_op jit(solution)/shard_map/ppermute | solution.py:38
  120.0 24.4 %collective-permute-start.20 = (bf16[2,4,32,2048]{3,2,1,0:T(8,128)(2,1)}, bf16[2,4,32,2048]{3,2,1,0:T(8,128)(2,1)}, u32[]{:S(2)}, u32[]{:S(2)}) collective-permute-start(bf16[2,4,32,2048]{3,2,1,0:T(8,128)(2,1)} %pad_maximum_fusion.8.ub_ref), channel_id=1, source_target_pairs={{0,4},{2,6},{4,0},{6,2},{8,12},{10,14},{12,8},{14,10},{16,20},{18,... | collective-permute-start | bytes 3145736 | tf_op jit(solution)/shard_map/ppermute | solution.py:21
  121.4 14.3 %collective-permute-start.22 = (bf16[2,128,1024]{2,1,0:T(8,128)(2,1)S(1)}, bf16[2,128,1024]{2,1,0:T(8,128)(2,1)S(1)}, u32[]{:S(2)}, u32[]{:S(2)}) collective-permute-start(bf16[2,128,1024]{2,1,0:T(8,128)(2,1)S(1)} %pad_maximum_fusion.17), channel_id=1, source_target_pairs={{0,8},{2,10},{4,12},{6,14},{8,0},{10,2},{12,4},{14,6},{16,24},{18,... | collective-permute-start | bytes 1572872 | tf_op jit(solution)/shard_map/ppermute | solution.py:21
  124.4 11.3 %collective-permute-start.28 = (bf16[2,32,1024]{2,1,0:T(8,128)(2,1)S(1)}, bf16[2,32,1024]{2,1,0:T(8,128)(2,1)S(1)}, u32[]{:S(2)}, u32[]{:S(2)}) collective-permute-start(bf16[2,32,1024]{2,1,0:T(8,128)(2,1)S(1)} %pad_maximum_fusion.25), channel_id=1, source_target_pairs={{0,8},{2,10},{4,12},{6,14},{8,0},{10,2},{12,4},{14,6},{16,24},{18,... | collective-permute-start | bytes 393224 | tf_op jit(solution)/shard_map/ppermute | solution.py:21
  136.8 30.4 %all-to-all-start = ((bf16[8,2,128,128]{3,2,1,0:T(8,128)(2,1)}), bf16[8,2,128,128]{3,2,1,0:T(8,128)(2,1)S(1)}, u32[]{:S(2)}, u32[]{:S(2)}) async-start(bf16[8,2,128,128]{3,2,1,0:T(8,128)(2,1)} %shard_map.471), calls=%async_computation | async-start | bytes 1048576 | tf_op jit(solution)/shard_map/all_to_all | solution.py:64
  141.7 25.3 %collective-permute-start.30 = (bf16[4,16,1024]{2,1,0:T(8,128)(2,1)S(1)}, bf16[4,16,1024]{2,1,0:T(8,128)(2,1)S(1)}, u32[]{:S(2)}, u32[]{:S(2)}) collective-permute-start(bf16[4,16,1024]{2,1,0:T(8,128)(2,1)S(1)} %get-tuple-element.273), channel_id=1, source_target_pairs={{0,1},{1,0},{2,3},{3,2},{4,5},{5,4},{6,7},{7,6},{8,9},{9,8},{10,11... | collective-permute-start | bytes 393224 | tf_op jit(solution)/shard_map/ppermute | solution.py:38
  143.2 23.9 %collective-permute-start.29 = (bf16[4,16,1024]{2,1,0:T(8,128)(2,1)S(1)}, bf16[4,16,1024]{2,1,0:T(8,128)(2,1)S(1)}, u32[]{:S(2)}, u32[]{:S(2)}) collective-permute-start(bf16[4,16,1024]{2,1,0:T(8,128)(2,1)S(1)} %get-tuple-element.274), channel_id=1, source_target_pairs={{0,4},{2,6},{4,0},{6,2},{8,12},{10,14},{12,8},{14,10},{16,20},{18,... | collective-permute-start | bytes 393224 | tf_op jit(solution)/shard_map/ppermute | solution.py:21
  145.8 19.2 %collective-permute-start.25 = (bf16[4,64,1024]{2,1,0:T(8,128)(2,1)S(1)}, bf16[4,64,1024]{2,1,0:T(8,128)(2,1)S(1)}, u32[]{:S(2)}, u32[]{:S(2)}) collective-permute-start(bf16[4,64,1024]{2,1,0:T(8,128)(2,1)S(1)} %get-tuple-element.255), channel_id=1, source_target_pairs={{0,1},{1,0},{2,3},{3,2},{4,5},{5,4},{6,7},{7,6},{8,9},{9,8},{10,11... | collective-permute-start | bytes 1572872 | tf_op jit(solution)/shard_map/ppermute | solution.py:38
  146.0 16.1 %collective-permute-start.23 = (bf16[4,64,1024]{2,1,0:T(8,128)(2,1)S(1)}, bf16[4,64,1024]{2,1,0:T(8,128)(2,1)S(1)}, u32[]{:S(2)}, u32[]{:S(2)}) collective-permute-start(bf16[4,64,1024]{2,1,0:T(8,128)(2,1)S(1)} %get-tuple-element.256), channel_id=1, source_target_pairs={{0,4},{2,6},{4,0},{6,2},{8,12},{10,14},{12,8},{14,10},{16,20},{18,... | collective-permute-start | bytes 1572872 | tf_op jit(solution)/shard_map/ppermute | solution.py:21
  163.1 28.4 %collective-permute-start.24 = (bf16[2,4,64,1024]{3,2,1,0:T(8,128)(2,1)}, bf16[2,4,64,1024]{3,2,1,0:T(8,128)(2,1)}, u32[]{:S(2)}, u32[]{:S(2)}) collective-permute-start(bf16[2,4,64,1024]{3,2,1,0:T(8,128)(2,1)} %pad_maximum_fusion.10.da_ref), channel_id=1, source_target_pairs={{0,1},{1,0},{2,3},{3,2},{4,5},{5,4},{6,7},{7,6},{8,9},{9,8},{10,11... | collective-permute-start | bytes 3145736 | tf_op jit(solution)/shard_map/ppermute | solution.py:38
  166.1 25.5 %collective-permute-start.26 = (bf16[2,4,64,1024]{3,2,1,0:T(8,128)(2,1)}, bf16[2,4,64,1024]{3,2,1,0:T(8,128)(2,1)}, u32[]{:S(2)}, u32[]{:S(2)}) collective-permute-start(bf16[2,4,64,1024]{3,2,1,0:T(8,128)(2,1)} %pad_maximum_fusion.11.db_ref), channel_id=1, source_target_pairs={{0,4},{2,6},{4,0},{6,2},{8,12},{10,14},{12,8},{14,10},{16,20},{18,... | collective-permute-start | bytes 3145736 | tf_op jit(solution)/shard_map/ppermute | solution.py:21
  177.5 14.1 %all-to-all-start.1 = ((bf16[8,2,128,128]{3,2,1,0:T(8,128)(2,1)}), bf16[8,2,128,128]{3,2,1,0:T(8,128)(2,1)S(1)}, u32[]{:S(2)}, u32[]{:S(2)}) async-start(bf16[8,2,128,128]{3,2,1,0:T(8,128)(2,1)} %bitcast.284), calls=%async_computation.1 | async-start | bytes 1048576 | tf_op jit(solution)/shard_map/all_to_all | solution.py:64
  182.0 9.6 %collective-permute-start.31 = (bf16[2,4,16,1024]{3,2,1,0:T(8,128)(2,1)S(1)}, bf16[2,4,16,1024]{3,2,1,0:T(8,128)(2,1)}, u32[]{:S(2)}, u32[]{:S(2)}) collective-permute-start(bf16[2,4,16,1024]{3,2,1,0:T(8,128)(2,1)S(1)} %pad_maximum_fusion.22.a_ref), channel_id=1, source_target_pairs={{0,1},{1,0},{2,3},{3,2},{4,5},{5,4},{6,7},{7,6},{8,9},{9,8},{10,11... | collective-permute-start | bytes 786440 | tf_op jit(solution)/shard_map/ppermute | solution.py:38
  182.0 17.3 %collective-permute-start.32 = (bf16[2,4,16,1024]{3,2,1,0:T(8,128)(2,1)S(1)}, bf16[2,4,16,1024]{3,2,1,0:T(8,128)(2,1)}, u32[]{:S(2)}, u32[]{:S(2)}) collective-permute-start(bf16[2,4,16,1024]{3,2,1,0:T(8,128)(2,1)S(1)} %pad_maximum_fusion.23.b_ref), channel_id=1, source_target_pairs={{0,4},{2,6},{4,0},{6,2},{8,12},{10,14},{12,8},{14,10},{16,20},{18,... | collective-permute-start | bytes 786440 | tf_op jit(solution)/shard_map/ppermute | solution.py:21
  245.2 24.9 %collective-permute-start.36 = (bf16[4,128,1024]{2,1,0:T(8,128)(2,1)}, bf16[4,128,1024]{2,1,0:T(8,128)(2,1)}, u32[]{:S(2)}, u32[]{:S(2)}) collective-permute-start(bf16[4,128,1024]{2,1,0:T(8,128)(2,1)} %get-tuple-element.238), channel_id=1, source_target_pairs={{0,1},{1,0},{2,3},{3,2},{4,5},{5,4},{6,7},{7,6},{8,9},{9,8},{10,11... | collective-permute-start | bytes 3145736 | tf_op jit(solution)/shard_map/ppermute | solution.py:38
  246.9 27.5 %collective-permute-start.37 = (bf16[4,2,32,2048]{3,2,1,0:T(8,128)(2,1)}, bf16[4,2,32,2048]{3,2,1,0:T(8,128)(2,1)}, u32[]{:S(2)}, u32[]{:S(2)}) collective-permute-start(bf16[4,2,32,2048]{3,2,1,0:T(8,128)(2,1)} %get-tuple-element.236), channel_id=1, source_target_pairs={{0,4},{2,6},{4,0},{6,2},{8,12},{10,14},{12,8},{14,10},{16,20},{18,... | collective-permute-start | bytes 3145736 | tf_op jit(solution)/shard_map/ppermute | solution.py:21
  259.7 40.8 %all-to-all-start.2 = ((bf16[8,2,128,128]{3,2,1,0:T(8,128)(2,1)}), bf16[8,2,128,128]{3,2,1,0:T(8,128)(2,1)S(1)}, u32[]{:S(2)}, u32[]{:S(2)}) async-start(bf16[8,2,128,128]{3,2,1,0:T(8,128)(2,1)} %copy-done.20), calls=%async_computation.2 | async-start | bytes 1048576 | tf_op jit(solution)/shard_map/all_to_all | solution.py:64
  275.0 45.0 %collective-permute-start.38 = (bf16[16,512]{1,0:T(8,128)(2,1)}, bf16[16,512]{1,0:T(8,128)(2,1)S(1)}, u32[]{:S(2)}, u32[]{:S(2)}) collective-permute-start(bf16[16,512]{1,0:T(8,128)(2,1)} %slice.501), channel_id=1, source_target_pairs={{4,0},{6,2},{8,4},{10,6},{12,8},{14,10},{16,12},{18,14},{20,16},{2... | collective-permute-start | bytes 49160 | tf_op jit(solution)/shard_map/ppermute | solution.py:1804
  289.9 76.7 %collective-permute-start.42 = (bf16[4,2,32,2048]{3,2,1,0:T(8,128)(2,1)}, bf16[4,2,32,2048]{3,2,1,0:T(8,128)(2,1)}, u32[]{:S(2)}, u32[]{:S(2)}) collective-permute-start(bf16[4,2,32,2048]{3,2,1,0:T(8,128)(2,1)} %fusion.5), channel_id=1, source_target_pairs={{0,1},{1,0},{2,3},{3,2},{4,5},{5,4},{6,7},{7,6},{8,9},{9,8},{10,11... | collective-permute-start | bytes 3145736 | tf_op jit(solution)/shard_map/ppermute | solution.py:38
  293.9 73.8 %collective-permute-start.40 = (bf16[4,128,1024]{2,1,0:T(8,128)(2,1)}, bf16[4,128,1024]{2,1,0:T(8,128)(2,1)}, u32[]{:S(2)}, u32[]{:S(2)}) collective-permute-start(bf16[4,128,1024]{2,1,0:T(8,128)(2,1)} %fusion.6), channel_id=1, source_target_pairs={{0,4},{2,6},{4,0},{6,2},{8,12},{10,14},{12,8},{14,10},{16,20},{18,... | collective-permute-start | bytes 3145736 | tf_op jit(solution)/shard_map/ppermute | solution.py:21
  295.0 45.5 %collective-permute-start.35 = (f32[256,1024]{1,0:T(8,128)}, f32[256,1024]{1,0:T(8,128)}, u32[]{:S(2)}, u32[]{:S(2)}) collective-permute-start(f32[256,1024]{1,0:T(8,128)} %constant_dynamic-slice_fusion.4), channel_id=1, source_target_pairs={{0,2},{2,0},{4,6},{6,4},{8,10},{10,8},{12,14},{14,12},{16,18},{18,... | collective-permute-start | bytes 3145736 | tf_op jit(solution)/shard_map/ppermute | solution.py:21
  298.0 67.1 %collective-permute-start.39 = (bf16[4,128,1024]{2,1,0:T(8,128)(2,1)}, bf16[4,128,1024]{2,1,0:T(8,128)(2,1)}, u32[]{:S(2)}, u32[]{:S(2)}) collective-permute-start(bf16[4,128,1024]{2,1,0:T(8,128)(2,1)} %get-tuple-element.176), channel_id=1, source_target_pairs={{0,1},{1,0},{2,3},{3,2},{4,5},{5,4},{6,7},{7,6},{8,9},{9,8},{10,11... | collective-permute-start | bytes 3145736 | tf_op jit(solution)/shard_map/ppermute | solution.py:38
  320.1 15.8 %collective-permute-start.62 = (f32[65,64]{1,0:T(8,128)S(1)}, f32[65,64]{1,0:T(8,128)S(1)}, u32[]{:S(2)}, u32[]{:S(2)}) collective-permute-start(f32[65,64]{1,0:T(8,128)S(1)} %pad_maximum_fusion.29), channel_id=1, source_target_pairs={{0,1},{1,0},{2,3},{3,2},{4,5},{5,4},{6,7},{7,6},{8,9},{9,8},{10,11... | collective-permute-start | bytes 49928 | tf_op jit(solution)/shard_map/ppermute | solution.py:38
  321.5 23.6 %all-to-all-start.3 = ((bf16[8,272,128]{2,1,0:T(8,128)(2,1)}), bf16[8,272,128]{2,1,0:T(8,128)(2,1)S(1)}, u32[]{:S(2)}, u32[]{:S(2)}) async-start(bf16[8,272,128]{2,1,0:T(8,128)(2,1)} %copy-done.13), calls=%async_computation.3 | async-start | bytes 1114112 | tf_op jit(solution)/shard_map/all_to_all | solution.py:64
  335.9 30.1 %collective-permute-start.41 = (bf16[4,2,32,2048]{3,2,1,0:T(8,128)(2,1)}, bf16[4,2,32,2048]{3,2,1,0:T(8,128)(2,1)}, u32[]{:S(2)}, u32[]{:S(2)}) collective-permute-start(bf16[4,2,32,2048]{3,2,1,0:T(8,128)(2,1)} %get-tuple-element.177), channel_id=1, source_target_pairs={{0,4},{2,6},{4,0},{6,2},{8,12},{10,14},{12,8},{14,10},{16,20},{18,... | collective-permute-start | bytes 3145736 | tf_op jit(solution)/shard_map/ppermute | solution.py:21
  340.6 40.2 %collective-permute-start.44 = (bf16[2,4,1,32,1024]{4,3,2,1,0:T(8,128)(2,1)}, bf16[2,4,1,32,1024]{4,3,2,1,0:T(8,128)(2,1)}, u32[]{:S(2)}, u32[]{:S(2)}) collective-permute-start(bf16[2,4,1,32,1024]{4,3,2,1,0:T(8,128)(2,1)} %copy-done.30), channel_id=1, source_target_pairs={{0,4},{2,6},{4,0},{6,2},{8,12},{10,14},{12,8},{14,10},{16,20},{18,... | collective-permute-start | bytes 1572872 | tf_op jit(solution)/shard_map/ppermute | solution.py:21
  345.1 50.8 %all-to-all-start.4 = ((bf16[16,128,128]{2,1,0:T(8,128)(2,1)}), bf16[16,128,128]{2,1,0:T(8,128)(2,1)}, u32[]{:S(2)}, u32[]{:S(2)}) async-start(bf16[16,128,128]{2,1,0:T(8,128)(2,1)} %copy-done.19), calls=%async_computation.4 | async-start | bytes 1048576 | tf_op jit(solution)/shard_map/all_to_all | solution.py:1839
  365.1 13.3 %collective-permute-start.45 = (bf16[2,4,2,32,512]{4,3,2,1,0:T(8,128)(2,1)S(1)}, bf16[2,4,2,32,512]{4,3,2,1,0:T(8,128)(2,1)S(1)}, u32[]{:S(2)}, u32[]{:S(2)}) collective-permute-start(bf16[2,4,2,32,512]{4,3,2,1,0:T(8,128)(2,1)S(1)} %copy-done.32), channel_id=1, source_target_pairs={{0,1},{1,0},{2,3},{3,2},{4,5},{5,4},{6,7},{7,6},{8,9},{9,8},{10,11... | collective-permute-start | bytes 1572872 | tf_op jit(solution)/shard_map/ppermute | solution.py:38
  366.0 23.6 %collective-permute-start.46 = (bf16[2,4,2,32,512]{4,3,2,1,0:T(8,128)(2,1)}, bf16[2,4,2,32,512]{4,3,2,1,0:T(8,128)(2,1)}, u32[]{:S(2)}, u32[]{:S(2)}) collective-permute-start(bf16[2,4,2,32,512]{4,3,2,1,0:T(8,128)(2,1)} %get-tuple-element.173), channel_id=1, source_target_pairs={{0,1},{1,0},{2,3},{3,2},{4,5},{5,4},{6,7},{7,6},{8,9},{9,8},{10,11... | collective-permute-start | bytes 1572872 | tf_op jit(solution)/shard_map/ppermute | solution.py:38
  366.6 25.0 %collective-permute-start.47 = (bf16[2,4,2,32,512]{4,3,2,1,0:T(8,128)(2,1)}, bf16[2,4,2,32,512]{4,3,2,1,0:T(8,128)(2,1)}, u32[]{:S(2)}, u32[]{:S(2)}) collective-permute-start(bf16[2,4,2,32,512]{4,3,2,1,0:T(8,128)(2,1)} %get-tuple-element.175), channel_id=1, source_target_pairs={{0,4},{2,6},{4,0},{6,2},{8,12},{10,14},{12,8},{14,10},{16,20},{18,... | collective-permute-start | bytes 1572872 | tf_op jit(solution)/shard_map/ppermute | solution.py:21
  373.7 41.3 %collective-permute-start.65 = (bf16[2,2,32,2048]{3,2,1,0:T(8,128)(2,1)}, bf16[2,2,32,2048]{3,2,1,0:T(8,128)(2,1)}, u32[]{:S(2)}, u32[]{:S(2)}) collective-permute-start(bf16[2,2,32,2048]{3,2,1,0:T(8,128)(2,1)} %slice.785), channel_id=1, source_target_pairs={{0,8},{2,10},{4,12},{6,14},{8,0},{10,2},{12,4},{14,6},{16,24},{18,... | collective-permute-start | bytes 1572872 | tf_op jit(solution)/shard_map/ppermute | solution.py:21
  380.8 43.1 %collective-permute-start.55 = (bf16[4,2,32,512]{3,2,1,0:T(8,128)(2,1)}, bf16[4,2,32,512]{3,2,1,0:T(8,128)(2,1)}, u32[]{:S(2)}, u32[]{:S(2)}) collective-permute-start(bf16[4,2,32,512]{3,2,1,0:T(8,128)(2,1)} %fusion.24), channel_id=1, source_target_pairs={{0,4},{2,6},{4,0},{6,2},{8,12},{10,14},{12,8},{14,10},{16,20},{18,... | collective-permute-start | bytes 786440 | tf_op jit(solution)/shard_map/ppermute | solution.py:21
  383.7 38.6 %collective-permute-start.58 = (bf16[4,1,32,1024]{3,2,0,1:T(8,128)(2,1)}, bf16[4,1,32,1024]{3,2,0,1:T(8,128)(2,1)}, u32[]{:S(2)}, u32[]{:S(2)}) collective-permute-start(bf16[4,1,32,1024]{3,2,0,1:T(8,128)(2,1)} %fusion.23), channel_id=1, source_target_pairs={{0,1},{1,0},{2,3},{3,2},{4,5},{5,4},{6,7},{7,6},{8,9},{9,8},{10,11... | collective-permute-start | bytes 786440 | tf_op jit(solution)/shard_map/ppermute | solution.py:38
  389.6 15.4 %collective-permute-start.43 = (f32[256,1024]{1,0:T(8,128)}, f32[256,1024]{1,0:T(8,128)S(1)}, u32[]{:S(2)}, u32[]{:S(2)}) collective-permute-start(f32[256,1024]{1,0:T(8,128)} %constant_dynamic-slice_fusion.3), channel_id=1, source_target_pairs={{0,2},{2,0},{4,6},{6,4},{8,10},{10,8},{12,14},{14,12},{16,18},{18,... | collective-permute-start | bytes 3145736 | tf_op jit(solution)/shard_map/ppermute | solution.py:21
  393.3 15.9 %collective-permute-start.54 = (bf16[4,2,32,512]{3,2,1,0:T(8,128)(2,1)}, bf16[4,2,32,512]{3,2,1,0:T(8,128)(2,1)}, u32[]{:S(2)}, u32[]{:S(2)}) collective-permute-start(bf16[4,2,32,512]{3,2,1,0:T(8,128)(2,1)} %fusion.26), channel_id=1, source_target_pairs={{0,1},{1,0},{2,3},{3,2},{4,5},{5,4},{6,7},{7,6},{8,9},{9,8},{10,11... | collective-permute-start | bytes 786440 | tf_op jit(solution)/shard_map/ppermute | solution.py:38
  409.2 12.2 %collective-permute-start.68 = (bf16[2,128,1024]{2,1,0:T(8,128)(2,1)}, bf16[2,128,1024]{2,1,0:T(8,128)(2,1)S(1)}, u32[]{:S(2)}, u32[]{:S(2)}) collective-permute-start(bf16[2,128,1024]{2,1,0:T(8,128)(2,1)} %slice.784), channel_id=1, source_target_pairs={{0,8},{2,10},{4,12},{6,14},{8,0},{10,2},{12,4},{14,6},{16,24},{18,... | collective-permute-start | bytes 1572872 | tf_op jit(solution)/shard_map/ppermute | solution.py:21
  410.9 18.3 %collective-permute-start.48 = (f32[216,128]{1,0:T(8,128)S(1)}, f32[216,128]{1,0:T(8,128)S(1)}, u32[]{:S(2)}, u32[]{:S(2)}) collective-permute-start(f32[216,128]{1,0:T(8,128)S(1)} %constant_dynamic-update-slice_fusion.6), channel_id=1, source_target_pairs={{0,24},{2,26},{4,28},{6,30},{8,16},{10,18},{12,20},{14,22},{16,8},... | collective-permute-start | bytes 331784 | tf_op jit(solution)/shard_map/ppermute | solution.py:21
  421.6 34.1 %collective-permute-start.59 = (bf16[2,2,2,32,512]{4,3,2,0,1:T(8,128)(2,1)S(1)}, bf16[2,2,2,32,512]{4,3,2,0,1:T(8,128)(2,1)S(1)}, u32[]{:S(2)}, u32[]{:S(2)}) collective-permute-start(bf16[2,2,2,32,512]{4,3,2,0,1:T(8,128)(2,1)S(1)} %fusion.18), channel_id=1, source_target_pairs={{0,8},{2,10},{4,12},{6,14},{8,0},{10,2},{12,4},{14,6},{16,24},{18,... | collective-permute-start | bytes 786440 | tf_op jit(solution)/shard_map/ppermute | solution.py:21
  427.7 29.9 %collective-permute-start.66 = (bf16[1,2,32,2048]{3,2,1,0:T(8,128)(2,1)S(1)}, bf16[1,2,32,2048]{3,2,1,0:T(8,128)(2,1)S(1)}, u32[]{:S(2)}, u32[]{:S(2)}) collective-permute-start(bf16[1,2,32,2048]{3,2,1,0:T(8,128)(2,1)S(1)} %slice.787), channel_id=1, source_target_pairs={{0,24},{2,26},{4,28},{6,30},{8,16},{10,18},{12,20},{14,22},{16,8},... | collective-permute-start | bytes 786440 | tf_op jit(solution)/shard_map/ppermute | solution.py:21
  429.2 37.2 %collective-permute-start.69 = (bf16[1,128,1024]{2,1,0:T(8,128)(2,1)S(1)}, bf16[1,128,1024]{2,1,0:T(8,128)(2,1)S(1)}, u32[]{:S(2)}, u32[]{:S(2)}) collective-permute-start(bf16[1,128,1024]{2,1,0:T(8,128)(2,1)S(1)} %slice.786), channel_id=1, source_target_pairs={{0,24},{2,26},{4,28},{6,30},{8,16},{10,18},{12,20},{14,22},{16,8},... | collective-permute-start | bytes 786440 | tf_op jit(solution)/shard_map/ppermute | solution.py:21
  431.3 24.0 %collective-permute-start.49 = (f32[216,128]{1,0:T(8,128)S(1)}, f32[216,128]{1,0:T(8,128)S(1)}, u32[]{:S(2)}, u32[]{:S(2)}) collective-permute-start(f32[216,128]{1,0:T(8,128)S(1)} %add.471), channel_id=1, source_target_pairs={{0,8},{2,10},{4,12},{6,14},{8,0},{10,2},{12,4},{14,6},{16,24},{18,... | collective-permute-start | bytes 331784 | tf_op jit(solution)/shard_map/ppermute | solution.py:21
  434.1 12.9 %collective-permute-start.64 = (bf16[1,1,32,1024]{3,2,0,1:T(8,128)(2,1)S(1)}, bf16[1,1,32,1024]{3,2,0,1:T(8,128)(2,1)S(1)}, u32[]{:S(2)}, u32[]{:S(2)}) collective-permute-start(bf16[1,1,32,1024]{3,2,0,1:T(8,128)(2,1)S(1)} %slice.791), channel_id=1, source_target_pairs={{0,24},{2,26},{4,28},{6,30},{8,16},{10,18},{12,20},{14,22},{16,8},... | collective-permute-start | bytes 196616 | tf_op jit(solution)/shard_map/ppermute | solution.py:21
  447.0 8.3 %collective-permute-start.57 = (bf16[1,2,32,512]{3,2,1,0:T(8,128)(2,1)S(1)}, bf16[1,2,32,512]{3,2,1,0:T(8,128)(2,1)S(1)}, u32[]{:S(2)}, u32[]{:S(2)}) collective-permute-start(bf16[1,2,32,512]{3,2,1,0:T(8,128)(2,1)S(1)} %slice.792), channel_id=1, source_target_pairs={{0,24},{2,26},{4,28},{6,30},{8,16},{10,18},{12,20},{14,22},{16,8},... | collective-permute-start | bytes 196616 | tf_op jit(solution)/shard_map/ppermute | solution.py:21
  455.4 12.2 %collective-permute-start.50 = (f32[216,128]{1,0:T(8,128)S(1)}, f32[216,128]{1,0:T(8,128)S(1)}, u32[]{:S(2)}, u32[]{:S(2)}) collective-permute-start(f32[216,128]{1,0:T(8,128)S(1)} %add.472), channel_id=1, source_target_pairs={{0,4},{2,6},{4,0},{6,2},{8,12},{10,14},{12,8},{14,10},{16,20},{18,... | collective-permute-start | bytes 331784 | tf_op jit(solution)/shard_map/ppermute | solution.py:21
  455.8 12.5 %collective-permute-start.60 = (bf16[1,2,2,32,512]{4,3,2,0,1:T(8,128)(2,1)S(1)}, bf16[1,2,2,32,512]{4,3,2,0,1:T(8,128)(2,1)S(1)}, u32[]{:S(2)}, u32[]{:S(2)}) collective-permute-start(bf16[1,2,2,32,512]{4,3,2,0,1:T(8,128)(2,1)S(1)} %slice.789), channel_id=1, source_target_pairs={{0,24},{2,26},{4,28},{6,30},{8,16},{10,18},{12,20},{14,22},{16,8},... | collective-permute-start | bytes 393224 | tf_op jit(solution)/shard_map/ppermute | solution.py:21
  457.9 17.6 %collective-permute-start.67 = (f32[32,2048]{1,0:T(8,128)S(1)}, f32[32,2048]{1,0:T(8,128)S(1)}, u32[]{:S(2)}, u32[]{:S(2)}) collective-permute-start(f32[32,2048]{1,0:T(8,128)S(1)} %get-tuple-element.268), channel_id=1, source_target_pairs={{0,2},{2,0},{4,6},{6,4},{8,10},{10,8},{12,14},{14,12},{16,18},{18,... | collective-permute-start | bytes 786440 | tf_op jit(solution)/shard_map/ppermute | solution.py:21
  468.9 15.8 %collective-permute-start.61 = (f32[32,1536]{1,0:T(8,128)S(1)}, f32[32,1536]{1,0:T(8,128)S(1)}, u32[]{:S(2)}, u32[]{:S(2)}) collective-permute-start(f32[32,1536]{1,0:T(8,128)S(1)} %get-tuple-element.270), channel_id=1, source_target_pairs={{0,2},{2,0},{4,6},{6,4},{8,10},{10,8},{12,14},{14,12},{16,18},{18,... | collective-permute-start | bytes 589832 | tf_op jit(solution)/shard_map/ppermute | solution.py:21
  (106 other events, 763.7 us)
